TPU v7x, 256 devices: a whole 4x4x8 slice. The times are simulated.
256 devices in a mesh: lat: 8 (over x, y_hi), lon: 32 (over z, y_lo, core).
Axes of the slice: x: 4, y: 4 (y_hi: 2, y_lo: 2; y = y_hi * 2 + y_lo), z: 8, core: 2. Of those that a mesh axis runs over, the one named last changes fastest.
Arguments:
- fields: bfloat16 [192, 128, 4096], P(None, 'lat', 'lon'), may hold values from -27.5 to 27.5
- cotangent: bfloat16 [192, 128, 4096], P(None, 'lat', 'lon'), may hold values from -6 to 6
- land_sea: int32 [128, 4096], P('lat', 'lon'), may hold values 0 or 1
- kernel: bfloat16 [192, 7, 7], replicated, may hold values from -0.875 to 0.875
- ln_gain: float32 [192], replicated, may hold values from 0.1 to 1.9
- proj_in: bfloat16 [768, 192], replicated, may hold values from -0.4375 to 0.4375
- proj_out: bfloat16 [192, 768], replicated, may hold values from -0.21875 to 0.21875
Outputs:
- updated: bfloat16 [192, 128, 4096], P(None, 'lat', 'lon')
- grad_fields: bfloat16 [192, 128, 4096], P(None, 'lat', 'lon')
- grad_kernel: float32 [192, 7, 7], replicated
- grad_gain: float32 [192], replicated
- grad_proj_in: float32 [768, 192], replicated
- grad_proj_out: float32 [192, 768], replicated
All inputs are finite; a program needn't handle non-finite values. No bound on the sum of `land_sea` on one device may be relied on, other than what follows from the above.
Results may differ from a plain program's by a relative error of at most 0.007.
Values may be sent and summed in bfloat16 or wider, within the bound.
No kernel may reach another device: no remote copies, remote signals or barrier semaphores. Data moves between devices by JAX's collectives and lax.ppermute only.
A program may use at most 128 MiB of HBM per device.

v0:
```python
from functools import partial

import jax
import jax.numpy as jnp
from jax import lax
from jax.sharding import PartitionSpec as P

conv_layout = ("NCHW", "OIHW", "NCHW")


def partner(block, axis, stride):
    count = lax.axis_size(axis)
    route = []
    for low in range(count):
        high = low | 1 << stride
        if high != low and high < count:
            route += [(low, high), (high, low)]
    return lax.ppermute(block, axis, route)


def padded_2(block, sides, width, periodic):
    for axis, dim in sides:
        count = lax.axis_size(axis)
        forward = [(i, i + 1) for i in range(count - 1)]
        if periodic:
            forward.append((count - 1, 0))
        backward = [(target, source) for source, target in forward]
        low = lax.ppermute(
            lax.slice_in_dim(block, block.shape[dim] - width, None, axis=dim), axis, forward
        )
        high = lax.ppermute(lax.slice_in_dim(block, 0, width, axis=dim), axis, backward)
        block = jnp.concatenate([low, block, high], axis=dim)
    return block


def for_sending(x):
    return jax.tree.map(lambda a: a.astype(jnp.bfloat16) if a.dtype == jnp.float32 else a, x)


def depthwise(source, weights):
    return lax.conv_general_dilated(
        source[None],
        weights[:, None],
        (1, 1),
        "VALID",
        dimension_numbers=conv_layout,
        feature_group_count=source.shape[0],
        preferred_element_type=jnp.float32,
    )[0]


def mirror_rows(strip_rows):
    for bit_level in range(lax.axis_size("lon").bit_length() - 1):
        strip_rows = partner(strip_rows, "lon", bit_level)
    return jnp.flip(strip_rows, axis=(1, 2))


def return_rows(strip_rows):
    for bit_level in range(lax.axis_size("lon").bit_length() - 1):
        strip_rows = partner(strip_rows.astype(jnp.bfloat16), "lon", bit_level).astype(
            strip_rows.dtype
        )
    return jnp.flip(strip_rows, axis=(1, 2))


def fold_rim(extended, axis_dim):
    inner_len = extended.shape[axis_dim] - 12
    core_part = lax.slice_in_dim(extended, 6, inner_len + 6, axis=axis_dim)
    low_rim = lax.slice_in_dim(extended, 0, 3, axis=axis_dim)
    high_rim = lax.slice_in_dim(extended, inner_len + 9, inner_len + 12, axis=axis_dim)
    low_pad = [(0, 0), (0, 0), (0, 0)]
    high_pad = [(0, 0), (0, 0), (0, 0)]
    low_pad[axis_dim] = (0, inner_len - 3)
    high_pad[axis_dim] = (inner_len - 3, 0)
    return core_part + jnp.pad(low_rim, low_pad) + jnp.pad(high_rim, high_pad)


def norm_mlp(conv_cells, field_cells, cot_cells, ocean_cells, ln_gain, proj_in, proj_out):
    center = conv_cells - jnp.mean(conv_cells, axis=0, keepdims=True)
    spread = lax.rsqrt(jnp.mean(center * center, axis=0, keepdims=True) + 1e-06)
    normed = center * spread
    scaled = (normed * ln_gain[:, None]).astype(jnp.bfloat16)
    hidden = jnp.dot(proj_in, scaled, preferred_element_type=jnp.float32)
    active, pullback = jax.vjp(partial(jax.nn.gelu, approximate=True), hidden)
    active = active.astype(jnp.bfloat16)
    mixed_out = jnp.dot(proj_out, active, preferred_element_type=jnp.float32)
    ocean_float = ocean_cells.astype(jnp.float32)[None]
    result = (field_cells.astype(jnp.float32) + ocean_float * mixed_out).astype(jnp.bfloat16)
    masked_cot = cot_cells * ocean_cells.astype(jnp.bfloat16)[None]
    grad_out_w = jnp.dot(masked_cot, active.T, preferred_element_type=jnp.float32)
    grad_act = jnp.dot(proj_out.T, masked_cot, preferred_element_type=jnp.float32)
    grad_hidden = pullback(grad_act)[0].astype(jnp.bfloat16)
    grad_in_w = jnp.dot(grad_hidden, scaled.T, preferred_element_type=jnp.float32)
    grad_normed = jnp.dot(proj_in.T, grad_hidden, preferred_element_type=jnp.float32)
    grad_gain = jnp.sum(grad_normed * normed, axis=1)
    grad_scaled = grad_normed * ln_gain[:, None]
    grad_conv = spread * (
        grad_scaled
        - jnp.mean(grad_scaled, axis=0, keepdims=True)
        - normed * jnp.mean(grad_scaled * normed, axis=0, keepdims=True)
    )
    return (result, grad_conv.astype(jnp.bfloat16), grad_in_w, grad_out_w, grad_gain)


def on_device(fields, cotangent, land_sea, kernel, ln_gain, proj_in, proj_out):
    channels, lat_rows, lon_cols = fields.shape
    is_top = lax.axis_index("lat") == lax.axis_size("lat") - 1
    ocean_mask = land_sea.astype(jnp.bfloat16)
    masked = fields * ocean_mask[None]
    widened = padded_2(masked, (("lon", 2),), 3, True)
    padded = padded_2(widened, (("lat", 1),), 3, False)
    folded = mirror_rows(widened[:, lat_rows - 3 :, :])
    upper_rows = padded[:, lat_rows + 3 :, :] + jnp.where(is_top, folded, jnp.zeros_like(folded))
    padded = jnp.concatenate([padded[:, : lat_rows + 3, :], upper_rows], axis=1)
    conv_out = depthwise(padded, kernel).reshape(channels, lat_rows * lon_cols)
    result, grad_conv, grad_in, grad_out, grad_gain = norm_mlp(
        conv_out,
        fields.reshape(channels, lat_rows * lon_cols),
        cotangent.reshape(channels, lat_rows * lon_cols),
        land_sea.reshape(lat_rows * lon_cols),
        ln_gain,
        proj_in,
        proj_out,
    )
    grad_conv = grad_conv.reshape(channels, lat_rows, lon_cols)
    grad_kern = depthwise(padded, grad_conv)
    flipped = jnp.flip(kernel, axis=(1, 2))
    spread_grad = jnp.pad(grad_conv, ((0, 0), (6, 6), (6, 6)))
    grad_pad = depthwise(spread_grad, flipped)
    sent_rows = jnp.where(is_top, grad_pad[:, lat_rows + 3 :, :], 0.0)
    returned = return_rows(sent_rows)
    grad_pad = grad_pad.at[:, lat_rows : lat_rows + 3, :].add(jnp.where(is_top, returned, 0.0))
    lat_full = padded_2(grad_pad.astype(jnp.bfloat16), (("lat", 1),), 3, False).astype(
        grad_pad.dtype
    )
    grad_rows = fold_rim(lat_full, 1)
    lon_full = padded_2(for_sending(grad_rows), (("lon", 2),), 3, True).astype(grad_rows.dtype)
    grad_masked = fold_rim(lon_full, 2)
    grad_fields = (
        cotangent.astype(jnp.float32) + land_sea.astype(jnp.float32)[None] * grad_masked
    ).astype(jnp.bfloat16)
    summed = lax.psum((grad_kern, grad_gain, grad_in, grad_out), ("lat", "lon"))
    factor = float(lat_rows * lax.axis_size("lat") * lon_cols * lax.axis_size("lon")) ** (-0.5)
    updated = result.reshape(channels, lat_rows, lon_cols)
    return (
        updated,
        grad_fields,
        summed[0] * factor,
        summed[1] * factor,
        summed[2] * factor,
        summed[3] * factor,
    )


def solution(mesh):
    in_specs = (P(None, "lat", "lon"), P(None, "lat", "lon"), P("lat", "lon"), P(), P(), P(), P())
    out_specs = (P(None, "lat", "lon"), P(None, "lat", "lon"), P(), P(), P(), P())
    return jax.shard_map(
        on_device, mesh=mesh, in_specs=in_specs, out_specs=out_specs, check_vma=False
    )
```

profile of v0, /device:TPU:3, one launch (start us, length us, event | category | flops | bytes accessed | tf_op | source)
XLA Modules:
  0.0 454.7 jit_solution(1091866901353867922)
XLA Ops:
  8.1 2.1 copy.83
  13.5 2.3 collective-permute-done.1
  16.7 3.5 collective-permute-start.4
  21.4 7.8 %collective-permute-done.5 = bf16[192,3,134]{0,1,2:T(4,128)(2,1)S(1)} collective-permute-done((bf16[192,3,134]{0,1,2:T(4,128)(2,1)S(1)}, bf16[192,3,134]{0,1,2:T(4,128)(2,1)S(1)}, u32[]{:S(2)}, u32[]{:S(2)}) %collective-permute-start.5) | collective-permute-done | bytes 154400 | tf_op jit(solution)/shard_map/ppermute | solution.py:18
  29.2 6.9 %collective-permute-done.6 = bf16[192,3,134]{0,1,2:T(4,128)(2,1)S(1)} collective-permute-done((bf16[192,3,134]{0,1,2:T(4,128)(2,1)S(1)}, bf16[192,3,134]{0,1,2:T(4,128)(2,1)S(1)}, u32[]{:S(2)}, u32[]{:S(2)}) %collective-permute-start.6) | collective-permute-done | bytes 154400 | tf_op jit(solution)/shard_map/ppermute | solution.py:18
  36.1 4.8 %collective-permute-start.7 = (bf16[192,3,134]{0,1,2:T(4,128)(2,1)S(1)}, bf16[192,3,134]{0,1,2:T(4,128)(2,1)}, u32[]{:S(2)}, u32[]{:S(2)}) collective-permute-start(bf16[192,3,134]{0,1,2:T(4,128)(2,1)S(1)} %collective-permute-done.6), channel_id=1, source_target_pairs={{0,8},{8,0},{1,9},{9,1},{2,10},{10,2},{3,11},{11,3},{4,12},{12,4},... | collective-permute-start | bytes 463112 | tf_op jit(solution)/shard_map/ppermute | solution.py:18
  40.8 12.1 %collective-permute-done.7 = bf16[192,3,134]{0,1,2:T(4,128)(2,1)} collective-permute-done((bf16[192,3,134]{0,1,2:T(4,128)(2,1)S(1)}, bf16[192,3,134]{0,1,2:T(4,128)(2,1)}, u32[]{:S(2)}, u32[]{:S(2)}) %collective-permute-start.7) | collective-permute-done | bytes 154400 | tf_op jit(solution)/shard_map/ppermute | solution.py:18
  52.9 2.2 collective-permute-start.8
  55.2 4.4 collective-permute-start.3
  64.2 2.4 collective-permute-start.2
  66.6 4.0 collective-permute-done.8
  70.7 2.8 rev.12
  74.6 2.3 fusion.65
  77.9 8.9 %fusion.43 = f32[16,8,17,192]{3,1,2,0:T(8,128)S(1)} fusion(bf16[192,22,1,7,6]{0,3,4,1,2:T(8,128)(2,1)S(1)} %slice.96, bf16[192,22,1,8,17]{0,3,4,1,2:T(8,128)(2,1)S(1)} %copy.85, pred[8,17]{0,1:T(8,128)(4,1)S(1)} %copy-done.26, bf16[192,1,7,7]{0,3,2,1:T(8,128)(2,1)S(1)} %bitcast.149), kind=kOutput, calls=%fused_computation.62 | convolution fusion | flops 46024704 | bytes 3193864 | tf_op jit(solution)/shard_map/conv_general_dilated | solution.py:41
  91.0 2.3 copy.88
  94.9 5.0 %fusion.6 = bf16[768,2048]{0,1:T(8,128)(2,1)S(1)} fusion(f32[2048,768]{1,0:T(8,128)S(1)} %fusion.68, bf16[192,768]{1,0:T(8,128)(2,1)S(1)} %copy-done.23, bf16[24,8,16,128]{3,2,1,0:T(8,128)(2,1)S(1)} %bitcast.145, bf16[2048]{0:T(1024)(128)(2,1)S(1)} %bitcast.151), kind=kOutput, calls=%fused_computation.8 | convolution fusion | flops 635830272 | bytes 10522624 | tf_op jit(solution)/shard_map/dot_general | solution.py:91
  102.7 2.3 copy.94
  109.0 13.0 %broadcast_select_fusion = f32[22,8,18,192]{3,1,2,0:T(8,128)S(1)} fusion(pred[8,18]{0,1:T(8,128)(4,1)S(1)} %copy-done.25, bf16[192,28,1,7,6]{0,3,4,1,2:T(8,128)(2,1)S(1)} %slice.98, bf16[192,28,1,8,18]{0,3,4,1,2:T(8,128)(2,1)S(1)} %copy.96, bf16[192,1,7,7]{0,3,2,1:T(8,128)(2,1)S(1)} %bitcast.150), kind=kOutput, calls=%fused_computation.55 | convolution fusion | flops 66410496 | bytes 4451856 | tf_op jit(solution)/shard_map/conv_general_dilated | solution.py:41
  124.0 3.0 collective-permute-start.9
  127.0 4.5 copy.103
  131.5 22.5 %fusion.13 = f32[1,192,7,7]{1,0,3,2:T(1,128)} fusion(bf16[192,1,16,128]{0,1,3,2:T(2,128)(2,1)} %copy.103, bf16[1,192,22,134]{1,2,3,0:T(8,128)(2,1)} %get-tuple-element.55), kind=kOutput, calls=%fused_computation.21 | convolution fusion | flops 38535168 | bytes 1956096 | tf_op jit(solution)/shard_map/conv_general_dilated | solution.py:41
  154.0 6.4 %fusion.47 = bf16[24,8,16,128]{3,1,2,0:T(8,128)(2,1)} fusion(bf16[192,768]{1,0:T(8,128)(2,1)S(1)} %copy-done.24, f32[24,8,16,128]{3,2,1,0:T(8,128)S(1)} %copy-done.9, f32[2048]{0:T(1024)S(1)} %get-tuple-element.66, f32[2048,768]{1,0:T(8,128)} %copy-done.2), kind=kOutput, calls=%fused_computation.65 | convolution fusion | flops 619315200 | bytes 8953856 | tf_op jit(solution)/shard_map/dot_general | solution.py:86
  161.8 6.0 %fusion.50 = f32[192,768]{1,0:T(8,128)} fusion(bf16[24,8,16,128]{3,2,1,0:T(8,128)(2,1)S(1)} %bitcast.146, bf16[2048]{0:T(1024)(128)(2,1)S(1)} %bitcast.152, f32[2048,768]{1,0:T(8,128)} %copy-done.2), kind=kOutput, calls=%fused_computation.70 | convolution fusion | flops 618528768 | bytes 7671808 | tf_op jit(solution)/shard_map/dot_general | solution.py:90
  171.0 78.6 %all-reduce.3 = (f32[192,7,7]{0,2,1:T(8,128)S(1)}, f32[192]{0:T(256)S(1)}) all-reduce(f32[192,7,7]{0,2,1:T(8,128)S(1)} %bitcast.148, f32[192]{0:T(256)S(1)} %get-tuple-element.48), channel_id=1, replica_groups=mesh['lat'=8,'lon'=32] {'lat','lon'}, use_global_device_ids=true, to_apply=%region_4.5 | all-reduce | flops 9600 | bytes 76800 | tf_op jit(solution)/shard_map/psum | solution.py:142
  250.4 14.1 %collective-permute-done.12 = bf16[192,3,134]{0,1,2:T(4,128)(2,1)S(1)} collective-permute-done((bf16[192,3,134]{0,1,2:T(4,128)(2,1)}, bf16[192,3,134]{0,1,2:T(4,128)(2,1)S(1)}, u32[]{:S(2)}, u32[]{:S(2)}) %collective-permute-start.12) | collective-permute-done | bytes 154400 | tf_op jit(solution)/shard_map/ppermute | solution.py:18
  268.2 13.3 %collective-permute-done.13 = bf16[192,3,134]{0,1,2:T(4,128)(2,1)S(1)} collective-permute-done((bf16[192,3,134]{0,1,2:T(4,128)(2,1)S(1)}, bf16[192,3,134]{0,1,2:T(4,128)(2,1)S(1)}, u32[]{:S(2)}, u32[]{:S(2)}) %collective-permute-start.13) | collective-permute-done | bytes 154400 | tf_op jit(solution)/shard_map/ppermute | solution.py:18
  282.9 5.8 %scatter-add.4 = bf16[192,22,134]{0,1,2:T(8,128)(2,1)S(1)} dynamic-update-slice(bf16[192,22,134]{0,1,2:T(8,128)(2,1)S(1)} %slice_bitcast_fusion, bf16[192,3,134]{0,1,2:T(4,128)(2,1)S(1)} %fusion.52, s32[]{:T(128)} %constant.75.clone.1, s32[]{:T(128)} %constant.76.clone.1, s32[]{:T(128)} %constant.75.clone.1) | dynamic-update-slice | bytes 308740 | tf_op jit(solution)/shard_map/scatter-add | solution.py:132
  289.0 4.0 collective-permute-start.14
  293.0 3.7 collective-permute-start.15
  296.7 136.2 %all-reduce.7.cloned.1.call-done = (f32[768,192]{0,1:T(8,128)}, f32[192,768]{1,0:T(8,128)}) async-done(((f32[768,192]{0,1:T(8,128)}, f32[192,768]{1,0:T(8,128)}), (f32[768,192]{0,1:T(8,128)}, f32[192,768]{1,0:T(8,128)})) %all-reduce.7.cloned.1.call-update) | async-done | bytes 1179664 | tf_op jit(solution)/shard_map/psum | solution.py:142
  436.9 3.8 collective-permute-start.16
  441.6 2.6 collective-permute-done.17
  (130 shorter events, 46.4 us)
Async XLA Ops:
  7.2 86.2 %copy-start = (bf16[768,192]{0,1:T(8,128)(2,1)S(1)}, bf16[768,192]{0,1:T(8,128)(2,1)}, u32[]{:S(2)}) copy-start(bf16[768,192]{0,1:T(8,128)(2,1)} %param.14) | copy-start | bytes 884740
  7.2 425.6 %all-reduce.7.cloned.1.call-start = ((), (), s32[]{:S(2)}) async-start(), calls=%async_computation | async-start | bytes 2359296 | tf_op jit(solution)/shard_map/psum | solution.py:142
  10.2 49.4 %copy-start.18 = (bf16[192,7,7]{0,2,1:T(8,128)(2,1)S(1)}, bf16[192,7,7]{0,2,1:T(8,128)(2,1)}, u32[]{:S(2)}) copy-start(bf16[192,7,7]{0,2,1:T(8,128)(2,1)} %param.12) | copy-start | bytes 56452
  10.2 50.8 %copy-start.10 = (bf16[192,16,128]{2,1,0:T(8,128)(2,1)S(1)}, bf16[192,16,128]{2,1,0:T(8,128)(2,1)}, u32[]{:S(2)}) copy-start(bf16[192,16,128]{2,1,0:T(8,128)(2,1)} %param.10) | copy-start | bytes 2359300
  10.6 52.3 %copy-start.8 = (bf16[192,16,128]{2,1,0:T(8,128)(2,1)S(1)}, bf16[192,16,128]{2,1,0:T(8,128)(2,1)}, u32[]{:S(2)}) copy-start(bf16[192,16,128]{2,1,0:T(8,128)(2,1)} %param.9) | copy-start | bytes 2359300
  10.6 2.9 collective-permute-start
  12.5 3.3 collective-permute-start.1
  16.7 4.7 %collective-permute-start.4 = (bf16[192,3,134]{0,1,2:T(4,128)(2,1)S(1)}, bf16[192,3,134]{0,1,2:T(4,128)(2,1)S(1)}, u32[]{:S(2)}, u32[]{:S(2)}) collective-permute-start(bf16[192,3,134]{0,1,2:T(4,128)(2,1)S(1)} %get-tuple-element.61), channel_id=1, source_target_pairs={{0,1},{1,0},{2,3},{3,2},{4,5},{5,4},{6,7},{7,6},{8,9},{9,8},{10,11... | collective-permute-start | bytes 463112 | tf_op jit(solution)/shard_map/ppermute | solution.py:18
  21.4 7.8 %collective-permute-start.5 = (bf16[192,3,134]{0,1,2:T(4,128)(2,1)S(1)}, bf16[192,3,134]{0,1,2:T(4,128)(2,1)S(1)}, u32[]{:S(2)}, u32[]{:S(2)}) collective-permute-start(bf16[192,3,134]{0,1,2:T(4,128)(2,1)S(1)} %collective-permute-done.4), channel_id=1, source_target_pairs={{0,2},{2,0},{1,3},{3,1},{4,6},{6,4},{5,7},{7,5},{8,10},{10,8},{9,1... | collective-permute-start | bytes 463112 | tf_op jit(solution)/shard_map/ppermute | solution.py:18
  29.2 6.9 %collective-permute-start.6 = (bf16[192,3,134]{0,1,2:T(4,128)(2,1)S(1)}, bf16[192,3,134]{0,1,2:T(4,128)(2,1)S(1)}, u32[]{:S(2)}, u32[]{:S(2)}) collective-permute-start(bf16[192,3,134]{0,1,2:T(4,128)(2,1)S(1)} %collective-permute-done.5), channel_id=1, source_target_pairs={{0,4},{4,0},{1,5},{5,1},{2,6},{6,2},{3,7},{7,3},{8,12},{12,8},{9,1... | collective-permute-start | bytes 463112 | tf_op jit(solution)/shard_map/ppermute | solution.py:18
  36.1 16.9 %collective-permute-start.7 = (bf16[192,3,134]{0,1,2:T(4,128)(2,1)S(1)}, bf16[192,3,134]{0,1,2:T(4,128)(2,1)}, u32[]{:S(2)}, u32[]{:S(2)}) collective-permute-start(bf16[192,3,134]{0,1,2:T(4,128)(2,1)S(1)} %collective-permute-done.6), channel_id=1, source_target_pairs={{0,8},{8,0},{1,9},{9,1},{2,10},{10,2},{3,11},{11,3},{4,12},{12,4},... | collective-permute-start | bytes 463112 | tf_op jit(solution)/shard_map/ppermute | solution.py:18
  52.9 17.7 %collective-permute-start.8 = (bf16[192,3,134]{0,1,2:T(4,128)(2,1)}, bf16[192,3,134]{0,1,2:T(4,128)(2,1)}, u32[]{:S(2)}, u32[]{:S(2)}) collective-permute-start(bf16[192,3,134]{0,1,2:T(4,128)(2,1)} %collective-permute-done.7), channel_id=1, source_target_pairs={{0,16},{16,0},{1,17},{17,1},{2,18},{18,2},{3,19},{19,3},{4,20},{20... | collective-permute-start | bytes 463112 | tf_op jit(solution)/shard_map/ppermute | solution.py:18
  55.2 18.3 %collective-permute-start.3 = (bf16[192,3,134]{0,1,2:T(4,128)(2,1)}, bf16[192,3,134]{0,1,2:T(4,128)(2,1)}, u32[]{:S(2)}, u32[]{:S(2)}) collective-permute-start(bf16[192,3,134]{0,1,2:T(4,128)(2,1)} %get-tuple-element.62), channel_id=1, source_target_pairs={{32,0},{64,32},{96,64},{128,96},{160,128},{192,160},{224,192},{33,... | collective-permute-start | bytes 463112 | tf_op jit(solution)/shard_map/ppermute | solution.py:31
  64.2 10.3 %collective-permute-start.2 = (bf16[192,3,134]{0,1,2:T(4,128)(2,1)S(1)}, bf16[192,3,134]{0,1,2:T(4,128)(2,1)S(1)}, u32[]{:S(2)}, u32[]{:S(2)}) collective-permute-start(bf16[192,3,134]{0,1,2:T(4,128)(2,1)S(1)} %get-tuple-element.61), channel_id=1, source_target_pairs={{0,32},{32,64},{64,96},{96,128},{128,160},{160,192},{192,224},{1,3... | collective-permute-start | bytes 463112 | tf_op jit(solution)/shard_map/ppermute | solution.py:28
  94.8 5.0 %copy-start.2 = (f32[2048,768]{1,0:T(8,128)}, f32[2048,768]{1,0:T(8,128)S(1)}, u32[]{:S(2)}) copy-start(f32[2048,768]{1,0:T(8,128)S(1)} %fusion.68) | copy-start | bytes 18874372
  102.6 4.3 copy-start.3
  124.0 36.4 %collective-permute-start.9 = (bf16[192,3,134]{0,1,2:T(4,128)(2,1)S(1)}, bf16[192,3,134]{0,1,2:T(4,128)(2,1)}, u32[]{:S(2)}, u32[]{:S(2)}) collective-permute-start(bf16[192,3,134]{0,1,2:T(4,128)(2,1)S(1)} %fusion.51), channel_id=1, source_target_pairs={{0,1},{1,0},{2,3},{3,2},{4,5},{5,4},{6,7},{7,6},{8,9},{9,8},{10,11... | collective-permute-start | bytes 463112 | tf_op jit(solution)/shard_map/ppermute | solution.py:18
  131.5 22.5 %copy-start.9 = (f32[24,8,16,128]{3,2,1,0:T(8,128)S(1)}, f32[24,8,16,128]{3,2,1,0:T(8,128)}, u32[]{:S(2)}) copy-start(f32[24,8,16,128]{3,2,1,0:T(8,128)} %convert.1) | copy-start | bytes 4718596
  131.5 22.5 %copy-start.24 = (bf16[192,768]{1,0:T(8,128)(2,1)S(1)}, bf16[192,768]{1,0:T(8,128)(2,1)}, u32[]{:S(2)}) copy-start(bf16[192,768]{1,0:T(8,128)(2,1)} %param.15) | copy-start | bytes 884740
  154.0 7.8 %copy-start.12 = (bf16[192,16,128]{2,1,0:T(8,128)(2,1)S(1)}, bf16[192,16,128]{2,1,0:T(8,128)(2,1)}, u32[]{:S(2)}) copy-start(bf16[192,16,128]{2,1,0:T(8,128)(2,1)} %param.10) | copy-start | bytes 2359300
  160.4 8.5 %copy-start.7 = (bf16[768,2048]{0,1:T(8,128)(2,1)S(1)}, bf16[768,2048]{0,1:T(8,128)(2,1)}, u32[]{:S(2)}) copy-start(bf16[768,2048]{0,1:T(8,128)(2,1)} %copy-done.6) | copy-start | bytes 9437188
  160.4 8.5 %collective-permute-start.10 = (bf16[192,3,134]{0,1,2:T(4,128)(2,1)}, bf16[192,3,134]{0,1,2:T(4,128)(2,1)}, u32[]{:S(2)}, u32[]{:S(2)}) collective-permute-start(bf16[192,3,134]{0,1,2:T(4,128)(2,1)} %collective-permute-done.9), channel_id=1, source_target_pairs={{0,2},{2,0},{1,3},{3,1},{4,6},{6,4},{5,7},{7,5},{8,10},{10,8},{9,1... | collective-permute-start | bytes 463112 | tf_op jit(solution)/shard_map/ppermute | solution.py:18
  168.9 80.7 %collective-permute-start.11 = (bf16[192,3,134]{0,1,2:T(4,128)(2,1)}, bf16[192,3,134]{0,1,2:T(4,128)(2,1)}, u32[]{:S(2)}, u32[]{:S(2)}) collective-permute-start(bf16[192,3,134]{0,1,2:T(4,128)(2,1)} %collective-permute-done.10), channel_id=1, source_target_pairs={{0,4},{4,0},{1,5},{5,1},{2,6},{6,2},{3,7},{7,3},{8,12},{12,8},{9,1... | collective-permute-start | bytes 463112 | tf_op jit(solution)/shard_map/ppermute | solution.py:18
  170.9 96.0 %copy-start.13 = (bf16[24,8,16,128]{3,1,2,0:T(8,128)(2,1)S(1)}, bf16[24,8,16,128]{3,1,2,0:T(8,128)(2,1)}, u32[]{:S(2)}) copy-start(bf16[24,8,16,128]{3,1,2,0:T(8,128)(2,1)} %fusion.47) | copy-start | bytes 2359300
  170.9 97.0 %slice-start = ((f32[22,8,18,192]{3,1,2,0:T(8,128)}), f32[3,8,18,192]{3,1,2,0:T(8,128)S(1)}, s32[]{:S(2)}) async-start(f32[22,8,18,192]{3,1,2,0:T(8,128)} %copy-done.5), calls=%async_computation.1 | async-start | bytes 884736 | tf_op jit(solution)/shard_map/conv_general_dilated | solution.py:41
  249.6 14.9 %collective-permute-start.12 = (bf16[192,3,134]{0,1,2:T(4,128)(2,1)}, bf16[192,3,134]{0,1,2:T(4,128)(2,1)S(1)}, u32[]{:S(2)}, u32[]{:S(2)}) collective-permute-start(bf16[192,3,134]{0,1,2:T(4,128)(2,1)} %collective-permute-done.11), channel_id=1, source_target_pairs={{0,8},{8,0},{1,9},{9,1},{2,10},{10,2},{3,11},{11,3},{4,12},{12,4},... | collective-permute-start | bytes 463112 | tf_op jit(solution)/shard_map/ppermute | solution.py:18
  264.5 17.0 %collective-permute-start.13 = (bf16[192,3,134]{0,1,2:T(4,128)(2,1)S(1)}, bf16[192,3,134]{0,1,2:T(4,128)(2,1)S(1)}, u32[]{:S(2)}, u32[]{:S(2)}) collective-permute-start(bf16[192,3,134]{0,1,2:T(4,128)(2,1)S(1)} %collective-permute-done.12), channel_id=1, source_target_pairs={{0,16},{16,0},{1,17},{17,1},{2,18},{18,2},{3,19},{19,3},{4,20},{20... | collective-permute-start | bytes 463112 | tf_op jit(solution)/shard_map/ppermute | solution.py:18
  289.0 145.8 %collective-permute-start.14 = (bf16[192,3,134]{0,1,2:T(4,128)(2,1)S(1)}, bf16[192,3,134]{0,1,2:T(4,128)(2,1)S(1)}, u32[]{:S(2)}, u32[]{:S(2)}) collective-permute-start(bf16[192,3,134]{0,1,2:T(4,128)(2,1)S(1)} %get-tuple-element.57), channel_id=1, source_target_pairs={{0,32},{32,64},{64,96},{96,128},{128,160},{160,192},{192,224},{1,3... | collective-permute-start | bytes 463112 | tf_op jit(solution)/shard_map/ppermute | solution.py:28
  293.0 141.8 %collective-permute-start.15 = (bf16[192,3,134]{0,1,2:T(4,128)(2,1)S(1)}, bf16[192,3,134]{0,1,2:T(4,128)(2,1)S(1)}, u32[]{:S(2)}, u32[]{:S(2)}) collective-permute-start(bf16[192,3,134]{0,1,2:T(4,128)(2,1)S(1)} %get-tuple-element.58), channel_id=1, source_target_pairs={{32,0},{64,32},{96,64},{128,96},{160,128},{192,160},{224,192},{33,... | collective-permute-start | bytes 463112 | tf_op jit(solution)/shard_map/ppermute | solution.py:31
  436.1 4.5 copy-start.14
  436.9 4.7 %collective-permute-start.16 = (bf16[192,16,3]{0,1,2:T(8,128)(2,1)S(1)}, bf16[192,16,3]{0,1,2:T(8,128)(2,1)S(1)}, u32[]{:S(2)}, u32[]{:S(2)}) collective-permute-start(bf16[192,16,3]{0,1,2:T(8,128)(2,1)S(1)} %get-tuple-element.59), channel_id=1, source_target_pairs={{0,1},{1,2},{2,3},{3,4},{4,5},{5,6},{6,7},{7,8},{8,9},{9,10},{10,1... | collective-permute-start | bytes 55304 | tf_op jit(solution)/shard_map/ppermute | solution.py:28
  440.7 3.5 collective-permute-start.17
  (15 other events, 30.8 us)
Sparse Core Ops, SparseCore 0:
  171.1 261.7 all-reduce.6
where the time goes:
time: 462 us; the launch traced here: 455 us
  waiting for transfers between devices  203 us (44%)
  blocking collectives  78.6 us (17%)
  matrix products  66.7 us (14%)
  local copies, waits for them, and re-layouts  37.7 us (8%)
  starting transfers between devices  37 us (8%)
  other arithmetic  17.2 us (4%)
  between operations  14.8 us (3%)
    psum x1, waiting for transfers between devices, on_device(): summed = lax.psum((grad_kern, grad_gain, grad_in, grad_out), ('lat', 'lon'))  136 us
    psum x1, blocking collectives, on_device(): summed = lax.psum((grad_kern, grad_gain, grad_in, grad_out), ('lat', 'lon'))  78.6 us
    ppermute x10, waiting for transfers between devices, partner(): return lax.ppermute(block, axis, route)  60.5 us
    conv_general_dilated x3, matrix products, depthwise(): lax.conv_general_dilated(source[None], weights[:, None], (1, 1), 'VALID',...  44.4 us
    ppermute x10, starting transfers between devices, partner(): return lax.ppermute(block, axis, route)  16.8 us
    ppermute x4, starting transfers between devices, padded_2(): lax.ppermute(lax.slice_in_dim(block, block.shape[dim] - width, None, axis...  12.1 us
  transfers between devices with their start and end apart: 19, of which 13 were waited for; matrix products, arithmetic and copies ran while one was open for 14% of the time, Pallas kernels for 0%

commit v1 on v0

v1 whole, which is shorter than its diff:
```python
from functools import partial
import numpy as np
import jax, jax.numpy as jnp
from jax import lax
from jax.experimental import pallas as pl
from jax.experimental.pallas import tpu as pltpu

CH, HID, R, Q = 192, 768, 16, 128
F, B = jnp.float32, jnp.bfloat16
C0 = 0.7978845608028654
C1 = C0 * 0.044715


def tap_onehot():
    oh = np.zeros((7, R, 32), np.float32)
    for r in range(R):
        for a in range(7):
            row = r + a
            slot = row - 3 if 3 <= row < R + 3 else (16 + row if row < 3 else row)
            oh[a, r, slot] = 1
    return oh


def toeplitz(kernel, north=None):
    oh = tap_onehot()
    if north is None:
        t = jnp.einsum("cab,ars->crbs", kernel, jnp.asarray(oh, B), preferred_element_type=F)
    else:
        up = np.zeros_like(oh); up[:, :, 19:] = oh[:, :, 19:]
        t = jnp.einsum("cab,ars->crbs", kernel, jnp.asarray(oh - up, B), preferred_element_type=F)
        t = t + jnp.einsum("cab,ars->crbs", north, jnp.asarray(up, B), preferred_element_type=F)
    return t.astype(B).reshape(CH, R, 224)


def band_mask():
    oh = tap_onehot().sum(0)
    return np.tile(oh[::-1], (1, 4)).astype(np.float32)


def front_kernel(e_ref, t_ref, f_ref, cot_ref, land_ref, gain_ref, pi_ref, pit_ref, po_ref, pot_ref, band_ref,
                 up_ref, gc_ref, w_ref,
                 im, s, mcs, u, g, grev, sc, mcb, act, gh, gacc, dks):
    CB = 8
    def conv_block(i, _):
        for j in range(CB):
            c = i * CB + j
            for b in range(7):
                im[c, b * 32:(b + 1) * 32, :] = e_ref[c, :, b:b + Q]
        for j in range(CB):
            c = i * CB + j
            s[pl.ds(c * R, R), :] = jnp.dot(t_ref[c], im[c], preferred_element_type=F)
        return 0
    lax.fori_loop(0, CH // CB, conv_block, 0)
    ocean = land_ref[...].astype(F)

    def sum_block(i, acc):
        for j in range(CB):
            acc = acc + s[pl.ds((i * CB + j) * R, R), :]
        return acc
    mean = lax.fori_loop(0, CH // CB, sum_block, jnp.zeros((R, Q), F)) * (1.0 / CH)

    def sq_block(i, acc):
        for j in range(CB):
            d = s[pl.ds((i * CB + j) * R, R), :] - mean
            acc = acc + d * d
        return acc
    var = lax.fori_loop(0, CH // CB, sq_block, jnp.zeros((R, Q), F)) * (1.0 / CH)
    rstd = lax.rsqrt(var + 1e-6)

    def norm_block(i, _):
        for j in range(CB):
            c = i * CB + j
            rows = pl.ds(c * R, R)
            s[rows, :] = (s[rows, :] - mean) * rstd
            mcs[rows, :] = cot_ref[c].astype(F) * ocean
        return 0
    lax.fori_loop(0, CH // CB, norm_block, 0)
    u[pl.ds(CH * R, R), :] = rstd
    gain = gain_ref[...]
    gacc[...] = jnp.zeros_like(gacc)

    def rows_step(p, _):
        r0 = p * 2
        cells = pl.ds(pl.multiple_of(p * 256, 256), 256)
        nrm = jnp.concatenate([s[pl.ds(r0, CH, stride=R), :], s[pl.ds(r0 + 1, CH, stride=R), :]], axis=1)
        scaled = (nrm * gain).astype(B)
        mc = jnp.concatenate([mcs[pl.ds(r0, CH, stride=R), :], mcs[pl.ds(r0 + 1, CH, stride=R), :]], axis=1).astype(B)
        sc[:, cells] = scaled
        mcb[:, cells] = mc
        mixed = jnp.zeros((CH, 256), F)
        gn = jnp.zeros((CH, 256), F)
        for h in range(3):
            hs = slice(h * 256, (h + 1) * 256)
            v = jnp.dot(pi_ref[hs, :], scaled, preferred_element_type=F)
            ga = jnp.dot(pot_ref[hs, :], mc, preferred_element_type=F)
            sq = v * v
            t = jnp.tanh(v * (C1 * sq + C0))
            half = 0.5 * t + 0.5
            a = v * half
            d = half + a * (1.0 - half) * (6.0 * C1 * sq + 2.0 * C0)
            ab = a.astype(B)
            gb = (ga * d).astype(B)
            act[hs, cells] = ab
            gh[hs, cells] = gb
            mixed = mixed + jnp.dot(po_ref[:, hs], ab, preferred_element_type=F)
            gn = gn + jnp.dot(pit_ref[:, hs], gb, preferred_element_type=F)
        rs = jnp.concatenate([u[pl.ds(CH * R + r0, 1), :], u[pl.ds(CH * R + r0 + 1, 1), :]], axis=1)
        gnn = gn * nrm
        gacc[...] += gnn[:, :Q] + gnn[:, Q:]
        gs = gn * gain
        m1 = jnp.sum(gs, axis=0, keepdims=True) * (1.0 / CH)
        m2 = jnp.sum(gnn * gain, axis=0, keepdims=True) * (1.0 / CH)
        gcv = rs * (gs - m1 - nrm * m2)
        u[pl.ds(r0, CH, stride=R), :] = mixed[:, :Q]
        u[pl.ds(r0 + 1, CH, stride=R), :] = mixed[:, Q:]
        g[pl.ds(r0, CH, stride=R), :] = gcv[:, :Q]
        g[pl.ds(r0 + 1, CH, stride=R), :] = gcv[:, Q:]
        grev[pl.ds(R - 1 - r0, CH, stride=R), :] = gcv[:, :Q]
        grev[pl.ds(R - 2 - r0, CH, stride=R), :] = gcv[:, Q:]
        return 0
    lax.fori_loop(0, R // 2, rows_step, 0)

    band = band_ref[...]
    nt = (((1,), (1,)), ((), ()))
    def out_block(i, _):
        los, his = [], []
        for j in range(CB):
            c = i * CB + j
            rows = pl.ds(c * R, R)
            up_ref[c] = (f_ref[c].astype(F) + ocean * u[rows, :]).astype(B)
            gc_ref[c] = g[rows, :].astype(B)
            dt = lax.dot_general(grev[rows, :].astype(B), im[c], nt, preferred_element_type=F)
            lo = pltpu.roll(dt[:, :Q] * band, 0, 1, stride=1, stride_axis=0)
            hi = jnp.concatenate([dt[:, Q:], jnp.zeros((R, 32), F)], axis=1)
            hi = pltpu.roll(hi * band, 0, 1, stride=1, stride_axis=0)
            los.append(jnp.sum(lo, axis=0, keepdims=True))
            his.append(jnp.sum(hi, axis=0, keepdims=True))
        dks[pl.ds(pl.multiple_of(i * CB, CB), CB), :Q] = jnp.concatenate(los, axis=0)
        dks[pl.ds(pl.multiple_of(i * CB, CB), CB), Q:] = jnp.concatenate(his, axis=0)
        return 0
    lax.fori_loop(0, CH // CB, out_block, 0)
    lane = lax.broadcasted_iota(jnp.int32, (CH, Q), 1) % 32
    def taps(x):
        own = pltpu.roll(x, Q - 12, 1)
        up = pltpu.roll(x, Q - 15, 1)
        low = pltpu.roll(x, Q - 31, 1)
        zero = jnp.zeros_like(x)
        return jnp.where(lane < 7, own, zero) + jnp.where((lane >= 4) & (lane < 7), up, zero) + jnp.where(lane < 3, low, zero)
    dk = taps(dks[:, :Q]) + pltpu.roll(taps(dks[:, Q:]), 8, 1)
    gg = jnp.sum(gacc[...], axis=1, keepdims=True)
    lane1 = lax.broadcasted_iota(jnp.int32, (CH, Q), 1)
    w_ref[pl.ds(12 * CH, CH), :] = jnp.where(lane1 == 127, gg, dk)
    w_ref[pl.ds(13 * CH, 64), :] = jnp.zeros((64, Q), F)
    for h in range(6):
        hs = slice(h * Q, (h + 1) * Q)
        w_ref[pl.ds(h * CH, CH), :] = lax.dot_general(mcb[...], act[hs, :], nt, preferred_element_type=F)
        w_ref[pl.ds((6 + h) * CH, CH), :] = lax.dot_general(sc[...], gh[hs, :], nt, preferred_element_type=F)


def front(e, t, fields, cot, land, gain, pi, po):
    vm = pl.BlockSpec(memory_space=pltpu.VMEM)
    return pl.pallas_call(
        front_kernel,
        out_shape=(jax.ShapeDtypeStruct((CH, R, Q), B), jax.ShapeDtypeStruct((CH, R, Q), B), jax.ShapeDtypeStruct((2560, Q), F)),
        in_specs=[vm] * 11, out_specs=(vm,) * 3,
        scratch_shapes=[
            pltpu.VMEM((CH, 224, Q), B), pltpu.VMEM((CH * R, Q), F), pltpu.VMEM((CH * R, Q), F),
            pltpu.VMEM((CH * R + R, Q), F), pltpu.VMEM((CH * R, Q), F), pltpu.VMEM((CH * R, Q), F),
            pltpu.VMEM((CH, R * Q), B), pltpu.VMEM((CH, R * Q), B), pltpu.VMEM((HID, R * Q), B), pltpu.VMEM((HID, R * Q), B),
            pltpu.VMEM((CH, Q), F), pltpu.VMEM((CH, 256), F),
        ],
        compiler_params=pltpu.CompilerParams(vmem_limit_bytes=56 << 20),
        name="front",
    )(e, t, fields, cot, land, gain.reshape(CH, 1), pi, pi.T, po, po.T, jnp.asarray(band_mask()))


def back_kernel(e_ref, t_ref, cot_ref, land_ref, o_ref, im):
    ocean = land_ref[...].astype(F)
    n = e_ref.shape[0]
    for c in range(n):
        for b in range(7):
            im[c, b * 32:(b + 1) * 32, :] = e_ref[c, :, b:b + Q]
    for c in range(n):
        gm = jnp.dot(t_ref[c], im[c], preferred_element_type=F)
        o_ref[c] = (cot_ref[c].astype(F) + ocean * gm).astype(B)


def back(e, t, cot, land):
    CB = 16
    return pl.pallas_call(
        back_kernel,
        grid=(CH // CB,),
        out_shape=jax.ShapeDtypeStruct((CH, R, Q), B),
        in_specs=[pl.BlockSpec((CB, 32, 134), lambda i: (i, 0, 0)), pl.BlockSpec((CB, R, 224), lambda i: (i, 0, 0)),
                  pl.BlockSpec((CB, R, Q), lambda i: (i, 0, 0)), pl.BlockSpec((R, Q), lambda i: (0, 0))],
        out_specs=pl.BlockSpec((CB, R, Q), lambda i: (i, 0, 0)),
        scratch_shapes=[pltpu.VMEM((CB, 224, Q), B)],
        compiler_params=pltpu.CompilerParams(vmem_limit_bytes=40 << 20),
        name="back",
    )(e, t, cot, land)


PLANES = ("x", "yh", "yl")
ALL = ("x", "yh", "z", "yl", "c")
LAT, LON = 8, 32


def lon_route(step):
    return [(y * LON + i, y * LON + (i + step) % LON) for y in range(LAT) for i in range(LON)]


def widen(block):
    left = lax.ppermute(block[:, :, Q - 3:], ALL, lon_route(1))
    right = lax.ppermute(block[:, :, :3], ALL, lon_route(-1))
    wide = jnp.concatenate([left, block, right], axis=2)
    low, high = wide[:, :3], wide[:, R - 3:]
    south = lax.ppermute(high, ALL, [(y * LON + i, (y + 1) * LON + i) for y in range(LAT - 1) for i in range(LON)])
    north = lax.ppermute(low, ALL, [(y * LON + i, (y - 1) * LON + i) for y in range(1, LAT) for i in range(LON)])
    top = LON * (LAT - 1)
    fold = lax.ppermute(high, ALL, [(top + i, top + LON - 1 - i) for i in range(LON)])
    mirror = jnp.asarray(np.eye(Q + 6)[::-1], B)
    fold = jnp.einsum("crq,qp->crp", fold[:, ::-1], mirror, preferred_element_type=F).astype(B)
    rest = jnp.zeros((CH, 10, Q + 6), B)
    return jnp.concatenate([wide, south, north + fold, rest], axis=1)


def exchange(value, axes, parts):
    return lax.all_to_all(jnp.broadcast_to(value[None], (parts,) + value.shape), axes, 0, 0)


def total(w):
    swap = [(i, i ^ 1) for i in range(256)]
    core = lax.axis_index("c")
    halves = w.reshape(2, 16, 80, Q)
    own = jnp.where(core == 0, halves[0], halves[1])
    other = jnp.where(core == 0, halves[1], halves[0]).astype(B)
    part = (own + lax.ppermute(other, ALL, swap).astype(F)).astype(B)
    part = lax.all_to_all(part, PLANES, 0, 0)
    part = jnp.sum(part.astype(F), axis=0).astype(B)
    part = exchange(part, ("z",), 8)
    part = (jnp.sum(part.astype(F), axis=0) * (128 * 4096) ** -0.5).astype(B)
    part = exchange(part, PLANES, 16)
    other = lax.ppermute(part, ALL, swap)
    first = jnp.where(core == 0, part, other).reshape(1280, Q)
    second = jnp.where(core == 0, other, part).reshape(1280, Q)
    return jnp.concatenate([first, second], axis=0)


def on_device(fields, cotangent, land_sea, kernel, ln_gain, proj_in, proj_out):
    lat = lax.axis_index("x") * 2 + lax.axis_index("yh")
    ocean = land_sea.astype(B)
    ext = widen(fields * ocean[None])
    updated, grad_conv, w = front(ext, toeplitz(kernel), fields, cotangent, land_sea, ln_gain, proj_in, proj_out)
    turned = jnp.flip(kernel, axis=(1, 2))
    grad_ext = widen(grad_conv)
    grad_fields = back(grad_ext, toeplitz(turned, jnp.where(lat == LAT - 1, kernel, turned)), cotangent, land_sea)
    w = total(w).astype(F)
    grad_out = w[:6 * CH].reshape(6, CH, Q).transpose(1, 0, 2).reshape(CH, HID)
    grad_in = w[6 * CH:12 * CH].reshape(6, CH, Q).transpose(0, 2, 1).reshape(HID, CH)
    tail = w[12 * CH:13 * CH]
    starts = [32 * (b % 4) + 8 * (b // 4) for b in range(7)]
    grad_kernel = jnp.stack([tail[:, i:i + 7] for i in starts], axis=2)
    return updated, grad_fields, grad_kernel, tail[:, Q - 1], grad_in, grad_out


def solution(mesh):
    fine = jax.sharding.Mesh(mesh.devices.reshape(4, 2, 8, 2, 2), ALL)
    P = jax.sharding.PartitionSpec
    lat, lon = ("x", "yh"), ("z", "yl", "c")
    block = P(None, lat, lon)
    return jax.shard_map(
        on_device,
        mesh=fine,
        in_specs=(block, block, P(lat, lon), P(), P(), P(), P()),
        out_specs=(block, block, P(), P(), P(), P()),
        check_vma=False,
    )
```

time: 462 us -> 190 us (0.41); the launches traced: 455 us -> 189 us
  waiting for transfers between devices: 203 us -> 29.5 us
  blocking collectives: 78.6 us -> 0 us
  matrix products: 66.7 us -> 9.31 us
  Pallas kernels: 0 us -> 49.7 us
  starting transfers between devices: 37 us -> 53.5 us
  between operations: 14.8 us -> 1.05 us
  local copies, waits for them, and re-layouts: 37.7 us -> 24 us
    psum x1 -> x0, waiting for transfers between devices: 136 us -> none  [on_device(): summed = lax.psum((grad_kern, grad_gain, grad_in, grad_out), ('lat', 'lon'))]
    psum x1 -> x0, blocking collectives: 78.6 us -> none  [on_device(): summed = lax.psum((grad_kern, grad_gain, grad_in, grad_out), ('lat', 'lon'))]
    pallas_call x0 -> x2, Pallas kernels: none -> 49.7 us  [the longest x1 40.1 us: front(): pl.pallas_call(front_kernel, out_shape=(jax.ShapeDtypeStruct((CH, R, Q),...]
    conv_general_dilated x3 -> x0, matrix products: 44.4 us -> none  [depthwise(): lax.conv_general_dilated(source[None], weights[:, None], (1, 1), 'VALID',...]
    ppermute x18 -> x12, waiting for transfers between devices: 66.4 us -> 24.7 us  [the longest x2 24.7 us: widen(): lax.ppermute(low, ALL, [(y * LON + i, (y - 1) * LON + i) for y in range(1...]
    all_to_all x0 -> x3, starting transfers between devices: none -> 29 us  [the longest x2 14.9 us: exchange(): lax.all_to_all(jnp.broadcast_to(value[None], (parts,) + value.shape), axe...]
    dot_general x6 -> x5, matrix products: 22.3 us -> 9.31 us  [the longest x1 3.98 us: toeplitz(): jnp.einsum('cab,ars->crbs', north, jnp.asarray(up, B), preferred_element_...]
    ppermute x18 -> x12, starting transfers between devices: 37 us -> 24.5 us  [the longest x2 9.25 us: widen(): lax.ppermute(high, ALL, [(y * LON + i, (y + 1) * LON + i) for y in range(...]
  transfers between devices with their start and end apart: 19 -> 15, of which waited for: 13 -> 4; matrix products, arithmetic and copies ran while one was open for 14% -> 20% of each run, Pallas kernels for 0% -> 5%
where the time goes in v1:
time: 190 us; the launch traced here: 189 us
  starting transfers between devices  53.5 us (28%)
  Pallas kernels  49.7 us (26%)
  waiting for transfers between devices  29.5 us (16%)
  local copies, waits for them, and re-layouts  24 us (13%)
  other arithmetic  21.8 us (11%)
  matrix products  9.31 us (5%)
    pallas_call x1, Pallas kernels, front(): pl.pallas_call(front_kernel, out_shape=(jax.ShapeDtypeStruct((CH, R, Q),...  40.1 us
    ppermute x2, waiting for transfers between devices, widen(): lax.ppermute(low, ALL, [(y * LON + i, (y - 1) * LON + i) for y in range(1...  24.7 us
    all_to_all x2, starting transfers between devices, exchange(): lax.all_to_all(jnp.broadcast_to(value[None], (parts,) + value.shape), axe...  14.9 us
    all_to_all x1, starting transfers between devices, total(): part = lax.all_to_all(part, PLANES, 0, 0)  14 us
    pallas_call x1, Pallas kernels, back(): pl.pallas_call(back_kernel, grid=(CH // CB,), out_shape=jax.ShapeDtypeStr...  9.66 us
    ppermute x2, starting transfers between devices, widen(): lax.ppermute(high, ALL, [(y * LON + i, (y + 1) * LON + i) for y in range(...  9.25 us
    concatenate x2, other arithmetic, widen(): return jnp.concatenate([wide, south, north + fold, rest], axis=1)  7.86 us
    ppermute x2, starting transfers between devices, widen(): lax.ppermute(low, ALL, [(y * LON + i, (y - 1) * LON + i) for y in range(1...  6.43 us
  transfers between devices with their start and end apart: 15, of which 4 were waited for; matrix products, arithmetic and copies ran while one was open for 20% of the time, Pallas kernels for 5%

profile of v1, /device:TPU:3, one launch (start us, length us, event | category | flops | bytes accessed | tf_op | source)
XLA Modules:
  0.0 188.9 jit_solution(16837718118846754316)
XLA Ops:
  1.4 1.2 broadcast_multiply_fusion
  3.7 1.9 %collective-permute-start = (bf16[192,16,3]{0,1,2:T(8,128)(2,1)S(1)}, bf16[192,16,3]{0,1,2:T(8,128)(2,1)S(1)}, u32[]{:S(2)}, u32[]{:S(2)}) collective-permute-start(bf16[192,16,3]{0,1,2:T(8,128)(2,1)S(1)} %copy.104), channel_id=1, source_target_pairs={{0,1},{1,2},{2,3},{3,4},{4,5},{5,6},{6,7},{7,8},{8,9},{9,10},{10,1... | collective-permute-start | bytes 55304 | tf_op jit(solution)/shard_map/ppermute | solution.py:213
  10.7 2.0 %pad_maximum_fusion.5 = (bf16[192,3,134]{2,1,0:T(4,128)(2,1)}, bf16[192,3,134]{2,1,0:T(4,128)(2,1)}) fusion(bf16[192,16,3]{2,1,0:T(8,128)(2,1)S(1)} %copy.107, bf16[192,16,128]{2,1,0:T(8,128)(2,1)S(1)} %broadcast_multiply_fusion, bf16[192,16,3]{2,1,0:T(8,128)(2,1)S(1)} %copy.106), kind=kLoop, calls=%fused_computation.15 | loop fusion | flops 926208 | bytes 1132032 | tf_op jit(solution)/shard_map/slice | solution.py:216
  12.7 1.6 collective-permute-start.4
  14.2 1.5 convolution_convert_fusion
  15.7 2.5 %copy.112.t_ref = bf16[192,16,224]{2,1,0:T(8,128)(2,1)} copy(bf16[192,16,224]{0,2,1:T(8,128)(2,1)S(1)} %bitcast.68) | data formatting | bytes 2752512 | tf_op jit(solution)/shard_map/reshape | solution.py:32
  18.3 4.7 %collective-permute-start.2 = (bf16[192,3,134]{2,1,0:T(4,128)(2,1)}, bf16[192,3,134]{2,1,0:T(4,128)(2,1)}, u32[]{:S(2)}, u32[]{:S(2)}) collective-permute-start(bf16[192,3,134]{2,1,0:T(4,128)(2,1)} %get-tuple-element.26), channel_id=1, source_target_pairs={{0,32},{1,33},{2,34},{3,35},{4,36},{5,37},{6,38},{7,39},{8,40},{9,... | collective-permute-start | bytes 463112 | tf_op jit(solution)/shard_map/ppermute | solution.py:217
  22.9 3.3 %collective-permute-start.3 = (bf16[192,3,134]{2,1,0:T(4,128)(2,1)}, bf16[192,3,134]{2,1,0:T(4,128)(2,1)}, u32[]{:S(2)}, u32[]{:S(2)}) collective-permute-start(bf16[192,3,134]{2,1,0:T(4,128)(2,1)} %get-tuple-element.27), channel_id=1, source_target_pairs={{32,0},{33,1},{34,2},{35,3},{36,4},{37,5},{38,6},{39,7},{40,8},{41... | collective-permute-start | bytes 463112 | tf_op jit(solution)/shard_map/ppermute | solution.py:218
  26.3 2.5 %rev.10 = bf16[192,3,134]{2,1,0:T(4,128)(2,1)S(1)} reverse(bf16[192,3,134]{2,1,0:T(4,128)(2,1)} %collective-permute-done.4), dimensions={1} | reverse | bytes 308736 | tf_op jit(solution)/shard_map/rev | solution.py:222
  29.4 11.7 %collective-permute-done.3 = bf16[192,3,134]{2,1,0:T(4,128)(2,1)} collective-permute-done((bf16[192,3,134]{2,1,0:T(4,128)(2,1)}, bf16[192,3,134]{2,1,0:T(4,128)(2,1)}, u32[]{:S(2)}, u32[]{:S(2)}) %collective-permute-start.3) | collective-permute-done | bytes 154400 | tf_op jit(solution)/shard_map/ppermute | solution.py:218
  41.1 1.2 add.28
  42.3 4.3 %maximum_maximum_fusion.e_ref = bf16[192,32,134]{2,1,0:T(8,128)(2,1)} fusion(bf16[192,3,134]{2,1,0:T(4,128)(2,1)S(1)} %add.28, bf16[192,3,134]{2,1,0:T(4,128)(2,1)} %collective-permute-done.2, bf16[192,16,3]{2,1,0:T(8,128)(2,1)S(1)} %copy-done.6, bf16[192,16,128]{2,1,0:T(8,128)(2,1)S(1)} %broadcast_multiply_fusion, bf16[192,16,3]{2,1,0:T(8,128)(2,1)S(1)} %copy.106, ...), kind=kLoop, calls=%fused_computation.2 | loop fusion | flops 9879552 | bytes 2778688 | tf_op jit(solution)/shard_map/concatenate | solution.py:224
  46.6 40.1 %front.1 = (bf16[192,16,128]{2,1,0:T(8,128)(2,1)}, bf16[192,16,128]{2,1,0:T(8,128)(2,1)}, f32[2560,128]{1,0:T(8,128)}) custom-call(bf16[192,32,134]{2,1,0:T(8,128)(2,1)} %maximum_maximum_fusion.e_ref, bf16[192,16,224]{2,1,0:T(8,128)(2,1)} %copy.112.t_ref, bf16[192,16,128]{2,1,0:T(8,128)(2,1)} %f_ref.1, bf16[192,16,128]{2,1,0:T(8,128)(2,1)} %cot_ref.3, ...), custom_call_target="tpu_custom_call" | custom-call | tf_op jit(solution)/shard_map/front/pallas_call | solution.py:162
  86.7 1.4 select_convert_fusion
  88.1 2.0 %collective-permute-start.10 = (bf16[16,80,128]{2,1,0:T(8,128)(2,1)S(1)}, bf16[16,80,128]{2,1,0:T(8,128)(2,1)S(1)}, u32[]{:S(2)}, u32[]{:S(2)}) collective-permute-start(bf16[16,80,128]{2,1,0:T(8,128)(2,1)S(1)} %bitcast.80), channel_id=1, source_target_pairs={{0,1},{1,0},{2,3},{3,2},{4,5},{5,4},{6,7},{7,6},{8,9},{9,8},{10,11... | collective-permute-start | bytes 983048 | tf_op jit(solution)/shard_map/ppermute | solution.py:237
  90.0 1.4 slice_select_fusion
  92.2 14.0 %all-to-all-start = ((bf16[16,80,128]{2,1,0:T(8,128)(2,1)}), bf16[16,80,128]{2,1,0:T(8,128)(2,1)S(1)}, u32[]{:S(2)}, u32[]{:S(2)}) async-start(bf16[16,80,128]{2,1,0:T(8,128)(2,1)} %add_convert_fusion), calls=%async_computation | async-start | bytes 655360 | tf_op jit(solution)/shard_map/all_to_all | solution.py:238
  106.3 2.5 %fusion.7 = f32[16,32,192,7]{2,1,3,0:T(8,128)} fusion(bf16[7,16,32,1]{2,0,3,1:T(8,128)(2,1)S(1)} %copy-done.12, bf16[192,7,7]{0,2,1:T(8,128)(2,1)S(1)} %rev.12), kind=kOutput, calls=%fused_computation.39 | convolution fusion | flops 9633792 | bytes 2778496 | tf_op jit(solution)/shard_map/cab,ars->crbs/dot_general | solution.py:30
  111.4 1.2 collective-permute-start.5
  113.7 6.1 %all-to-all-start.1 = ((bf16[8,80,128]{2,1,0:T(8,128)(2,1)}), bf16[8,80,128]{2,1,0:T(8,128)(2,1)S(1)}, u32[]{:S(2)}, u32[]{:S(2)}) async-start(bf16[8,80,128]{2,1,0:T(8,128)(2,1)} %broadcast_in_dim.4), calls=%async_computation.1 | async-start | bytes 327680 | tf_op jit(solution)/shard_map/all_to_all | solution.py:228
  121.3 1.9 pad_maximum_fusion.2
  123.8 4.4 %all-to-all-done.1 = bf16[8,80,128]{2,1,0:T(8,128)(2,1)S(1)} async-done(((bf16[8,80,128]{2,1,0:T(8,128)(2,1)}), bf16[8,80,128]{2,1,0:T(8,128)(2,1)S(1)}, u32[]{:S(2)}, u32[]{:S(2)}) %all-to-all-start.1) | async-done | bytes 163872 | tf_op jit(solution)/shard_map/all_to_all | solution.py:228
  129.0 8.8 %all-to-all-start.2 = ((bf16[16,80,128]{2,1,0:T(8,128)(2,1)}), bf16[16,80,128]{2,1,0:T(8,128)(2,1)}, u32[]{:S(2)}, u32[]{:S(2)}) async-start(bf16[16,80,128]{2,1,0:T(8,128)(2,1)} %broadcast_in_dim.5), calls=%async_computation.2 | async-start | bytes 655360 | tf_op jit(solution)/shard_map/all_to_all | solution.py:228
  137.9 4.0 %fusion = bf16[192,16,7,32]{0,3,2,1:T(8,128)(2,1)} fusion(f32[16,32,192,7]{2,1,3,0:T(8,128)} %fusion.7, bf16[7,16,32,1]{2,0,3,1:T(8,128)(2,1)S(1)} %copy-done.11, bf16[192,7,7]{0,2,1:T(8,128)(2,1)S(1)} %broadcast_select_fusion.2), kind=kOutput, calls=%fused_computation.1 | convolution fusion | flops 11010048 | bytes 4154752 | tf_op jit(solution)/shard_map/cab,ars->crbs/dot_general | solution.py:31
  141.8 3.4 %copy.123.t_ref = bf16[192,16,224]{2,1,0:T(8,128)(2,1)S(1)} copy(bf16[192,16,224]{0,2,1:T(8,128)(2,1)} %bitcast.67) | data formatting | bytes 2752512 | tf_op jit(solution)/shard_map/reshape | solution.py:32
  145.3 4.6 %collective-permute-start.7 = (bf16[192,3,134]{2,1,0:T(4,128)(2,1)}, bf16[192,3,134]{2,1,0:T(4,128)(2,1)}, u32[]{:S(2)}, u32[]{:S(2)}) collective-permute-start(bf16[192,3,134]{2,1,0:T(4,128)(2,1)} %get-tuple-element.24), channel_id=1, source_target_pairs={{0,32},{1,33},{2,34},{3,35},{4,36},{5,37},{6,38},{7,39},{8,40},{9,... | collective-permute-start | bytes 463112 | tf_op jit(solution)/shard_map/ppermute | solution.py:217
  149.9 3.1 %collective-permute-start.8 = (bf16[192,3,134]{2,1,0:T(4,128)(2,1)S(1)}, bf16[192,3,134]{2,1,0:T(4,128)(2,1)}, u32[]{:S(2)}, u32[]{:S(2)}) collective-permute-start(bf16[192,3,134]{2,1,0:T(4,128)(2,1)S(1)} %get-tuple-element.25), channel_id=1, source_target_pairs={{32,0},{33,1},{34,2},{35,3},{36,4},{37,5},{38,6},{39,7},{40,8},{41... | collective-permute-start | bytes 463112 | tf_op jit(solution)/shard_map/ppermute | solution.py:218
  153.0 1.2 rev.11
  156.3 13.0 %collective-permute-done.8 = bf16[192,3,134]{2,1,0:T(4,128)(2,1)} collective-permute-done((bf16[192,3,134]{2,1,0:T(4,128)(2,1)S(1)}, bf16[192,3,134]{2,1,0:T(4,128)(2,1)}, u32[]{:S(2)}, u32[]{:S(2)}) %collective-permute-start.8) | collective-permute-done | bytes 154400 | tf_op jit(solution)/shard_map/ppermute | solution.py:218
  169.3 1.3 add.27
  171.2 3.5 %maximum_maximum_fusion.1.e_ref = bf16[192,32,134]{2,1,0:T(8,128)(2,1)S(1)} fusion(bf16[192,3,134]{2,1,0:T(4,128)(2,1)S(1)} %add.27, bf16[192,3,134]{2,1,0:T(4,128)(2,1)} %collective-permute-done.7, bf16[192,16,3]{2,1,0:T(8,128)(2,1)} %copy-done.4, bf16[192,16,128]{2,1,0:T(8,128)(2,1)S(1)} %copy-done.2, bf16[192,16,3]{2,1,0:T(8,128)(2,1)} %copy-done.3, ...), kind=kLoop, calls=%fused_computation.3 | loop fusion | flops 9879552 | bytes 2778688 | tf_op jit(solution)/shard_map/concatenate | solution.py:224
  174.8 9.7 %back.1 = bf16[192,16,128]{2,1,0:T(8,128)(2,1)} custom-call(bf16[192,32,134]{2,1,0:T(8,128)(2,1)S(1)} %maximum_maximum_fusion.1.e_ref, bf16[192,16,224]{2,1,0:T(8,128)(2,1)S(1)} %copy.123.t_ref, bf16[192,16,128]{2,1,0:T(8,128)(2,1)S(1)} %copy-done, s32[16,128]{1,0:T(8,128)S(1)} %copy-done.1), custom_call_target="tpu_custom_call" | custom-call | tf_op jit(solution)/shard_map/back/pallas_call | solution.py:190
  (85 shorter events, 22.0 us)
Async XLA Ops:
  0.6 5.8 %copy-start.10 = (bf16[192,7,7]{0,2,1:T(8,128)(2,1)S(1)}, bf16[192,7,7]{0,2,1:T(8,128)(2,1)}, u32[]{:S(2)}) copy-start(bf16[192,7,7]{0,2,1:T(8,128)(2,1)} %param.16) | copy-start | bytes 56452
  0.6 5.9 %copy-start.13 = (f32[192]{0:T(256)S(1)}, f32[192]{0:T(256)}, u32[]{:S(2)}) copy-start(f32[192]{0:T(256)} %param.17) | copy-start | bytes 2308
  0.7 6.7 %copy-start.7 = (bf16[768,192]{0,1:T(8,128)(2,1)S(1)}, bf16[768,192]{0,1:T(8,128)(2,1)}, u32[]{:S(2)}) copy-start(bf16[768,192]{0,1:T(8,128)(2,1)} %param.18) | copy-start | bytes 884740
  0.7 7.6 %copy-start.8 = (bf16[192,768]{1,0:T(8,128)(2,1)S(1)}, bf16[192,768]{1,0:T(8,128)(2,1)}, u32[]{:S(2)}) copy-start(bf16[192,768]{1,0:T(8,128)(2,1)} %po_ref.1) | copy-start | bytes 884740
  3.7 5.5 %collective-permute-start = (bf16[192,16,3]{0,1,2:T(8,128)(2,1)S(1)}, bf16[192,16,3]{0,1,2:T(8,128)(2,1)S(1)}, u32[]{:S(2)}, u32[]{:S(2)}) collective-permute-start(bf16[192,16,3]{0,1,2:T(8,128)(2,1)S(1)} %copy.104), channel_id=1, source_target_pairs={{0,1},{1,2},{2,3},{3,4},{4,5},{5,6},{6,7},{7,8},{8,9},{9,10},{10,1... | collective-permute-start | bytes 55304 | tf_op jit(solution)/shard_map/ppermute | solution.py:213
  6.3 3.6 %collective-permute-start.1 = (bf16[192,16,3]{0,1,2:T(8,128)(2,1)S(1)}, bf16[192,16,3]{0,1,2:T(8,128)(2,1)S(1)}, u32[]{:S(2)}, u32[]{:S(2)}) collective-permute-start(bf16[192,16,3]{0,1,2:T(8,128)(2,1)S(1)} %copy.105), channel_id=1, source_target_pairs={{0,31},{1,0},{2,1},{3,2},{4,3},{5,4},{6,5},{7,6},{8,7},{9,8},{10,9... | collective-permute-start | bytes 55304 | tf_op jit(solution)/shard_map/ppermute | solution.py:214
  10.6 2.0 %copy-start.5 = (bf16[192,16,3]{2,1,0:T(8,128)(2,1)}, bf16[192,16,3]{2,1,0:T(8,128)(2,1)S(1)}, u32[]{:S(2)}) copy-start(bf16[192,16,3]{2,1,0:T(8,128)(2,1)S(1)} %copy.107) | copy-start | bytes 55300
  12.7 16.1 %copy-start.9 = (bf16[134,134,1]{0,1,2:T(8,128)(2,1)S(1)}, bf16[134,134,1]{0,1,2:T(8,128)(2,1)}, u32[]{:S(2)}) copy-start(bf16[134,134,1]{0,1,2:T(8,128)(2,1)} %constant.42) | copy-start | bytes 107740
  12.7 13.6 %collective-permute-start.4 = (bf16[192,3,134]{2,1,0:T(4,128)(2,1)}, bf16[192,3,134]{2,1,0:T(4,128)(2,1)}, u32[]{:S(2)}, u32[]{:S(2)}) collective-permute-start(bf16[192,3,134]{2,1,0:T(4,128)(2,1)} %get-tuple-element.26), channel_id=1, source_target_pairs={{224,255},{225,254},{226,253},{227,252},{228,251},{229,250},{230,2... | collective-permute-start | bytes 463112 | tf_op jit(solution)/shard_map/ppermute | solution.py:220
  18.2 24.1 %copy-start.6 = (bf16[192,16,3]{2,1,0:T(8,128)(2,1)S(1)}, bf16[192,16,3]{2,1,0:T(8,128)(2,1)}, u32[]{:S(2)}) copy-start(bf16[192,16,3]{2,1,0:T(8,128)(2,1)} %copy-done.5) | copy-start | bytes 55300
  18.3 24.0 %collective-permute-start.2 = (bf16[192,3,134]{2,1,0:T(4,128)(2,1)}, bf16[192,3,134]{2,1,0:T(4,128)(2,1)}, u32[]{:S(2)}, u32[]{:S(2)}) collective-permute-start(bf16[192,3,134]{2,1,0:T(4,128)(2,1)} %get-tuple-element.26), channel_id=1, source_target_pairs={{0,32},{1,33},{2,34},{3,35},{4,36},{5,37},{6,38},{7,39},{8,40},{9,... | collective-permute-start | bytes 463112 | tf_op jit(solution)/shard_map/ppermute | solution.py:217
  22.9 18.1 %collective-permute-start.3 = (bf16[192,3,134]{2,1,0:T(4,128)(2,1)}, bf16[192,3,134]{2,1,0:T(4,128)(2,1)}, u32[]{:S(2)}, u32[]{:S(2)}) collective-permute-start(bf16[192,3,134]{2,1,0:T(4,128)(2,1)} %get-tuple-element.27), channel_id=1, source_target_pairs={{32,0},{33,1},{34,2},{35,3},{36,4},{37,5},{38,6},{39,7},{40,8},{41... | collective-permute-start | bytes 463112 | tf_op jit(solution)/shard_map/ppermute | solution.py:218
  86.7 19.6 %copy-start.12 = (bf16[7,16,32,1]{2,0,3,1:T(8,128)(2,1)S(1)}, bf16[7,16,32,1]{2,0,3,1:T(8,128)(2,1)}, u32[]{:S(2)}) copy-start(bf16[7,16,32,1]{2,0,3,1:T(8,128)(2,1)} %constant.44) | copy-start | bytes 21508
  88.1 20.7 %copy-start.2 = (bf16[192,16,128]{2,1,0:T(8,128)(2,1)S(1)}, bf16[192,16,128]{2,1,0:T(8,128)(2,1)}, u32[]{:S(2)}) copy-start(bf16[192,16,128]{2,1,0:T(8,128)(2,1)} %get-tuple-element.10) | copy-start | bytes 2359300
  88.1 3.3 %collective-permute-start.10 = (bf16[16,80,128]{2,1,0:T(8,128)(2,1)S(1)}, bf16[16,80,128]{2,1,0:T(8,128)(2,1)S(1)}, u32[]{:S(2)}, u32[]{:S(2)}) collective-permute-start(bf16[16,80,128]{2,1,0:T(8,128)(2,1)S(1)} %bitcast.80), channel_id=1, source_target_pairs={{0,1},{1,0},{2,3},{3,2},{4,5},{5,4},{6,7},{7,6},{8,9},{9,8},{10,11... | collective-permute-start | bytes 983048 | tf_op jit(solution)/shard_map/ppermute | solution.py:237
  92.2 20.7 %all-to-all-start = ((bf16[16,80,128]{2,1,0:T(8,128)(2,1)}), bf16[16,80,128]{2,1,0:T(8,128)(2,1)S(1)}, u32[]{:S(2)}, u32[]{:S(2)}) async-start(bf16[16,80,128]{2,1,0:T(8,128)(2,1)} %add_convert_fusion), calls=%async_computation | async-start | bytes 655360 | tf_op jit(solution)/shard_map/all_to_all | solution.py:238
  110.5 27.3 %copy-start.11 = (bf16[7,16,32,1]{2,0,3,1:T(8,128)(2,1)S(1)}, bf16[7,16,32,1]{2,0,3,1:T(8,128)(2,1)}, u32[]{:S(2)}) copy-start(bf16[7,16,32,1]{2,0,3,1:T(8,128)(2,1)} %constant.45) | copy-start | bytes 21508
  110.5 10.0 %collective-permute-start.6 = (bf16[192,16,3]{0,1,2:T(8,128)(2,1)S(1)}, bf16[192,16,3]{0,1,2:T(8,128)(2,1)S(1)}, u32[]{:S(2)}, u32[]{:S(2)}) collective-permute-start(bf16[192,16,3]{0,1,2:T(8,128)(2,1)S(1)} %copy.116), channel_id=1, source_target_pairs={{0,31},{1,0},{2,1},{3,2},{4,3},{5,4},{6,5},{7,6},{8,7},{9,8},{10,9... | collective-permute-start | bytes 55304 | tf_op jit(solution)/shard_map/ppermute | solution.py:214
  111.4 8.4 %collective-permute-start.5 = (bf16[192,16,3]{0,1,2:T(8,128)(2,1)S(1)}, bf16[192,16,3]{0,1,2:T(8,128)(2,1)S(1)}, u32[]{:S(2)}, u32[]{:S(2)}) collective-permute-start(bf16[192,16,3]{0,1,2:T(8,128)(2,1)S(1)} %copy.115), channel_id=1, source_target_pairs={{0,1},{1,2},{2,3},{3,4},{4,5},{5,6},{6,7},{7,8},{8,9},{9,10},{10,1... | collective-permute-start | bytes 55304 | tf_op jit(solution)/shard_map/ppermute | solution.py:213
  113.7 14.5 %all-to-all-start.1 = ((bf16[8,80,128]{2,1,0:T(8,128)(2,1)}), bf16[8,80,128]{2,1,0:T(8,128)(2,1)S(1)}, u32[]{:S(2)}, u32[]{:S(2)}) async-start(bf16[8,80,128]{2,1,0:T(8,128)(2,1)} %broadcast_in_dim.4), calls=%async_computation.1 | async-start | bytes 327680 | tf_op jit(solution)/shard_map/all_to_all | solution.py:228
  120.5 21.3 %copy-start.3 = (bf16[192,16,3]{2,1,0:T(8,128)(2,1)}, bf16[192,16,3]{2,1,0:T(8,128)(2,1)S(1)}, u32[]{:S(2)}) copy-start(bf16[192,16,3]{2,1,0:T(8,128)(2,1)S(1)} %copy.117) | copy-start | bytes 55300
  121.2 20.6 %copy-start.4 = (bf16[192,16,3]{2,1,0:T(8,128)(2,1)}, bf16[192,16,3]{2,1,0:T(8,128)(2,1)S(1)}, u32[]{:S(2)}) copy-start(bf16[192,16,3]{2,1,0:T(8,128)(2,1)S(1)} %copy.118) | copy-start | bytes 55300
  123.1 29.8 %collective-permute-start.9 = (bf16[192,3,134]{2,1,0:T(4,128)(2,1)}, bf16[192,3,134]{2,1,0:T(4,128)(2,1)S(1)}, u32[]{:S(2)}, u32[]{:S(2)}) collective-permute-start(bf16[192,3,134]{2,1,0:T(4,128)(2,1)} %get-tuple-element.24), channel_id=1, source_target_pairs={{224,255},{225,254},{226,253},{227,252},{228,251},{229,250},{230,2... | collective-permute-start | bytes 463112 | tf_op jit(solution)/shard_map/ppermute | solution.py:220
  129.0 41.6 %all-to-all-start.2 = ((bf16[16,80,128]{2,1,0:T(8,128)(2,1)}), bf16[16,80,128]{2,1,0:T(8,128)(2,1)}, u32[]{:S(2)}, u32[]{:S(2)}) async-start(bf16[16,80,128]{2,1,0:T(8,128)(2,1)} %broadcast_in_dim.5), calls=%async_computation.2 | async-start | bytes 655360 | tf_op jit(solution)/shard_map/all_to_all | solution.py:228
  145.3 26.0 %collective-permute-start.7 = (bf16[192,3,134]{2,1,0:T(4,128)(2,1)}, bf16[192,3,134]{2,1,0:T(4,128)(2,1)}, u32[]{:S(2)}, u32[]{:S(2)}) collective-permute-start(bf16[192,3,134]{2,1,0:T(4,128)(2,1)} %get-tuple-element.24), channel_id=1, source_target_pairs={{0,32},{1,33},{2,34},{3,35},{4,36},{5,37},{6,38},{7,39},{8,40},{9,... | collective-permute-start | bytes 463112 | tf_op jit(solution)/shard_map/ppermute | solution.py:217
  149.9 19.5 %collective-permute-start.8 = (bf16[192,3,134]{2,1,0:T(4,128)(2,1)S(1)}, bf16[192,3,134]{2,1,0:T(4,128)(2,1)}, u32[]{:S(2)}, u32[]{:S(2)}) collective-permute-start(bf16[192,3,134]{2,1,0:T(4,128)(2,1)S(1)} %get-tuple-element.25), channel_id=1, source_target_pairs={{32,0},{33,1},{34,2},{35,3},{36,4},{37,5},{38,6},{39,7},{40,8},{41... | collective-permute-start | bytes 463112 | tf_op jit(solution)/shard_map/ppermute | solution.py:218
  156.3 18.5 %copy-start = (bf16[192,16,128]{2,1,0:T(8,128)(2,1)S(1)}, bf16[192,16,128]{2,1,0:T(8,128)(2,1)}, u32[]{:S(2)}) copy-start(bf16[192,16,128]{2,1,0:T(8,128)(2,1)} %cot_ref.3) | copy-start | bytes 2359300
  156.3 18.5 %copy-start.1 = (s32[16,128]{1,0:T(8,128)S(1)}, s32[16,128]{1,0:T(8,128)}, u32[]{:S(2)}) copy-start(s32[16,128]{1,0:T(8,128)} %land_ref.3) | copy-start | bytes 24580
  170.7 13.8 %collective-permute-start.11 = (bf16[16,80,128]{2,1,0:T(8,128)(2,1)}, bf16[16,80,128]{2,1,0:T(8,128)(2,1)S(1)}, u32[]{:S(2)}, u32[]{:S(2)}) collective-permute-start(bf16[16,80,128]{2,1,0:T(8,128)(2,1)} %all-to-all-done.2), channel_id=1, source_target_pairs={{0,1},{1,0},{2,3},{3,2},{4,5},{5,4},{6,7},{7,6},{8,9},{9,8},{10,11... | collective-permute-start | bytes 983048 | tf_op jit(solution)/shard_map/ppermute | solution.py:243

commit v2 on v1

v2 whole, which is shorter than its diff:
```python
import numpy as np
import jax
import jax.numpy as jnp
from jax import lax
from jax.experimental import pallas as pl
from jax.experimental.pallas import tpu as pltpu

CH, HID, R, Q = 192, 768, 16, 128
TAPS = 176
BLOCKS = 32
MSG = 3 * CH + 96
F, B = jnp.float32, jnp.bfloat16
C0 = 0.7978845608028654
C1 = C0 * 0.044715
NT = (((1,), (1,)), ((), ()))
VM = pl.BlockSpec(memory_space=pltpu.VMEM)
SM = pl.BlockSpec(memory_space=pltpu.SMEM)


def rim_base(b):
    return 112 + 8 * b if b < 2 else 128 + 8 * (b - 2)


def turn(base, shift):
    return base // 128 * 128 + (base % 128 + shift) % 128


def tables():
    inner = np.zeros((49, 256), np.float32)
    upper = np.zeros((49, 256), np.float32)
    valid = np.zeros((R, 256), np.float32)
    collect = np.zeros((256, Q), np.float32)
    for b in range(7):
        own, rim = 16 * b, rim_base(b)
        for a in range(7):
            tap, goal = a * 7 + b, 8 * a + b
            inner[tap, turn(own, a - 3)] += 1
            collect[turn(own, a + 12), goal] += 1
            if a < 3:
                inner[tap, turn(rim, a)] += 1
                collect[turn(rim, a + 15), goal] += 1
            if a > 3:
                upper[tap, turn(rim, a - 15)] += 1
                collect[turn(rim, a), goal] += 1
        for r in range(R):
            for a in range(7):
                row = r + a
                if 3 <= row < R + 3:
                    valid[r, own + row - 3] = 1
                elif row < 3:
                    valid[r, rim + row] = 1
                else:
                    valid[r, rim + row - 15] = 1
    assert (inner + upper).sum(0).max() == 1 and collect.sum(1).max() == 1
    return inner, upper, valid, collect


INNER, UPPER, VALID, COLLECT = tables()


def lanes(rows):
    return lax.broadcasted_iota(jnp.int32, (rows, Q), 1)


def shifted(own, side, step, lane):
    if step == 0:
        return own
    if step > 0:
        return pltpu.roll(jnp.where(lane < step, side, own), Q - step, 1)
    return pltpu.roll(jnp.where(lane >= Q + step, side, own), -step, 1)


def pack_sides(tile, c, held, lane):
    j = c % 16
    moved = pltpu.roll(tile, 8 * j + 3, 1)
    return moved if held is None else jnp.where(lane >= 8 * j, moved, held)


def prepare_kernel(at_ref, taps_ref, tab_ref, valid_ref, pit_ref, po_ref, gain_ref, t1_ref, t2_ref, pi_ref, pot_ref, col_ref, k1, k2):
    def spread_taps(n):
        cut = slice(n * 256, (n + 1) * 256)
        parts = [lax.dot_general(taps_ref[a], tab_ref[a, :, cut], (((0,), (0,)), ((), ())), preferred_element_type=F) for a in range(7)]
        return sum(parts[1:], parts[0])
    k1[...] = spread_taps(0)
    k2[...] = spread_taps(1)

    @pl.when(at_ref[0] != 0)
    def _():
        k2[...] = spread_taps(2)

    def block(i, _):
        rows = pl.ds(pl.multiple_of(i * 16, 16), 16)
        for src, dst in ((k1, t1_ref), (k2, t2_ref)):
            k = src[rows, :]
            for j in range(16):
                for h in range(2):
                    cut = slice(h * Q, (h + 1) * Q)
                    x = jnp.broadcast_to(k[j:j + 1, cut], (R, Q))
                    x = pltpu.roll(x, 0, 1, stride=1, stride_axis=0) * valid_ref[:, cut]
                    dst[i * 16 + j, :, cut] = x.astype(B)
        return 0
    lax.fori_loop(0, CH // 16, block, 0)
    pi_ref[...] = jnp.transpose(pit_ref[...].astype(F)).astype(B)
    pot_ref[...] = jnp.transpose(po_ref[...].astype(F)).astype(B)
    col_ref[...] = jnp.transpose(jnp.broadcast_to(gain_ref[...], (8, CH)))[:, :1]


def prepare(at, kernel, pit, po, gain):
    tab = np.concatenate([INNER + UPPER, (INNER + UPPER)[::-1], INNER[::-1] + UPPER], axis=1)
    mat = jax.ShapeDtypeStruct((CH, R, 256), B)
    return pl.pallas_call(
        prepare_kernel,
        out_shape=(mat, mat, jax.ShapeDtypeStruct((HID, CH), B), jax.ShapeDtypeStruct((HID, CH), B), jax.ShapeDtypeStruct((CH, 1), F)),
        in_specs=[SM] + [VM] * 6, out_specs=(VM,) * 5, name="prepare",
        scratch_shapes=[pltpu.VMEM((CH, 256), F)] * 2,
        compiler_params=pltpu.CompilerParams(vmem_limit_bytes=56 << 20),
        cost_estimate=pl.CostEstimate(flops=1 << 30, bytes_accessed=8 << 20, transcendentals=0),
    )(at, kernel.transpose(1, 2, 0), jnp.asarray(tab.reshape(7, 7, 768), B), jnp.asarray(VALID), pit, po, gain.reshape(1, CH))


def start_kernel(f_ref, land_ref, m_ref, side_ref, low_ref, high_ref, s):
    ocean = land_ref[...].astype(F)
    lane = lanes(R)
    def block(i, _):
        for t in range(2):
            held = None
            for j in range(16):
                c = i * 32 + t * 16 + j
                x = f_ref[c].astype(F) * ocean
                s[pl.ds(c * R, R), :] = x
                x = x.astype(B)
                m_ref[c] = x
                held = pack_sides(x, j, held, lane)
            side_ref[i * 2 + t] = held
        return 0
    lax.fori_loop(0, CH // 32, block, 0)
    for k in range(3):
        low_ref[pl.ds(k * CH, CH), :] = s[pl.ds(k, CH, stride=R), :].astype(B)
        high_ref[pl.ds(k * CH, CH), :] = s[pl.ds(R - 3 + k, CH, stride=R), :].astype(B)


def start(fields, land):
    rim = jax.ShapeDtypeStruct((3 * CH, Q), B)
    return pl.pallas_call(
        start_kernel,
        out_shape=(jax.ShapeDtypeStruct((CH, R, Q), B), jax.ShapeDtypeStruct((12, R, Q), B), rim, rim),
        in_specs=[VM] * 2, out_specs=(VM,) * 4, scratch_shapes=[pltpu.VMEM((CH * R, Q), F)], name="start",
        compiler_params=pltpu.CompilerParams(vmem_limit_bytes=56 << 20),
    )(fields, land)


def corner_kernel(left_ref, right_ref, low_ref, high_ref, *refs):
    side_ref, lo_ref, hi_ref = refs[1:4] if len(refs) > 3 else refs
    lane = lanes(R) % 8
    rows = 3 * CH
    lo_ref[:rows, :] = low_ref[...]
    hi_ref[:rows, :] = high_ref[...]
    both = [jnp.where(lane < 3, left_ref[t].astype(F), right_ref[t].astype(F)) for t in range(12)]
    for t in range(12):
        side_ref[t] = both[t].astype(B)
    for t in range(0, 12, 2):
        here = pl.ds(rows + 8 * t, 16)
        lo_ref[here, :] = jnp.concatenate([both[t][:8], both[t + 1][:8]], axis=0).astype(B)
        hi_ref[here, :] = jnp.concatenate([both[t][8:], both[t + 1][8:]], axis=0).astype(B)


def corners(left, right, low, high, *later):
    msg = jax.ShapeDtypeStruct((MSG, Q), B)
    anywhere = [pl.BlockSpec(memory_space=pl.ANY)] * len(later)
    return pl.pallas_call(
        corner_kernel,
        out_shape=(jax.ShapeDtypeStruct((12, R, Q), B), msg, msg) + tuple(jax.ShapeDtypeStruct(x.shape, x.dtype) for x in later),
        in_specs=[VM] * 4 + anywhere, out_specs=(VM,) * 3 + tuple(anywhere), name="corners",
        input_output_aliases={4: 3} if later else {},
        compiler_params=pltpu.CompilerParams(vmem_limit_bytes=8 << 20),
    )(left, right, low, high, *later)


def unpack_rims(top, south_ref, north_ref, fold_ref, mirror_ref, rim, edge):
    rim[...] = jnp.zeros_like(rim)
    rows = 3 * CH
    for k in range(3):
        rim[pl.ds(k, CH, stride=8), :] = south_ref[pl.ds(k * CH, CH), :].astype(F)
    up = lax.broadcasted_iota(jnp.int32, (8, Q), 0) >= 4

    @pl.when(top == 0)
    def _():
        for k in range(3):
            rim[pl.ds(4 + k, CH, stride=8), :] = north_ref[pl.ds(k * CH, CH), :].astype(F)
        for t in range(0, 12, 2):
            n, z = north_ref[pl.ds(rows + 8 * t, 16), :].astype(F), south_ref[pl.ds(rows + 8 * t, 16), :].astype(F)
            for h in range(2):
                cut = slice(8 * h, 8 * h + 8)
                edge[t + h] = jnp.where(up, pltpu.roll(n[cut], 4, 0), pltpu.roll(z[cut], 3, 0))

    @pl.when(top != 0)
    def _():
        for k in range(3):
            plane = jnp.dot(fold_ref[pl.ds(k * CH, CH), :], mirror_ref[:, :Q], preferred_element_type=F)
            rim[pl.ds(6 - k, CH, stride=8), :] = plane
        for t in range(0, 12, 2):
            n = jnp.dot(fold_ref[pl.ds(rows + 8 * t, 16), :], mirror_ref[:, Q:], preferred_element_type=F)
            z = south_ref[pl.ds(rows + 8 * t, 16), :].astype(F)
            for h in range(2):
                x = n[8 * h:8 * h + 8]
                flip = jnp.concatenate([x[:4], x[7:8], x[6:7], x[5:6], x[4:5]], axis=0)
                edge[t + h] = jnp.where(up, flip, pltpu.roll(z[8 * h:8 * h + 8], 3, 0))


def mirrors():
    cols = np.eye(Q, dtype=np.float32)[::-1]
    ends = np.zeros((Q, Q), np.float32)
    for g in range(16):
        for k in range(6):
            ends[8 * g + k, 8 * g + 5 - k] = 1
    return jnp.asarray(np.concatenate([cols, ends], axis=1), B)


def operand(c, j, own, side, rim, edge, out):
    back = (Q - (8 * j + 3)) % Q
    beside = pltpu.roll(side, back, 1)
    lane = lanes(R)
    for b in range(7):
        out[b * R:(b + 1) * R, :] = shifted(own, beside, b - 3, lane)
    beside = pltpu.roll(edge, back, 1)
    lane = lanes(8)
    rims = [shifted(rim, beside, b - 3, lane) for b in range(7)] + [jnp.zeros((8, Q), F)]
    for b in range(0, 8, 2):
        out[112 + 8 * b:128 + 8 * b, :] = jnp.concatenate(rims[b:b + 2], axis=0).astype(B)


def front_kernel(at_ref, m_ref, side_ref, south_ref, north_ref, fold_ref, t_ref, f_ref, cot_ref, land_ref, gain_ref,
                 pi_ref, pit_ref, po_ref, pot_ref, mirror_ref,
                 up_ref, gc_ref, grev_ref, gside_ref, low_ref, high_ref, gacc, wall,
                 im, rim, edge, s, mcs, u, g, grev, sc, mcb, act, gh):
    unpack_rims(at_ref[0], south_ref, north_ref, fold_ref, mirror_ref, rim, edge)

    def conv_block(i, _):
        for j in range(BLOCKS):
            c = i * BLOCKS + j
            t = i * (BLOCKS // 16) + j // 16
            operand(c, j % 16, m_ref[c], side_ref[t], rim[pl.ds(pl.multiple_of(c * 8, 8), 8), :], edge[t], im.at[c])
        for j in range(BLOCKS):
            c = i * BLOCKS + j
            s[pl.ds(pl.multiple_of(c * R, R), R), :] = jnp.dot(t_ref[c][:, :TAPS], im[c], preferred_element_type=F)
        return 0
    lax.fori_loop(0, CH // BLOCKS, conv_block, 0)
    ocean = land_ref[...].astype(F)

    def sum_block(i, acc):
        for j in range(BLOCKS):
            acc = acc + s[pl.ds(pl.multiple_of((i * BLOCKS + j) * R, R), R), :]
        return acc
    mean = lax.fori_loop(0, CH // BLOCKS, sum_block, jnp.zeros((R, Q), F)) * (1.0 / CH)

    def sq_block(i, acc):
        for j in range(BLOCKS):
            d = s[pl.ds(pl.multiple_of((i * BLOCKS + j) * R, R), R), :] - mean
            acc = acc + d * d
        return acc
    var = lax.fori_loop(0, CH // BLOCKS, sq_block, jnp.zeros((R, Q), F)) * (1.0 / CH)
    rstd = lax.rsqrt(var + 1e-6)

    def norm_block(i, _):
        for j in range(BLOCKS):
            c = i * BLOCKS + j
            rows = pl.ds(pl.multiple_of(c * R, R), R)
            s[rows, :] = (s[rows, :] - mean) * rstd
            mcs[rows, :] = cot_ref[c].astype(F) * ocean
        return 0
    lax.fori_loop(0, CH // BLOCKS, norm_block, 0)
    u[pl.ds(CH * R, R), :] = rstd
    gain = gain_ref[...]
    gacc[...] = jnp.zeros_like(gacc)

    def rows_step(p, _):
        r0 = p * 2
        cells = pl.ds(pl.multiple_of(p * 256, 256), 256)
        nrm = jnp.concatenate([s[pl.ds(r0, CH, stride=R), :], s[pl.ds(r0 + 1, CH, stride=R), :]], axis=1)
        scaled = (nrm * gain).astype(B)
        mc = jnp.concatenate([mcs[pl.ds(r0, CH, stride=R), :], mcs[pl.ds(r0 + 1, CH, stride=R), :]], axis=1).astype(B)
        sc[:, cells] = scaled
        mcb[:, cells] = mc
        mixed = jnp.zeros((CH, 256), F)
        gn = jnp.zeros((CH, 256), F)
        hidden = jnp.dot(pi_ref[...], scaled, preferred_element_type=F)
        grad_act = jnp.dot(pot_ref[...], mc, preferred_element_type=F)
        for h in range(3):
            hs = slice(h * 256, (h + 1) * 256)
            v = hidden[hs]
            ga = grad_act[hs]
            sq = v * v
            t = jnp.tanh(v * (C1 * sq + C0))
            half = 0.5 * t + 0.5
            a = v * half
            d = half + a * (1.0 - half) * (6.0 * C1 * sq + 2.0 * C0)
            ab = a.astype(B)
            gb = (ga * d).astype(B)
            act[hs, cells] = ab
            gh[hs, cells] = gb
            mixed = mixed + jnp.dot(po_ref[:, hs], ab, preferred_element_type=F)
            gn = gn + jnp.dot(pit_ref[:, hs], gb, preferred_element_type=F)
        rs = jnp.concatenate([u[pl.ds(CH * R + r0, 1), :], u[pl.ds(CH * R + r0 + 1, 1), :]], axis=1)
        gnn = gn * nrm
        gacc[...] += gnn[:, :Q] + gnn[:, Q:]
        gs = gn * gain
        m1 = jnp.sum(gs, axis=0, keepdims=True) * (1.0 / CH)
        m2 = jnp.sum(gnn * gain, axis=0, keepdims=True) * (1.0 / CH)
        gcv = rs * (gs - m1 - nrm * m2)
        for h in range(2):
            cut = slice(h * Q, (h + 1) * Q)
            u[pl.ds(r0 + h, CH, stride=R), :] = mixed[:, cut]
            g[pl.ds(r0 + h, CH, stride=R), :] = gcv[:, cut]
            grev[pl.ds(R - 1 - r0 - h, CH, stride=R), :] = gcv[:, cut]
        return 0
    lax.fori_loop(0, R // 2, rows_step, 0)

    lane = lanes(R)

    def out_block(i, _):
        held = None
        for j in range(BLOCKS):
            c = i * BLOCKS + j
            rows = pl.ds(pl.multiple_of(c * R, R), R)
            up_ref[c] = (f_ref[c].astype(F) + ocean * u[rows, :]).astype(B)
            gb = g[rows, :].astype(B)
            gc_ref[c] = gb
            grev_ref[c] = grev[rows, :].astype(B)
            held = pack_sides(gb, j % 16, None if j % 16 == 0 else held, lane)
            if j % 16 == 15:
                gside_ref[i * (BLOCKS // 16) + j // 16] = held
        return 0
    lax.fori_loop(0, CH // BLOCKS, out_block, 0)
    for k in range(3):
        low_ref[pl.ds(k * CH, CH), :] = g[pl.ds(k, CH, stride=R), :].astype(B)
        high_ref[pl.ds(k * CH, CH), :] = g[pl.ds(R - 3 + k, CH, stride=R), :].astype(B)
    wall[pl.ds(12 * CH, 256), :] = jnp.zeros((256, Q), B)
    for h in range(6):
        hs = slice(h * Q, (h + 1) * Q)
        wall[pl.ds(h * CH, CH), :] = lax.dot_general(mcb[...], act[hs, :], NT, preferred_element_type=F).astype(B)
        wall[pl.ds((6 + h) * CH, CH), :] = lax.dot_general(sc[...], gh[hs, :], NT, preferred_element_type=F).astype(B)


def front(at, masked, side, south, north, fold, t, fields, cot, land, gain, pi, pit, po, pot):
    block, rim = jax.ShapeDtypeStruct((CH, R, Q), B), jax.ShapeDtypeStruct((3 * CH, Q), B)
    plane = pltpu.VMEM((CH * R, Q), F)
    return pl.pallas_call(
        front_kernel,
        out_shape=(block, block, block, jax.ShapeDtypeStruct((12, R, Q), B), rim, rim, jax.ShapeDtypeStruct((CH, Q), F),
                   jax.ShapeDtypeStruct((2560, Q), B)),
        in_specs=[SM] + [VM] * 15, out_specs=(VM,) * 8,
        scratch_shapes=[
            pltpu.VMEM((CH, TAPS, Q), B), pltpu.VMEM((CH * 8, Q), F), pltpu.VMEM((12, 8, Q), F),
            plane, plane, pltpu.VMEM((CH * R + R, Q), F), plane, plane,
            pltpu.VMEM((CH, R * Q), B), pltpu.VMEM((CH, R * Q), B), pltpu.VMEM((HID, R * Q), B), pltpu.VMEM((HID, R * Q), B),
        ],
        compiler_params=pltpu.CompilerParams(vmem_limit_bytes=40 << 20),
        cost_estimate=pl.CostEstimate(flops=6 << 30, bytes_accessed=12 << 20, transcendentals=3 << 20),
        name="front",
    )(at, masked, side, south, north, fold, t, fields, cot, land, gain, pi, pit, po, pot, mirrors())


def tap_kernel(at_ref, m_ref, side_ref, south_ref, north_ref, fold_ref, grev_ref, gacc_ref, mirror_ref, valid_ref, collect_ref, w_ref,
               o_ref, im, rim, edge, dks):
    unpack_rims(at_ref[0], south_ref, north_ref, fold_ref, mirror_ref, rim, edge)

    def block(i, _):
        sums = [[], []]
        for j in range(BLOCKS):
            c = i * BLOCKS + j
            t = i * (BLOCKS // 16) + j // 16
            operand(c, j % 16, m_ref[c], side_ref[t], rim[pl.ds(pl.multiple_of(c * 8, 8), 8), :], edge[t], im.at[j])
        for j in range(BLOCKS):
            dt = lax.dot_general(grev_ref[i * BLOCKS + j], im[j], NT, preferred_element_type=F)
            dt = [dt[:, :Q], jnp.concatenate([dt[:, Q:], jnp.zeros((R, 256 - TAPS), F)], axis=1)]
            for h in range(2):
                x = pltpu.roll(dt[h] * valid_ref[:, h * Q:(h + 1) * Q], 0, 1, stride=1, stride_axis=0)
                sums[h].append(jnp.sum(x, axis=0, keepdims=True))
        for h in range(2):
            dks[pl.ds(pl.multiple_of(i * BLOCKS, BLOCKS), BLOCKS), h * Q:(h + 1) * Q] = jnp.concatenate(sums[h], axis=0)
        return 0
    lax.fori_loop(0, CH // BLOCKS, block, 0)
    taps = jnp.dot(dks[...], collect_ref[...], preferred_element_type=F, precision=lax.Precision.HIGHEST)
    gg = jnp.sum(gacc_ref[...], axis=1, keepdims=True)
    o_ref[:CH, :] = jnp.where(lanes(CH) == Q - 1, gg, taps).astype(B)
    o_ref[CH:, :] = jnp.zeros((256 - CH, Q), B)


def taps(at, masked, rims, grev, gacc, w):
    return pl.pallas_call(
        tap_kernel,
        grid=(1,),
        out_shape=jax.ShapeDtypeStruct(w.shape, B),
        in_specs=[SM] + [VM] * 10 + [pl.BlockSpec(memory_space=pl.ANY)],
        out_specs=pl.BlockSpec((256, Q), lambda i: (9, 0)),
        scratch_shapes=[pltpu.VMEM((BLOCKS, TAPS, Q), B), pltpu.VMEM((CH * 8, Q), F), pltpu.VMEM((12, 8, Q), F), pltpu.VMEM((CH, 256), F)],
        compiler_params=pltpu.CompilerParams(vmem_limit_bytes=40 << 20),
        cost_estimate=pl.CostEstimate(flops=2 << 30, bytes_accessed=8 << 20, transcendentals=0),
        input_output_aliases={11: 0},
        name="taps",
    )(at, masked, *rims, grev, gacc, mirrors(), jnp.asarray(VALID[::-1].copy()), jnp.asarray(COLLECT), w)


def back_kernel(first, at_ref, m_ref, side_ref, south_ref, north_ref, fold_ref, t_ref, cot_ref, land_ref, mirror_ref, after_ref, *refs):
    o_ref, im, rim, edge = refs[-4:]
    i = pl.program_id(0)

    @pl.when(i == 0)
    def _():
        unpack_rims(at_ref[0], south_ref, north_ref, fold_ref, mirror_ref, rim, edge)
    ocean = land_ref[...].astype(F)
    for j in range(BLOCKS):
        c = (first + i) * BLOCKS + j
        t = (first + i) * (BLOCKS // 16) + j // 16
        operand(c, j % 16, m_ref[j], side_ref[t], rim[pl.ds(pl.multiple_of(c * 8, 8), 8), :], edge[t], im.at[j])
    for j in range(BLOCKS):
        gm = jnp.dot(t_ref[j][:, :TAPS], im[j], preferred_element_type=F)
        o_ref[j] = (cot_ref[j].astype(F) + ocean * gm).astype(B)


def back(at, grad, rims, t, cot, land, after, first, count, begun=None):
    some = lambda *shape: pl.BlockSpec((BLOCKS,) + shape, lambda i: (first + i, 0, 0))
    anywhere = pl.BlockSpec(memory_space=pl.ANY)
    extra = [] if begun is None else [begun]
    return pl.pallas_call(
        lambda *refs: back_kernel(first, *refs),
        grid=(count,),
        out_shape=jax.ShapeDtypeStruct((CH, R, Q), B),
        in_specs=[SM, some(R, Q), VM, VM, VM, VM, some(R, 256), some(R, Q), VM, VM, anywhere] + [anywhere] * len(extra),
        out_specs=some(R, Q),
        scratch_shapes=[pltpu.VMEM((BLOCKS, TAPS, Q), B), pltpu.VMEM((CH * 8, Q), F), pltpu.VMEM((12, 8, Q), F)],
        compiler_params=pltpu.CompilerParams(vmem_limit_bytes=56 << 20),
        cost_estimate=pl.CostEstimate(flops=1 << 30, bytes_accessed=8 << 20, transcendentals=0),
        input_output_aliases={11: 0} if extra else {},
        name="back",
    )(at, grad, *rims, t, cot, land, mirrors(), after, *extra)


def spread_kernel(x_ref, *refs):
    o_ref = refs[-1]
    total = x_ref[0].astype(F)
    for k in range(1, x_ref.shape[0]):
        total = total + x_ref[k].astype(F)
    total = total.astype(B)
    for k in range(o_ref.shape[0]):
        o_ref[k] = total


def spread(x, copies, *after):
    return pl.pallas_call(
        spread_kernel, out_shape=jax.ShapeDtypeStruct((copies,) + x.shape[1:], B),
        in_specs=[VM] + [pl.BlockSpec(memory_space=pl.ANY)] * len(after), out_specs=VM, name="spread",
        compiler_params=pltpu.CompilerParams(vmem_limit_bytes=8 << 20),
    )(x, *after)


def along(i, bits):
    code = (i ^ (i >> 1)) ^ bits
    return code ^ (code >> 1)


def finish_kernel(at_ref, a_ref, b_ref, after_ref, out_ref, in_ref, kern_ref, gain_ref, wall):
    x, y, c = at_ref[1], at_ref[2], at_ref[3]
    for k in range(32):
        src = (a_ref, b_ref)[k // 16]
        chunk = along(x, k % 4) * 8 + along(y, k // 4 % 4) * 2 + (c ^ (k // 16))
        wall[pl.ds(pl.multiple_of(chunk * 80, 80), 80), :] = src[pl.ds(k % 16 * 80, 80), :]
    scale = (128 * 4096) ** -0.5
    for h in range(6):
        hs = slice(h * Q, (h + 1) * Q)
        out_ref[:, hs] = wall[pl.ds(h * CH, CH), :].astype(F) * scale
        in_ref[:, hs] = wall[pl.ds((6 + h) * CH, CH), :].astype(F) * scale
    tail = jnp.transpose(wall[pl.ds(12 * CH, CH), :].astype(F) * scale)
    for a in range(7):
        kern_ref[a] = tail[8 * a:8 * a + 7, :]
    gain_ref[...] = tail[Q - 1:, :]


def finish(at, first, second, after):
    shapes = ((CH, HID), (CH, HID), (7, 7, CH), (1, CH))
    return pl.pallas_call(
        finish_kernel,
        out_shape=tuple(jax.ShapeDtypeStruct(x, F) for x in shapes),
        in_specs=[SM, VM, VM, pl.BlockSpec(memory_space=pl.ANY)], out_specs=(VM,) * 4, name="finish",
        scratch_shapes=[pltpu.VMEM((2560, Q), B)],
        compiler_params=pltpu.CompilerParams(vmem_limit_bytes=16 << 20),
    )(at, first, second, after)


ALL = ("x", "yh", "z", "yl", "c")
LAT, LON = 8, 32
PLANE = ("x", "yh", "yl", "c")


def lon_route(step):
    return [(y * LON + i, y * LON + (i + step) % LON) for y in range(LAT) for i in range(LON)]


def rims(side, low, high, *later):
    left = lax.ppermute(side, ALL, lon_route(1))
    right = lax.ppermute(side, ALL, lon_route(-1))
    side, low, high, *later = corners(left, right, low, high, *later)
    top = LON * (LAT - 1)
    fold = lax.ppermute(high, ALL, [(top + i, top + LON - 1 - i) for i in range(LON)])
    south = lax.ppermute(high, ALL, [(y * LON + i, (y + 1) * LON + i) for y in range(LAT - 1) for i in range(LON)])
    north = lax.ppermute(low, ALL, [(y * LON + i, (y - 1) * LON + i) for y in range(1, LAT) for i in range(LON)])
    return (side, south, north, fold), *later


def swap_route(bx=0, by=0, bc=0):
    def flat(x, y, z, c):
        return ((x * 2 + y // 2) * 8 + z) * 4 + (y % 2) * 2 + c
    return [
        (flat(x, y, z, c), flat(along(x, bx), along(y, by), z, c ^ bc))
        for x in range(4) for y in range(4) for z in range(8) for c in range(2)
    ]


def on_device(fields, cotangent, land_sea, kernel, ln_gain, proj_in, proj_out):
    x, y, c = lax.axis_index("x"), lax.axis_index("yh") * 2 + lax.axis_index("yl"), lax.axis_index("c")
    is_top = x * 2 + lax.axis_index("yh") == LAT - 1
    at = jnp.stack([is_top.astype(jnp.int32), x, y, c]).astype(jnp.int32)
    masked, side, low, high = start(fields, land_sea)
    one, two, pi, pot, gain = prepare(at, kernel, proj_in.T, proj_out, ln_gain)
    ends, one = rims(side, low, high, one)
    updated, grad, reverse, side, low, high, gacc, w = front(
        at, masked, *ends, one, fields, cotangent, land_sea, gain, pi, proj_in.T, proj_out, pot)
    w = taps(at, masked, ends, reverse, gacc, w)
    ends, w = rims(side, low, high, w)
    w = spread(lax.all_to_all(w.reshape(32, 80, Q), PLANE, 0, 0), 8, *ends)
    grad_fields = back(at, grad, ends, two, cotangent, land_sea, w, 0, 6)
    w = spread(lax.all_to_all(w, "z", 0, 0), 1, grad_fields)[0]
    w = jnp.concatenate([w] + [lax.ppermute(w, ALL, swap_route(bx=k)) for k in (1, 2, 3)])
    w = jnp.concatenate([w] + [lax.ppermute(w, ALL, swap_route(by=k)) for k in (1, 2, 3)])
    grad_out, grad_in, grad_kernel, grad_gain = finish(at, w, lax.ppermute(w, ALL, swap_route(bc=1)), grad_fields)
    return updated, grad_fields, grad_kernel.transpose(2, 0, 1), grad_gain.reshape(CH), grad_in.T, grad_out


def solution(mesh):
    fine = jax.sharding.Mesh(mesh.devices.reshape(4, 2, 8, 2, 2), ALL)
    P = jax.sharding.PartitionSpec
    lat, lon = ("x", "yh"), ("z", "yl", "c")
    block = P(None, lat, lon)
    return jax.shard_map(
        on_device,
        mesh=fine,
        in_specs=(block, block, P(lat, lon), P(), P(), P(), P()),
        out_specs=(block, block, P(), P(), P(), P()),
        check_vma=False,
    )
```

time: 190 us -> 137 us (0.72)
  other arithmetic: 21.8 us -> 0.59 us
  local copies, waits for them, and re-layouts: 24 us -> 5.24 us
  matrix products: 9.31 us -> 0 us
  waiting for transfers between devices: 29.5 us -> 24 us
  Pallas kernels: 49.7 us -> 52 us
    all_to_all x3 -> x2, starting transfers between devices: 29 us -> 14.6 us  [the longest x1 9.86 us: on_device(): w = spread(lax.all_to_all(w.reshape(32, 80, Q), PLANE, 0, 0), 8, *ends)]
    ppermute x12 -> x17, starting transfers between devices: 24.5 us -> 37.3 us  [the longest x2 9.26 us: rims(): lax.ppermute(low, ALL, [(y * LON + i, (y - 1) * LON + i) for y in range(1...]
    dot_general x5 -> x0, matrix products: 9.31 us -> none  [the longest x1 3.98 us: toeplitz(): jnp.einsum('cab,ars->crbs', north, jnp.asarray(up, B), preferred_element_...]
    concatenate x2 -> x1, other arithmetic: 7.86 us -> 0.01 us  [on_device(): jnp.concatenate([w] + [lax.ppermute(w, ALL, swap_route(bx=k)) for k in (1...]
    reshape x4 -> x0, local copies, waits for them, and re-layouts: 7.79 us -> none  [the longest x2 5.91 us: toeplitz(): return t.astype(B).reshape(CH, R, 224)]
    all_to_all x3 -> x2, waiting for transfers between devices: 4.72 us -> 0.01 us  [the longest x1 0.01 us: on_device(): w = spread(lax.all_to_all(w.reshape(32, 80, Q), PLANE, 0, 0), 8, *ends)]
    slice x3 -> x0, other arithmetic: 4.64 us -> none  [the longest x2 3.89 us: widen(): low, high = (wide[:, :3], wide[:, R - 3:])]
    rev x3 -> x0, local copies, waits for them, and re-layouts: 3.84 us -> none  [the longest x2 3.72 us: widen(): fold[:, ::-1]]
  transfers between devices with their start and end apart: 15 -> 19, of which waited for: 4 -> 7; matrix products, arithmetic and copies ran while one was open for 20% -> 0% of each run, Pallas kernels for 5% -> 19%
where the time goes in v2:
time: 137 us; the launch traced here: 135 us
  Pallas kernels  52 us (38%)
  starting transfers between devices  51.9 us (38%)
  waiting for transfers between devices  24 us (18%)
  local copies, waits for them, and re-layouts  5.24 us (4%)
    pallas_call x1, Pallas kernels, front(): pl.pallas_call(front_kernel, out_shape=(block, block, block, jax.ShapeDty...  20.9 us
    pallas_call x1, Pallas kernels, taps(): pl.pallas_call(tap_kernel, grid=(1,), out_shape=jax.ShapeDtypeStruct(w.sh...  11.1 us
    ppermute x2, waiting for transfers between devices, rims(): lax.ppermute(low, ALL, [(y * LON + i, (y - 1) * LON + i) for y in range(1...  10.6 us
    all_to_all x1, starting transfers between devices, on_device(): w = spread(lax.all_to_all(w.reshape(32, 80, Q), PLANE, 0, 0), 8, *ends)  9.86 us
    ppermute x2, starting transfers between devices, rims(): lax.ppermute(low, ALL, [(y * LON + i, (y - 1) * LON + i) for y in range(1...  9.26 us
    pallas_call x1, Pallas kernels, back(): pl.pallas_call(lambda *refs: back_kernel(first, *refs), grid=(count,), ou...  8.49 us
    ppermute x2, starting transfers between devices, rims(): right = lax.ppermute(side, ALL, lon_route(-1))  6.96 us
    ppermute x3, starting transfers between devices, on_device(): lax.ppermute(w, ALL, swap_route(bx=k))  6.76 us
  transfers between devices with their start and end apart: 19, of which 7 were waited for; matrix products, arithmetic and copies ran while one was open for 0% of the time, Pallas kernels for 19%

profile of v2, /device:TPU:3, one launch (start us, length us, event | category | flops | bytes accessed | tf_op | source)
XLA Modules:
  0.0 134.7 jit_solution(15610433856841841055)
XLA Ops:
  0.6 2.7 %start.1 = (bf16[192,16,128]{2,1,0:T(8,128)(2,1)}, bf16[12,16,128]{2,1,0:T(8,128)(2,1)}, bf16[576,128]{1,0:T(8,128)(2,1)}, bf16[576,128]{1,0:T(8,128)(2,1)}) custom-call(bf16[192,16,128]{2,1,0:T(8,128)(2,1)} %f_ref.3, s32[16,128]{1,0:T(8,128)} %refs_8_.1), custom_call_target="tpu_custom_call" | custom-call | tf_op jit(solution)/shard_map/start/pallas_call | solution.py:144
  3.3 0.7 collective-permute-start.1
  4.0 1.2 collective-permute-start
  5.2 0.6 pad_add_fusion.at_ref.refs_0_
  5.8 6.2 %prepare.1 = (bf16[192,16,256]{2,1,0:T(8,128)(2,1)}, bf16[192,16,256]{2,1,0:T(8,128)(2,1)}, bf16[768,192]{1,0:T(8,128)(2,1)}, bf16[768,192]{1,0:T(8,128)(2,1)}, f32[192,1]{1,0:T(8,128)}) custom-call(s32[4]{0:T(128)} %pad_add_fusion.at_ref.refs_0_, bf16[7,7,192]{2,1,0:T(8,128)(2,1)} %bitcast.21, bf16[7,7,768]{2,1,0:T(8,128)(2,1)} %constant.30.clone.tab_ref, ...), custom_call_target="tpu_custom_call" | custom-call | flops 1073741824 | bytes 8388608 | tf_op jit(solution)/shard_map/prepare/pallas_call | solution.py:111
  12.0 1.4 %copy-done.2 = bf16[192,16,256]{2,1,0:T(8,128)(2,1)S(1)} copy-done((bf16[192,16,256]{2,1,0:T(8,128)(2,1)S(1)}, bf16[192,16,256]{2,1,0:T(8,128)(2,1)}, u32[]{:S(2)}) %copy-start.2) | copy-done | bytes 1572888
  13.5 1.1 copy-done.3
  14.6 4.7 %collective-permute-start.3 = (bf16[672,128]{1,0:T(8,128)(2,1)S(1)}, bf16[672,128]{1,0:T(8,128)(2,1)S(1)}, u32[]{:S(2)}, u32[]{:S(2)}) collective-permute-start(bf16[672,128]{1,0:T(8,128)(2,1)S(1)} %get-tuple-element.42), channel_id=1, source_target_pairs={{32,0},{33,1},{34,2},{35,3},{36,4},{37,5},{38,6},{39,7},{40,8},{41... | collective-permute-start | bytes 516104 | tf_op jit(solution)/shard_map/ppermute | solution.py:506
  19.3 0.7 collective-permute-start.4
  20.0 2.1 %collective-permute-start.2 = (bf16[672,128]{1,0:T(8,128)(2,1)S(1)}, bf16[672,128]{1,0:T(8,128)(2,1)S(1)}, u32[]{:S(2)}, u32[]{:S(2)}) collective-permute-start(bf16[672,128]{1,0:T(8,128)(2,1)S(1)} %get-tuple-element.41), channel_id=1, source_target_pairs={{0,32},{1,33},{2,34},{3,35},{4,36},{5,37},{6,38},{7,39},{8,40},{9,... | collective-permute-start | bytes 516104 | tf_op jit(solution)/shard_map/ppermute | solution.py:505
  22.3 6.4 %collective-permute-done.2.south_ref = bf16[672,128]{1,0:T(8,128)(2,1)S(1)} collective-permute-done((bf16[672,128]{1,0:T(8,128)(2,1)S(1)}, bf16[672,128]{1,0:T(8,128)(2,1)S(1)}, u32[]{:S(2)}, u32[]{:S(2)}) %collective-permute-start.2) | collective-permute-done | bytes 172064 | tf_op jit(solution)/shard_map/ppermute | solution.py:505
  28.7 1.4 %copy-done.4 = bf16[192,16,256]{2,1,0:T(8,128)(2,1)S(1)} copy-done((bf16[192,16,256]{2,1,0:T(8,128)(2,1)S(1)}, bf16[192,16,256]{2,1,0:T(8,128)(2,1)}, u32[]{:S(2)}) %copy-start.4) | copy-done | bytes 1572888
  30.1 20.9 %front.1 = (bf16[192,16,128]{2,1,0:T(8,128)(2,1)}, bf16[192,16,128]{2,1,0:T(8,128)(2,1)S(1)}, bf16[192,16,128]{2,1,0:T(8,128)(2,1)S(1)}, bf16[12,16,128]{2,1,0:T...) custom-call(s32[4]{0:T(128)S(1)} %copy-done.16, ...), custom_call_target="tpu_custom_call" | custom-call | flops 6442450944 | bytes 12582912 | tf_op jit(solution)/shard_map/front/pallas_call | solution.py:347
  51.1 6.3 %collective-permute-start.6 = (bf16[12,16,128]{2,1,0:T(8,128)(2,1)S(1)}, bf16[12,16,128]{2,1,0:T(8,128)(2,1)S(1)}, u32[]{:S(2)}, u32[]{:S(2)}) collective-permute-start(bf16[12,16,128]{2,1,0:T(8,128)(2,1)S(1)} %get-tuple-element.49), channel_id=1, source_target_pairs={{0,31},{1,0},{2,1},{3,2},{4,3},{5,4},{6,5},{7,6},{8,7},{9,8},{10,9... | collective-permute-start | bytes 147464 | tf_op jit(solution)/shard_map/ppermute | solution.py:501
  57.4 11.1 %taps.1.refs_0_ = bf16[2560,128]{1,0:T(8,128)(2,1)} custom-call(s32[4]{0:T(128)S(1)} %copy-done.16, bf16[192,16,128]{2,1,0:T(8,128)(2,1)S(1)} %copy-done.18, bf16[12,16,128]{2,1,0:T(8,128)(2,1)S(1)} %get-tuple-element.40.side_ref, bf16[672,128]{1,0:T(8,128)(2,1)S(1)} %collective-permute-done.2.south_ref, ...), custom_call_target="tpu_custom_call", output_to_operand_aliasing={{}: (11, {})} | custom-call | flops 2147483648 | bytes 8388608 | tf_op jit(solution)/shard_map/taps/pallas_call | solution.py:390
  68.5 9.9 %all-to-all-start = ((bf16[32,80,128]{2,1,0:T(8,128)(2,1)}), bf16[32,80,128]{2,1,0:T(8,128)(2,1)S(1)}, u32[]{:S(2)}, u32[]{:S(2)}) async-start(bf16[32,80,128]{2,1,0:T(8,128)(2,1)} %bitcast.7), calls=%async_computation | async-start | bytes 1310720 | tf_op jit(solution)/shard_map/all_to_all | solution.py:530
  78.4 4.6 %collective-permute-start.8 = (bf16[672,128]{1,0:T(8,128)(2,1)S(1)}, bf16[672,128]{1,0:T(8,128)(2,1)S(1)}, u32[]{:S(2)}, u32[]{:S(2)}) collective-permute-start(bf16[672,128]{1,0:T(8,128)(2,1)S(1)} %get-tuple-element.57), channel_id=1, source_target_pairs={{32,0},{33,1},{34,2},{35,3},{36,4},{37,5},{38,6},{39,7},{40,8},{41... | collective-permute-start | bytes 516104 | tf_op jit(solution)/shard_map/ppermute | solution.py:506
  83.0 0.7 collective-permute-start.9
  83.7 2.2 %collective-permute-start.7 = (bf16[672,128]{1,0:T(8,128)(2,1)S(1)}, bf16[672,128]{1,0:T(8,128)(2,1)S(1)}, u32[]{:S(2)}, u32[]{:S(2)}) collective-permute-start(bf16[672,128]{1,0:T(8,128)(2,1)S(1)} %get-tuple-element.56), channel_id=1, source_target_pairs={{0,32},{1,33},{2,34},{3,35},{4,36},{5,37},{6,38},{7,39},{8,40},{9,... | collective-permute-start | bytes 516104 | tf_op jit(solution)/shard_map/ppermute | solution.py:505
  85.9 10.5 %collective-permute-done.8.refs_2_.refs_4_ = bf16[672,128]{1,0:T(8,128)(2,1)S(1)} collective-permute-done((bf16[672,128]{1,0:T(8,128)(2,1)S(1)}, bf16[672,128]{1,0:T(8,128)(2,1)S(1)}, u32[]{:S(2)}, u32[]{:S(2)}) %collective-permute-start.8) | collective-permute-done | bytes 172064 | tf_op jit(solution)/shard_map/ppermute | solution.py:506
  96.4 0.8 spread.2.refs_10_
  97.2 4.7 %all-to-all-start.1 = ((bf16[8,80,128]{2,1,0:T(8,128)(2,1)}), bf16[8,80,128]{2,1,0:T(8,128)(2,1)S(1)}, u32[]{:S(2)}, u32[]{:S(2)}) async-start(bf16[8,80,128]{2,1,0:T(8,128)(2,1)} %spread.2.refs_10_), calls=%async_computation.1 | async-start | bytes 327680 | tf_op jit(solution)/shard_map/all_to_all | solution.py:532
  102.0 8.5 %back.1.refs_0_.after_ref = bf16[192,16,128]{2,1,0:T(8,128)(2,1)} custom-call(s32[4]{0:T(128)} %pad_add_fusion.at_ref.refs_0_, bf16[192,16,128]{2,1,0:T(8,128)(2,1)} %copy-done.6, bf16[12,16,128]{2,1,0:T(8,128)(2,1)} %copy-done.11, bf16[672,128]{1,0:T(8,128)(2,1)} %copy-done.10, bf16[672,128]{1,0:T(8,128)(2,1)} %copy-done.8, bf16[672,128]{1,0:T(8,128)(2,1)} %copy-done.9, ...), custom_call_target="tpu_custom_call" | custom-call | flops 1073741824 | bytes 8388608 | tf_op jit(solution)/shard_map/back/pallas_call | solution.py:425
  110.5 1.1 copy-done
  111.6 5.8 %collective-permute-start.12 = (bf16[80,128]{1,0:T(8,128)(2,1)S(1)}, bf16[80,128]{1,0:T(8,128)(2,1)S(1)}, u32[]{:S(2)}, u32[]{:S(2)}) collective-permute-start(bf16[80,128]{1,0:T(8,128)(2,1)S(1)} %bitcast.13), channel_id=1, source_target_pairs={{0,128},{1,129},{4,132},{5,133},{8,136},{9,137},{12,140},{13,141},... | collective-permute-start | bytes 61448 | tf_op jit(solution)/shard_map/ppermute | solution.py:533
  117.4 1.0 collective-permute-start.10
  118.6 1.5 %collective-permute-done.11 = bf16[80,128]{1,0:T(8,128)(2,1)S(1)} collective-permute-done((bf16[80,128]{1,0:T(8,128)(2,1)S(1)}, bf16[80,128]{1,0:T(8,128)(2,1)S(1)}, u32[]{:S(2)}, u32[]{:S(2)}) %collective-permute-start.11) | collective-permute-done | bytes 20512 | tf_op jit(solution)/shard_map/ppermute | solution.py:533
  120.1 2.8 %collective-permute-start.14 = (bf16[320,128]{1,0:T(8,128)(2,1)S(1)}, bf16[320,128]{1,0:T(8,128)(2,1)S(1)}, u32[]{:S(2)}, u32[]{:S(2)}) collective-permute-start(bf16[320,128]{1,0:T(8,128)(2,1)S(1)} %pad_maximum_fusion), channel_id=1, source_target_pairs={{0,34},{1,35},{4,38},{5,39},{8,42},{9,43},{12,46},{13,47},{16,50},... | collective-permute-start | bytes 245768 | tf_op jit(solution)/shard_map/ppermute | solution.py:534
  122.9 4.1 %collective-permute-done.13 = bf16[320,128]{1,0:T(8,128)(2,1)S(1)} collective-permute-done((bf16[320,128]{1,0:T(8,128)(2,1)S(1)}, bf16[320,128]{1,0:T(8,128)(2,1)S(1)}, u32[]{:S(2)}, u32[]{:S(2)}) %collective-permute-start.13) | collective-permute-done | bytes 81952 | tf_op jit(solution)/shard_map/ppermute | solution.py:534
  127.1 4.6 %collective-permute-start.16 = (bf16[1280,128]{1,0:T(8,128)(2,1)S(1)}, bf16[1280,128]{1,0:T(8,128)(2,1)S(1)}, u32[]{:S(2)}, u32[]{:S(2)}) collective-permute-start(bf16[1280,128]{1,0:T(8,128)(2,1)S(1)} %constant_dynamic-update-slice_fusion.a_ref), channel_id=1, source_target_pairs={{0,1},{1,0},{4,5},{5,4},{8,9},{9,8},{12,13},{13,12},{16,17},{17,16... | collective-permute-start | bytes 983048 | tf_op jit(solution)/shard_map/ppermute | solution.py:535
  131.7 1.3 collective-permute-done.16.b_ref
  133.0 1.7 %finish.1 = (f32[192,768]{1,0:T(8,128)}, f32[192,768]{1,0:T(8,128)}, f32[7,7,192]{2,1,0:T(8,128)}, f32[1,192]{1,0:T(1,128)}) custom-call(s32[4]{0:T(128)S(1)} %copy-done.17, bf16[1280,128]{1,0:T(8,128)(2,1)S(1)} %constant_dynamic-update-slice_fusion.a_ref, bf16[1280,128]{1,0:T(8,128)(2,1)S(1)} %collective-permute-done.16.b_ref, ...), custom_call_target="tpu_custom_call" | custom-call | tf_op jit(solution)/shard_map/finish/pallas_call | solution.py:481
  (77 shorter events, 0.8 us)
Async XLA Ops:
  3.3 8.7 %collective-permute-start.1 = (bf16[12,16,128]{2,1,0:T(8,128)(2,1)}, bf16[12,16,128]{2,1,0:T(8,128)(2,1)S(1)}, u32[]{:S(2)}, u32[]{:S(2)}) collective-permute-start(bf16[12,16,128]{2,1,0:T(8,128)(2,1)} %get-tuple-element.36), channel_id=1, source_target_pairs={{0,31},{1,0},{2,1},{3,2},{4,3},{5,4},{6,5},{7,6},{8,7},{9,8},{10,9... | collective-permute-start | bytes 147464 | tf_op jit(solution)/shard_map/ppermute | solution.py:501
  4.0 8.0 %collective-permute-start = (bf16[12,16,128]{2,1,0:T(8,128)(2,1)}, bf16[12,16,128]{2,1,0:T(8,128)(2,1)S(1)}, u32[]{:S(2)}, u32[]{:S(2)}) collective-permute-start(bf16[12,16,128]{2,1,0:T(8,128)(2,1)} %get-tuple-element.36), channel_id=1, source_target_pairs={{0,1},{1,2},{2,3},{3,4},{4,5},{5,6},{6,7},{7,8},{8,9},{9,10},{10,1... | collective-permute-start | bytes 147464 | tf_op jit(solution)/shard_map/ppermute | solution.py:500
  5.8 22.9 %copy-start.5 = (bf16[192,16,128]{2,1,0:T(8,128)(2,1)S(1)}, bf16[192,16,128]{2,1,0:T(8,128)(2,1)}, u32[]{:S(2)}) copy-start(bf16[192,16,128]{2,1,0:T(8,128)(2,1)} %refs_7_.1) | copy-start | bytes 2359300
  5.8 22.9 %copy-start.7 = (bf16[192,16,128]{2,1,0:T(8,128)(2,1)S(1)}, bf16[192,16,128]{2,1,0:T(8,128)(2,1)}, u32[]{:S(2)}) copy-start(bf16[192,16,128]{2,1,0:T(8,128)(2,1)} %f_ref.3) | copy-start | bytes 2359300
  5.8 22.9 %copy-start.14 = (bf16[128,256]{1,0:T(8,128)(2,1)S(1)}, bf16[128,256]{1,0:T(8,128)(2,1)}, u32[]{:S(2)}) copy-start(bf16[128,256]{1,0:T(8,128)(2,1)} %constant.32.clone.mirror_ref.refs_9_) | copy-start | bytes 196612
  5.8 22.9 %copy-start.15 = (s32[16,128]{1,0:T(8,128)S(1)}, s32[16,128]{1,0:T(8,128)}, u32[]{:S(2)}) copy-start(s32[16,128]{1,0:T(8,128)} %refs_8_.1) | copy-start | bytes 24580
  5.8 22.9 %copy-start.18 = (bf16[192,16,128]{2,1,0:T(8,128)(2,1)S(1)}, bf16[192,16,128]{2,1,0:T(8,128)(2,1)}, u32[]{:S(2)}) copy-start(bf16[192,16,128]{2,1,0:T(8,128)(2,1)} %get-tuple-element.35.m_ref) | copy-start | bytes 2359300
  5.8 22.9 %copy-start.19 = (bf16[768,192]{0,1:T(8,128)(2,1)S(1)}, bf16[768,192]{0,1:T(8,128)(2,1)}, u32[]{:S(2)}) copy-start(bf16[768,192]{0,1:T(8,128)(2,1)} %param.19) | copy-start | bytes 884740
  5.8 22.9 %copy-start.20 = (bf16[192,768]{1,0:T(8,128)(2,1)S(1)}, bf16[192,768]{1,0:T(8,128)(2,1)}, u32[]{:S(2)}) copy-start(bf16[192,768]{1,0:T(8,128)(2,1)} %po_ref.3) | copy-start | bytes 884740
  14.6 7.6 %collective-permute-start.3 = (bf16[672,128]{1,0:T(8,128)(2,1)S(1)}, bf16[672,128]{1,0:T(8,128)(2,1)S(1)}, u32[]{:S(2)}, u32[]{:S(2)}) collective-permute-start(bf16[672,128]{1,0:T(8,128)(2,1)S(1)} %get-tuple-element.42), channel_id=1, source_target_pairs={{32,0},{33,1},{34,2},{35,3},{36,4},{37,5},{38,6},{39,7},{40,8},{41... | collective-permute-start | bytes 516104 | tf_op jit(solution)/shard_map/ppermute | solution.py:506
  19.3 3.0 %collective-permute-start.4 = (bf16[672,128]{1,0:T(8,128)(2,1)S(1)}, bf16[672,128]{1,0:T(8,128)(2,1)S(1)}, u32[]{:S(2)}, u32[]{:S(2)}) collective-permute-start(bf16[672,128]{1,0:T(8,128)(2,1)S(1)} %get-tuple-element.41), channel_id=1, source_target_pairs={{224,255},{225,254},{226,253},{227,252},{228,251},{229,250},{230,2... | collective-permute-start | bytes 516104 | tf_op jit(solution)/shard_map/ppermute | solution.py:504
  20.0 8.7 %collective-permute-start.2 = (bf16[672,128]{1,0:T(8,128)(2,1)S(1)}, bf16[672,128]{1,0:T(8,128)(2,1)S(1)}, u32[]{:S(2)}, u32[]{:S(2)}) collective-permute-start(bf16[672,128]{1,0:T(8,128)(2,1)S(1)} %get-tuple-element.41), channel_id=1, source_target_pairs={{0,32},{1,33},{2,34},{3,35},{4,36},{5,37},{6,38},{7,39},{8,40},{9,... | collective-permute-start | bytes 516104 | tf_op jit(solution)/shard_map/ppermute | solution.py:505
  30.1 27.2 %copy-start.21 = (f32[256,128]{1,0:T(8,128)S(1)}, f32[256,128]{1,0:T(8,128)}, u32[]{:S(2)}) copy-start(f32[256,128]{1,0:T(8,128)} %constant.34.clone.collect_ref) | copy-start | bytes 393220
  30.1 27.2 %copy-start.22 = (f32[16,256]{1,0:T(8,128)S(1)}, f32[16,256]{1,0:T(8,128)}, u32[]{:S(2)}) copy-start(f32[16,256]{1,0:T(8,128)} %constant.33.clone.valid_ref) | copy-start | bytes 49156
  51.1 17.4 %copy-start.6 = (bf16[192,16,128]{2,1,0:T(8,128)(2,1)}, bf16[192,16,128]{2,1,0:T(8,128)(2,1)S(1)}, u32[]{:S(2)}) copy-start(bf16[192,16,128]{2,1,0:T(8,128)(2,1)S(1)} %get-tuple-element.48.refs_1_) | copy-start | bytes 2359300
  51.1 17.4 %collective-permute-start.6 = (bf16[12,16,128]{2,1,0:T(8,128)(2,1)S(1)}, bf16[12,16,128]{2,1,0:T(8,128)(2,1)S(1)}, u32[]{:S(2)}, u32[]{:S(2)}) collective-permute-start(bf16[12,16,128]{2,1,0:T(8,128)(2,1)S(1)} %get-tuple-element.49), channel_id=1, source_target_pairs={{0,31},{1,0},{2,1},{3,2},{4,3},{5,4},{6,5},{7,6},{8,7},{9,8},{10,9... | collective-permute-start | bytes 147464 | tf_op jit(solution)/shard_map/ppermute | solution.py:501
  57.4 11.1 %collective-permute-start.5 = (bf16[12,16,128]{2,1,0:T(8,128)(2,1)S(1)}, bf16[12,16,128]{2,1,0:T(8,128)(2,1)S(1)}, u32[]{:S(2)}, u32[]{:S(2)}) collective-permute-start(bf16[12,16,128]{2,1,0:T(8,128)(2,1)S(1)} %get-tuple-element.49), channel_id=1, source_target_pairs={{0,1},{1,2},{2,3},{3,4},{4,5},{5,6},{6,7},{7,8},{8,9},{9,10},{10,1... | collective-permute-start | bytes 147464 | tf_op jit(solution)/shard_map/ppermute | solution.py:500
  68.5 33.4 %copy-start.11 = (bf16[12,16,128]{2,1,0:T(8,128)(2,1)}, bf16[12,16,128]{2,1,0:T(8,128)(2,1)S(1)}, u32[]{:S(2)}) copy-start(bf16[12,16,128]{2,1,0:T(8,128)(2,1)S(1)} %get-tuple-element.55.refs_0_.refs_2_) | copy-start | bytes 147460
  68.5 27.8 %all-to-all-start = ((bf16[32,80,128]{2,1,0:T(8,128)(2,1)}), bf16[32,80,128]{2,1,0:T(8,128)(2,1)S(1)}, u32[]{:S(2)}, u32[]{:S(2)}) async-start(bf16[32,80,128]{2,1,0:T(8,128)(2,1)} %bitcast.7), calls=%async_computation | async-start | bytes 1310720 | tf_op jit(solution)/shard_map/all_to_all | solution.py:530
  78.4 18.0 %collective-permute-start.8 = (bf16[672,128]{1,0:T(8,128)(2,1)S(1)}, bf16[672,128]{1,0:T(8,128)(2,1)S(1)}, u32[]{:S(2)}, u32[]{:S(2)}) collective-permute-start(bf16[672,128]{1,0:T(8,128)(2,1)S(1)} %get-tuple-element.57), channel_id=1, source_target_pairs={{32,0},{33,1},{34,2},{35,3},{36,4},{37,5},{38,6},{39,7},{40,8},{41... | collective-permute-start | bytes 516104 | tf_op jit(solution)/shard_map/ppermute | solution.py:506
  83.0 13.4 %collective-permute-start.9 = (bf16[672,128]{1,0:T(8,128)(2,1)S(1)}, bf16[672,128]{1,0:T(8,128)(2,1)S(1)}, u32[]{:S(2)}, u32[]{:S(2)}) collective-permute-start(bf16[672,128]{1,0:T(8,128)(2,1)S(1)} %get-tuple-element.56), channel_id=1, source_target_pairs={{224,255},{225,254},{226,253},{227,252},{228,251},{229,250},{230,2... | collective-permute-start | bytes 516104 | tf_op jit(solution)/shard_map/ppermute | solution.py:504
  83.7 12.7 %collective-permute-start.7 = (bf16[672,128]{1,0:T(8,128)(2,1)S(1)}, bf16[672,128]{1,0:T(8,128)(2,1)S(1)}, u32[]{:S(2)}, u32[]{:S(2)}) collective-permute-start(bf16[672,128]{1,0:T(8,128)(2,1)S(1)} %get-tuple-element.56), channel_id=1, source_target_pairs={{0,32},{1,33},{2,34},{3,35},{4,36},{5,37},{6,38},{7,39},{8,40},{9,... | collective-permute-start | bytes 516104 | tf_op jit(solution)/shard_map/ppermute | solution.py:505
  97.2 13.3 %all-to-all-start.1 = ((bf16[8,80,128]{2,1,0:T(8,128)(2,1)}), bf16[8,80,128]{2,1,0:T(8,128)(2,1)S(1)}, u32[]{:S(2)}, u32[]{:S(2)}) async-start(bf16[8,80,128]{2,1,0:T(8,128)(2,1)} %spread.2.refs_10_), calls=%async_computation.1 | async-start | bytes 327680 | tf_op jit(solution)/shard_map/all_to_all | solution.py:532
  111.6 21.4 %copy-start.1 = (bf16[192,16,128]{2,1,0:T(8,128)(2,1)S(1)}, bf16[192,16,128]{2,1,0:T(8,128)(2,1)}, u32[]{:S(2)}) copy-start(bf16[192,16,128]{2,1,0:T(8,128)(2,1)} %back.1.refs_0_.after_ref) | copy-start | bytes 2359300
  111.6 21.4 %copy-start.17 = (s32[4]{0:T(128)S(1)}, s32[4]{0:T(128)}, u32[]{:S(2)}) copy-start(s32[4]{0:T(128)} %pad_add_fusion.at_ref.refs_0_) | copy-start | bytes 52
  111.6 6.9 %collective-permute-start.12 = (bf16[80,128]{1,0:T(8,128)(2,1)S(1)}, bf16[80,128]{1,0:T(8,128)(2,1)S(1)}, u32[]{:S(2)}, u32[]{:S(2)}) collective-permute-start(bf16[80,128]{1,0:T(8,128)(2,1)S(1)} %bitcast.13), channel_id=1, source_target_pairs={{0,128},{1,129},{4,132},{5,133},{8,136},{9,137},{12,140},{13,141},... | collective-permute-start | bytes 61448 | tf_op jit(solution)/shard_map/ppermute | solution.py:533
  117.4 2.6 %collective-permute-start.11 = (bf16[80,128]{1,0:T(8,128)(2,1)S(1)}, bf16[80,128]{1,0:T(8,128)(2,1)S(1)}, u32[]{:S(2)}, u32[]{:S(2)}) collective-permute-start(bf16[80,128]{1,0:T(8,128)(2,1)S(1)} %bitcast.14), channel_id=1, source_target_pairs={{0,192},{1,193},{4,196},{5,197},{8,200},{9,201},{12,204},{13,205},... | collective-permute-start | bytes 61448 | tf_op jit(solution)/shard_map/ppermute | solution.py:533
  117.4 2.6 %collective-permute-start.10 = (bf16[80,128]{1,0:T(8,128)(2,1)S(1)}, bf16[80,128]{1,0:T(8,128)(2,1)S(1)}, u32[]{:S(2)}, u32[]{:S(2)}) collective-permute-start(bf16[80,128]{1,0:T(8,128)(2,1)S(1)} %bitcast.15), channel_id=1, source_target_pairs={{0,64},{1,65},{4,68},{5,69},{8,72},{9,73},{12,76},{13,77},{16,80},... | collective-permute-start | bytes 61448 | tf_op jit(solution)/shard_map/ppermute | solution.py:533
  120.0 7.0 %collective-permute-start.15 = (bf16[320,128]{1,0:T(8,128)(2,1)S(1)}, bf16[320,128]{1,0:T(8,128)(2,1)S(1)}, u32[]{:S(2)}, u32[]{:S(2)}) collective-permute-start(bf16[320,128]{1,0:T(8,128)(2,1)S(1)} %pad_maximum_fusion), channel_id=1, source_target_pairs={{0,32},{1,33},{4,36},{5,37},{8,40},{9,41},{12,44},{13,45},{16,48},... | collective-permute-start | bytes 245768 | tf_op jit(solution)/shard_map/ppermute | solution.py:534
  120.1 6.9 %collective-permute-start.14 = (bf16[320,128]{1,0:T(8,128)(2,1)S(1)}, bf16[320,128]{1,0:T(8,128)(2,1)S(1)}, u32[]{:S(2)}, u32[]{:S(2)}) collective-permute-start(bf16[320,128]{1,0:T(8,128)(2,1)S(1)} %pad_maximum_fusion), channel_id=1, source_target_pairs={{0,34},{1,35},{4,38},{5,39},{8,42},{9,43},{12,46},{13,47},{16,50},... | collective-permute-start | bytes 245768 | tf_op jit(solution)/shard_map/ppermute | solution.py:534
  122.9 4.1 %collective-permute-start.13 = (bf16[320,128]{1,0:T(8,128)(2,1)S(1)}, bf16[320,128]{1,0:T(8,128)(2,1)S(1)}, u32[]{:S(2)}, u32[]{:S(2)}) collective-permute-start(bf16[320,128]{1,0:T(8,128)(2,1)S(1)} %pad_maximum_fusion), channel_id=1, source_target_pairs={{0,2},{1,3},{4,6},{5,7},{8,10},{9,11},{12,14},{13,15},{16,18},{17,... | collective-permute-start | bytes 245768 | tf_op jit(solution)/shard_map/ppermute | solution.py:534
  127.1 5.8 %collective-permute-start.16 = (bf16[1280,128]{1,0:T(8,128)(2,1)S(1)}, bf16[1280,128]{1,0:T(8,128)(2,1)S(1)}, u32[]{:S(2)}, u32[]{:S(2)}) collective-permute-start(bf16[1280,128]{1,0:T(8,128)(2,1)S(1)} %constant_dynamic-update-slice_fusion.a_ref), channel_id=1, source_target_pairs={{0,1},{1,0},{4,5},{5,4},{8,9},{9,8},{12,13},{13,12},{16,17},{17,16... | collective-permute-start | bytes 983048 | tf_op jit(solution)/shard_map/ppermute | solution.py:535
  (13 other events, 96.9 us)

commit v3 on v2

--- a/solution.py
+++ b/solution.py
@@ -15,6 +15,8 @@
 NT = (((1,), (1,)), ((), ()))
 VM = pl.BlockSpec(memory_space=pltpu.VMEM)
 SM = pl.BlockSpec(memory_space=pltpu.SMEM)
+ANY = pl.BlockSpec(memory_space=pl.ANY)
+HBM = pl.BlockSpec(memory_space=pltpu.HBM)
 
 
 def rim_base(b):
@@ -76,46 +78,64 @@
     return moved if held is None else jnp.where(lane >= 8 * j, moved, held)
 
 
-def prepare_kernel(at_ref, taps_ref, tab_ref, valid_ref, pit_ref, po_ref, gain_ref, t1_ref, t2_ref, pi_ref, pot_ref, col_ref, k1, k2):
-    def spread_taps(n):
-        cut = slice(n * 256, (n + 1) * 256)
-        parts = [lax.dot_general(taps_ref[a], tab_ref[a, :, cut], (((0,), (0,)), ((), ())), preferred_element_type=F) for a in range(7)]
-        return sum(parts[1:], parts[0])
-    k1[...] = spread_taps(0)
-    k2[...] = spread_taps(1)
+def spread_taps(taps_ref, tab_ref, n):
+    cut = slice(n * 256, (n + 1) * 256)
+    parts = [lax.dot_general(taps_ref[a], tab_ref[a, :, cut], (((0,), (0,)), ((), ())), preferred_element_type=F) for a in range(7)]
+    return sum(parts[1:], parts[0])
+
+
+def fill_matrices(k_ref, valid_ref, out_ref):
+    def block(i, _):
+        k = k_ref[pl.ds(pl.multiple_of(i * 16, 16), 16), :]
+        for j in range(16):
+            for h in range(2):
+                cut = slice(h * Q, (h + 1) * Q)
+                x = jnp.broadcast_to(k[j:j + 1, cut], (R, Q))
+                x = pltpu.roll(x, 0, 1, stride=1, stride_axis=0) * valid_ref[:, cut]
+                out_ref[i * 16 + j, :, cut] = x.astype(B)
+        return 0
+    lax.fori_loop(0, CH // 16, block, 0)
+
+
+def forward_kernel(taps_ref, tab_ref, valid_ref, gain_ref, t_ref, col_ref, k):
+    k[...] = spread_taps(taps_ref, tab_ref, 0)
+    fill_matrices(k, valid_ref, t_ref)
+    col_ref[...] = jnp.transpose(jnp.broadcast_to(gain_ref[...], (8, CH)))[:, :1]
+
+
+def backward_kernel(at_ref, taps_ref, tab_ref, valid_ref, pit_ref, po_ref, t_ref, pi_ref, pot_ref, k):
+    k[...] = spread_taps(taps_ref, tab_ref, 0)
 
     @pl.when(at_ref[0] != 0)
     def _():
-        k2[...] = spread_taps(2)
-
-    def block(i, _):
-        rows = pl.ds(pl.multiple_of(i * 16, 16), 16)
-        for src, dst in ((k1, t1_ref), (k2, t2_ref)):
-            k = src[rows, :]
-            for j in range(16):
-                for h in range(2):
-                    cut = slice(h * Q, (h + 1) * Q)
-                    x = jnp.broadcast_to(k[j:j + 1, cut], (R, Q))
-                    x = pltpu.roll(x, 0, 1, stride=1, stride_axis=0) * valid_ref[:, cut]
-                    dst[i * 16 + j, :, cut] = x.astype(B)
-        return 0
-    lax.fori_loop(0, CH // 16, block, 0)
+        k[...] = spread_taps(taps_ref, tab_ref, 1)
+    fill_matrices(k, valid_ref, t_ref)
     pi_ref[...] = jnp.transpose(pit_ref[...].astype(F)).astype(B)
     pot_ref[...] = jnp.transpose(po_ref[...].astype(F)).astype(B)
-    col_ref[...] = jnp.transpose(jnp.broadcast_to(gain_ref[...], (8, CH)))[:, :1]
-
-
-def prepare(at, kernel, pit, po, gain):
-    tab = np.concatenate([INNER + UPPER, (INNER + UPPER)[::-1], INNER[::-1] + UPPER], axis=1)
-    mat = jax.ShapeDtypeStruct((CH, R, 256), B)
-    return pl.pallas_call(
-        prepare_kernel,
-        out_shape=(mat, mat, jax.ShapeDtypeStruct((HID, CH), B), jax.ShapeDtypeStruct((HID, CH), B), jax.ShapeDtypeStruct((CH, 1), F)),
-        in_specs=[SM] + [VM] * 6, out_specs=(VM,) * 5, name="prepare",
-        scratch_shapes=[pltpu.VMEM((CH, 256), F)] * 2,
+
+
+def forward_matrices(kernel, gain):
+    return pl.pallas_call(
+        forward_kernel,
+        out_shape=(jax.ShapeDtypeStruct((CH, R, 256), B), jax.ShapeDtypeStruct((CH, 1), F)),
+        in_specs=[VM] * 4, out_specs=(VM,) * 2, name="forward_matrices",
+        scratch_shapes=[pltpu.VMEM((CH, 256), F)],
         compiler_params=pltpu.CompilerParams(vmem_limit_bytes=56 << 20),
         cost_estimate=pl.CostEstimate(flops=1 << 30, bytes_accessed=8 << 20, transcendentals=0),
-    )(at, kernel.transpose(1, 2, 0), jnp.asarray(tab.reshape(7, 7, 768), B), jnp.asarray(VALID), pit, po, gain.reshape(1, CH))
+    )(kernel.transpose(1, 2, 0), jnp.asarray((INNER + UPPER).reshape(7, 7, 256), B), jnp.asarray(VALID), gain.reshape(1, CH))
+
+
+def backward_matrices(at, kernel, pit, po):
+    tab = np.concatenate([(INNER + UPPER)[::-1], INNER[::-1] + UPPER], axis=1)
+    turned = jax.ShapeDtypeStruct((HID, CH), B)
+    return pl.pallas_call(
+        backward_kernel,
+        out_shape=(jax.ShapeDtypeStruct((CH, R, 256), B), turned, turned),
+        in_specs=[SM] + [VM] * 5, out_specs=(VM,) * 3, name="backward_matrices",
+        scratch_shapes=[pltpu.VMEM((CH, 256), F)],
+        compiler_params=pltpu.CompilerParams(vmem_limit_bytes=56 << 20),
+        cost_estimate=pl.CostEstimate(flops=1 << 30, bytes_accessed=8 << 20, transcendentals=0),
+    )(at, kernel.transpose(1, 2, 0), jnp.asarray(tab.reshape(7, 7, 512), B), jnp.asarray(VALID), pit, po)
 
 
 def start_kernel(f_ref, land_ref, m_ref, side_ref, low_ref, high_ref, s):
@@ -150,7 +170,7 @@
 
 
 def corner_kernel(left_ref, right_ref, low_ref, high_ref, *refs):
-    side_ref, lo_ref, hi_ref = refs[1:4] if len(refs) > 3 else refs
+    side_ref, lo_ref, hi_ref = refs[-3:]
     lane = lanes(R) % 8
     rows = 3 * CH
     lo_ref[:rows, :] = low_ref[...]
@@ -164,16 +184,13 @@
         hi_ref[here, :] = jnp.concatenate([both[t][8:], both[t + 1][8:]], axis=0).astype(B)
 
 
-def corners(left, right, low, high, *later):
+def corners(left, right, low, high, after):
     msg = jax.ShapeDtypeStruct((MSG, Q), B)
-    anywhere = [pl.BlockSpec(memory_space=pl.ANY)] * len(later)
-    return pl.pallas_call(
-        corner_kernel,
-        out_shape=(jax.ShapeDtypeStruct((12, R, Q), B), msg, msg) + tuple(jax.ShapeDtypeStruct(x.shape, x.dtype) for x in later),
-        in_specs=[VM] * 4 + anywhere, out_specs=(VM,) * 3 + tuple(anywhere), name="corners",
-        input_output_aliases={4: 3} if later else {},
+    return pl.pallas_call(
+        corner_kernel, out_shape=(jax.ShapeDtypeStruct((12, R, Q), B), msg, msg),
+        in_specs=[VM] * 4 + [HBM], out_specs=(VM,) * 3, name="corners",
         compiler_params=pltpu.CompilerParams(vmem_limit_bytes=8 << 20),
-    )(left, right, low, high, *later)
+    )(left, right, low, high, after)
 
 
 def unpack_rims(top, south_ref, north_ref, fold_ref, mirror_ref, rim, edge):
@@ -229,13 +246,37 @@
         out[112 + 8 * b:128 + 8 * b, :] = jnp.concatenate(rims[b:b + 2], axis=0).astype(B)
 
 
-def front_kernel(at_ref, m_ref, side_ref, south_ref, north_ref, fold_ref, t_ref, f_ref, cot_ref, land_ref, gain_ref,
-                 pi_ref, pit_ref, po_ref, pot_ref, mirror_ref,
-                 up_ref, gc_ref, grev_ref, gside_ref, low_ref, high_ref, gacc, wall,
-                 im, rim, edge, s, mcs, u, g, grev, sc, mcb, act, gh):
+def front_kernel(at_ref, m_hbm, side_ref, south_ref, north_ref, fold_ref, t_hbm, f_hbm, cot_hbm, land_ref, gain_ref,
+                 pi_hbm, pit_hbm, po_hbm, pot_hbm, mirror_ref, after_ref,
+                 up_hbm, gc_hbm, grev_hbm, gside_ref, low_ref, high_ref, gacc, wall, kept_ref,
+                 im, rim, edge, s, mcs, u, g, grev, sc, mcb, act, gh, kept_sem,
+                 m_ref, t_ref, f_ref, cot_ref, pi_ref, pit_ref, po_ref, pot_ref, m_sem, t_sem, sem,
+                 up_ref, gc_ref, grev_ref, out_sem):
+    def keep(i):
+        here = pl.ds(i * BLOCKS, BLOCKS)
+        return pltpu.make_async_copy(im.at[here], kept_ref.at[here], kept_sem.at[i])
+
+    def fetch(i):
+        here = pl.ds(i * BLOCKS, BLOCKS)
+        return (pltpu.make_async_copy(m_hbm.at[here], m_ref.at[here], m_sem.at[i]),
+                pltpu.make_async_copy(t_hbm.at[here], t_ref.at[here], t_sem.at[i]))
+    def send(i):
+        here = pl.ds(i * BLOCKS, BLOCKS)
+        pairs = ((up_ref, up_hbm), (gc_ref, gc_hbm), (grev_ref, grev_hbm))
+        return [pltpu.make_async_copy(a.at[here], b.at[here], out_sem.at[3 * i + k]) for k, (a, b) in enumerate(pairs)]
+    for i in range(CH // BLOCKS):
+        for copy in fetch(i):
+            copy.start()
+    whole = ((cot_hbm, cot_ref), (pi_hbm, pi_ref), (pit_hbm, pit_ref), (po_hbm, po_ref), (pot_hbm, pot_ref), (f_hbm, f_ref))
+    whole = [pltpu.make_async_copy(a, b, sem.at[i]) for i, (a, b) in enumerate(whole)]
+    for copy in whole:
+        copy.start()
+
     unpack_rims(at_ref[0], south_ref, north_ref, fold_ref, mirror_ref, rim, edge)
 
     def conv_block(i, _):
+        for copy in fetch(i):
+            copy.wait()
         for j in range(BLOCKS):
             c = i * BLOCKS + j
             t = i * (BLOCKS // 16) + j // 16
@@ -243,6 +284,7 @@
         for j in range(BLOCKS):
             c = i * BLOCKS + j
             s[pl.ds(pl.multiple_of(c * R, R), R), :] = jnp.dot(t_ref[c][:, :TAPS], im[c], preferred_element_type=F)
+        keep(i).start()
         return 0
     lax.fori_loop(0, CH // BLOCKS, conv_block, 0)
     ocean = land_ref[...].astype(F)
@@ -268,6 +310,7 @@
             s[rows, :] = (s[rows, :] - mean) * rstd
             mcs[rows, :] = cot_ref[c].astype(F) * ocean
         return 0
+    whole[0].wait()
     lax.fori_loop(0, CH // BLOCKS, norm_block, 0)
     u[pl.ds(CH * R, R), :] = rstd
     gain = gain_ref[...]
@@ -313,7 +356,10 @@
             g[pl.ds(r0 + h, CH, stride=R), :] = gcv[:, cut]
             grev[pl.ds(R - 1 - r0 - h, CH, stride=R), :] = gcv[:, cut]
         return 0
+    for copy in whole[1:5]:
+        copy.wait()
     lax.fori_loop(0, R // 2, rows_step, 0)
+    whole[5].wait()
 
     lane = lanes(R)
 
@@ -329,6 +375,8 @@
             held = pack_sides(gb, j % 16, None if j % 16 == 0 else held, lane)
             if j % 16 == 15:
                 gside_ref[i * (BLOCKS // 16) + j // 16] = held
+        for copy in send(i):
+            copy.start()
         return 0
     lax.fori_loop(0, CH // BLOCKS, out_block, 0)
     for k in range(3):
@@ -339,39 +387,51 @@
         hs = slice(h * Q, (h + 1) * Q)
         wall[pl.ds(h * CH, CH), :] = lax.dot_general(mcb[...], act[hs, :], NT, preferred_element_type=F).astype(B)
         wall[pl.ds((6 + h) * CH, CH), :] = lax.dot_general(sc[...], gh[hs, :], NT, preferred_element_type=F).astype(B)
-
-
-def front(at, masked, side, south, north, fold, t, fields, cot, land, gain, pi, pit, po, pot):
+    for i in range(CH // BLOCKS):
+        keep(i).wait()
+        for copy in send(i):
+            copy.wait()
+
+
+def front(at, masked, side, south, north, fold, t, fields, cot, land, gain, pi, pit, po, pot, after):
     block, rim = jax.ShapeDtypeStruct((CH, R, Q), B), jax.ShapeDtypeStruct((3 * CH, Q), B)
     plane = pltpu.VMEM((CH * R, Q), F)
     return pl.pallas_call(
         front_kernel,
         out_shape=(block, block, block, jax.ShapeDtypeStruct((12, R, Q), B), rim, rim, jax.ShapeDtypeStruct((CH, Q), F),
-                   jax.ShapeDtypeStruct((2560, Q), B)),
-        in_specs=[SM] + [VM] * 15, out_specs=(VM,) * 8,
+                   jax.ShapeDtypeStruct((2560, Q), B), jax.ShapeDtypeStruct((CH, TAPS, Q), B)),
+        in_specs=[SM, HBM, VM, VM, VM, VM, HBM, HBM, HBM, VM, VM, HBM, HBM, HBM, HBM, VM, HBM], out_specs=(HBM,) * 3 + (VM,) * 5 + (HBM,),
         scratch_shapes=[
             pltpu.VMEM((CH, TAPS, Q), B), pltpu.VMEM((CH * 8, Q), F), pltpu.VMEM((12, 8, Q), F),
             plane, plane, pltpu.VMEM((CH * R + R, Q), F), plane, plane,
             pltpu.VMEM((CH, R * Q), B), pltpu.VMEM((CH, R * Q), B), pltpu.VMEM((HID, R * Q), B), pltpu.VMEM((HID, R * Q), B),
+            pltpu.SemaphoreType.DMA((CH // BLOCKS,)),
+            pltpu.VMEM((CH, R, Q), B), pltpu.VMEM((CH, R, 256), B), pltpu.VMEM((CH, R, Q), B), pltpu.VMEM((CH, R, Q), B),
+            pltpu.VMEM((HID, CH), B), pltpu.VMEM((CH, HID), B), pltpu.VMEM((CH, HID), B), pltpu.VMEM((HID, CH), B),
+            pltpu.SemaphoreType.DMA((CH // BLOCKS,)), pltpu.SemaphoreType.DMA((CH // BLOCKS,)), pltpu.SemaphoreType.DMA((6,)),
+            pltpu.VMEM((CH, R, Q), B), pltpu.VMEM((CH, R, Q), B), pltpu.VMEM((CH, R, Q), B), pltpu.SemaphoreType.DMA((CH // BLOCKS * 3,)),
         ],
-        compiler_params=pltpu.CompilerParams(vmem_limit_bytes=40 << 20),
+        compiler_params=pltpu.CompilerParams(vmem_limit_bytes=58 << 20),
         cost_estimate=pl.CostEstimate(flops=6 << 30, bytes_accessed=12 << 20, transcendentals=3 << 20),
         name="front",
-    )(at, masked, side, south, north, fold, t, fields, cot, land, gain, pi, pit, po, pot, mirrors())
-
-
-def tap_kernel(at_ref, m_ref, side_ref, south_ref, north_ref, fold_ref, grev_ref, gacc_ref, mirror_ref, valid_ref, collect_ref, w_ref,
-               o_ref, im, rim, edge, dks):
-    unpack_rims(at_ref[0], south_ref, north_ref, fold_ref, mirror_ref, rim, edge)
+    )(at, masked, side, south, north, fold, t, fields, cot, land, gain, pi, pit, po, pot, mirrors(), after)
+
+
+def tap_kernel(im_hbm, grev_hbm, gacc_ref, valid_ref, collect_ref, w_ref, o_ref, im_ref, grev_ref, dks, im_sem, grev_sem):
+    def fetch(i):
+        here = pl.ds(i * BLOCKS, BLOCKS)
+        return (pltpu.make_async_copy(im_hbm.at[here], im_ref.at[here], im_sem.at[i]),
+                pltpu.make_async_copy(grev_hbm.at[here], grev_ref.at[here], grev_sem.at[i]))
+    for i in range(CH // BLOCKS):
+        for copy in fetch(i):
+            copy.start()
 
     def block(i, _):
+        for copy in fetch(i):
+            copy.wait()
         sums = [[], []]
         for j in range(BLOCKS):
-            c = i * BLOCKS + j
-            t = i * (BLOCKS // 16) + j // 16
-            operand(c, j % 16, m_ref[c], side_ref[t], rim[pl.ds(pl.multiple_of(c * 8, 8), 8), :], edge[t], im.at[j])
-        for j in range(BLOCKS):
-            dt = lax.dot_general(grev_ref[i * BLOCKS + j], im[j], NT, preferred_element_type=F)
+            dt = lax.dot_general(grev_ref[i * BLOCKS + j], im_ref[i * BLOCKS + j], NT, preferred_element_type=F)
             dt = [dt[:, :Q], jnp.concatenate([dt[:, Q:], jnp.zeros((R, 256 - TAPS), F)], axis=1)]
             for h in range(2):
                 x = pltpu.roll(dt[h] * valid_ref[:, h * Q:(h + 1) * Q], 0, 1, stride=1, stride_axis=0)
@@ -386,19 +446,21 @@
     o_ref[CH:, :] = jnp.zeros((256 - CH, Q), B)
 
 
-def taps(at, masked, rims, grev, gacc, w):
+def taps(kept, grev, gacc, w):
+    blocks = CH // BLOCKS
     return pl.pallas_call(
         tap_kernel,
         grid=(1,),
         out_shape=jax.ShapeDtypeStruct(w.shape, B),
-        in_specs=[SM] + [VM] * 10 + [pl.BlockSpec(memory_space=pl.ANY)],
+        in_specs=[HBM, HBM, VM, VM, VM, HBM],
         out_specs=pl.BlockSpec((256, Q), lambda i: (9, 0)),
-        scratch_shapes=[pltpu.VMEM((BLOCKS, TAPS, Q), B), pltpu.VMEM((CH * 8, Q), F), pltpu.VMEM((12, 8, Q), F), pltpu.VMEM((CH, 256), F)],
-        compiler_params=pltpu.CompilerParams(vmem_limit_bytes=40 << 20),
+        scratch_shapes=[pltpu.VMEM((CH, TAPS, Q), B), pltpu.VMEM((CH, R, Q), B), pltpu.VMEM((CH, 256), F),
+                        pltpu.SemaphoreType.DMA((blocks,)), pltpu.SemaphoreType.DMA((blocks,))],
+        compiler_params=pltpu.CompilerParams(vmem_limit_bytes=58 << 20),
         cost_estimate=pl.CostEstimate(flops=2 << 30, bytes_accessed=8 << 20, transcendentals=0),
-        input_output_aliases={11: 0},
+        input_output_aliases={5: 0},
         name="taps",
-    )(at, masked, *rims, grev, gacc, mirrors(), jnp.asarray(VALID[::-1].copy()), jnp.asarray(COLLECT), w)
+    )(kept, grev, gacc, jnp.asarray(VALID[::-1].copy()), jnp.asarray(COLLECT), w)
 
 
 def back_kernel(first, at_ref, m_ref, side_ref, south_ref, north_ref, fold_ref, t_ref, cot_ref, land_ref, mirror_ref, after_ref, *refs):
@@ -420,7 +482,7 @@
 
 def back(at, grad, rims, t, cot, land, after, first, count, begun=None):
     some = lambda *shape: pl.BlockSpec((BLOCKS,) + shape, lambda i: (first + i, 0, 0))
-    anywhere = pl.BlockSpec(memory_space=pl.ANY)
+    anywhere = HBM
     extra = [] if begun is None else [begun]
     return pl.pallas_call(
         lambda *refs: back_kernel(first, *refs),
@@ -436,6 +498,38 @@
     )(at, grad, *rims, t, cot, land, mirrors(), after, *extra)
 
 
+def half_kernel(at_ref, w_hbm, *refs):
+    o_ref, sem = refs[-2:]
+    copy = pltpu.make_async_copy(w_hbm.at[pl.ds(pl.multiple_of((1 - at_ref[3]) * 1280, 1280), 1280)], o_ref, sem)
+    copy.start()
+    copy.wait()
+
+
+def half(at, w, *after):
+    return pl.pallas_call(
+        half_kernel, out_shape=jax.ShapeDtypeStruct((1280, Q), B),
+        in_specs=[SM, HBM] + [HBM] * len(after), out_specs=VM, name="half",
+        scratch_shapes=[pltpu.SemaphoreType.DMA],
+        compiler_params=pltpu.CompilerParams(vmem_limit_bytes=8 << 20),
+    )(at, w, *after)
+
+
+def merge_kernel(at_ref, w_hbm, other_ref, after_ref, o_ref, own, sem):
+    copy = pltpu.make_async_copy(w_hbm.at[pl.ds(pl.multiple_of(at_ref[3] * 1280, 1280), 1280)], own, sem)
+    copy.start()
+    copy.wait()
+    o_ref[...] = (own[...].astype(F) + other_ref[...].astype(F)).astype(B)
+
+
+def merge(at, w, other, after):
+    return pl.pallas_call(
+        merge_kernel, out_shape=jax.ShapeDtypeStruct((1280, Q), B),
+        in_specs=[SM, HBM, VM, HBM], out_specs=VM, name="merge",
+        scratch_shapes=[pltpu.VMEM((1280, Q), B), pltpu.SemaphoreType.DMA],
+        compiler_params=pltpu.CompilerParams(vmem_limit_bytes=8 << 20),
+    )(at, w, other, after)
+
+
 def spread_kernel(x_ref, *refs):
     o_ref = refs[-1]
     total = x_ref[0].astype(F)
@@ -449,7 +543,7 @@
 def spread(x, copies, *after):
     return pl.pallas_call(
         spread_kernel, out_shape=jax.ShapeDtypeStruct((copies,) + x.shape[1:], B),
-        in_specs=[VM] + [pl.BlockSpec(memory_space=pl.ANY)] * len(after), out_specs=VM, name="spread",
+        in_specs=[VM] + [HBM] * len(after), out_specs=VM, name="spread",
         compiler_params=pltpu.CompilerParams(vmem_limit_bytes=8 << 20),
     )(x, *after)
 
@@ -463,7 +557,7 @@
     x, y, c = at_ref[1], at_ref[2], at_ref[3]
     for k in range(32):
         src = (a_ref, b_ref)[k // 16]
-        chunk = along(x, k % 4) * 8 + along(y, k // 4 % 4) * 2 + (c ^ (k // 16))
+        chunk = along(x, k % 4) * 4 + along(y, k // 4 % 4) + (c ^ (k // 16)) * 16
         wall[pl.ds(pl.multiple_of(chunk * 80, 80), 80), :] = src[pl.ds(k % 16 * 80, 80), :]
     scale = (128 * 4096) ** -0.5
     for h in range(6):
@@ -481,7 +575,7 @@
     return pl.pallas_call(
         finish_kernel,
         out_shape=tuple(jax.ShapeDtypeStruct(x, F) for x in shapes),
-        in_specs=[SM, VM, VM, pl.BlockSpec(memory_space=pl.ANY)], out_specs=(VM,) * 4, name="finish",
+        in_specs=[SM, VM, VM, HBM], out_specs=(VM,) * 4, name="finish",
         scratch_shapes=[pltpu.VMEM((2560, Q), B)],
         compiler_params=pltpu.CompilerParams(vmem_limit_bytes=16 << 20),
     )(at, first, second, after)
@@ -489,22 +583,22 @@
 
 ALL = ("x", "yh", "z", "yl", "c")
 LAT, LON = 8, 32
-PLANE = ("x", "yh", "yl", "c")
+PLANE = ("x", "yh", "yl")
 
 
 def lon_route(step):
     return [(y * LON + i, y * LON + (i + step) % LON) for y in range(LAT) for i in range(LON)]
 
 
-def rims(side, low, high, *later):
+def rims(side, low, high, after):
     left = lax.ppermute(side, ALL, lon_route(1))
     right = lax.ppermute(side, ALL, lon_route(-1))
-    side, low, high, *later = corners(left, right, low, high, *later)
+    side, low, high = corners(left, right, low, high, after)
     top = LON * (LAT - 1)
     fold = lax.ppermute(high, ALL, [(top + i, top + LON - 1 - i) for i in range(LON)])
     south = lax.ppermute(high, ALL, [(y * LON + i, (y + 1) * LON + i) for y in range(LAT - 1) for i in range(LON)])
     north = lax.ppermute(low, ALL, [(y * LON + i, (y - 1) * LON + i) for y in range(1, LAT) for i in range(LON)])
-    return (side, south, north, fold), *later
+    return (side, south, north, fold), (left, right)
 
 
 def swap_route(bx=0, by=0, bc=0):
@@ -521,13 +615,16 @@
     is_top = x * 2 + lax.axis_index("yh") == LAT - 1
     at = jnp.stack([is_top.astype(jnp.int32), x, y, c]).astype(jnp.int32)
     masked, side, low, high = start(fields, land_sea)
-    one, two, pi, pot, gain = prepare(at, kernel, proj_in.T, proj_out, ln_gain)
-    ends, one = rims(side, low, high, one)
-    updated, grad, reverse, side, low, high, gacc, w = front(
-        at, masked, *ends, one, fields, cotangent, land_sea, gain, pi, proj_in.T, proj_out, pot)
-    w = taps(at, masked, ends, reverse, gacc, w)
-    ends, w = rims(side, low, high, w)
-    w = spread(lax.all_to_all(w.reshape(32, 80, Q), PLANE, 0, 0), 8, *ends)
+    one, gain = forward_matrices(kernel, ln_gain)
+    ends, _ = rims(side, low, high, one)
+    two, pi, pot = backward_matrices(at, kernel, proj_in.T, proj_out)
+    updated, grad, reverse, side, low, high, gacc, w, kept = front(
+        at, masked, *ends, one, fields, cotangent, land_sea, gain, pi, proj_in.T, proj_out, pot, two)
+    w = taps(kept, reverse, gacc, w)
+    ends, beside = rims(side, low, high, w)
+    other = lax.ppermute(half(at, w, *beside), ALL, swap_route(bc=1))
+    w = merge(at, w, other, ends[0])
+    w = spread(lax.all_to_all(w.reshape(16, 80, Q), PLANE, 0, 0), 8, *ends)
     grad_fields = back(at, grad, ends, two, cotangent, land_sea, w, 0, 6)
     w = spread(lax.all_to_all(w, "z", 0, 0), 1, grad_fields)[0]
     w = jnp.concatenate([w] + [lax.ppermute(w, ALL, swap_route(bx=k)) for k in (1, 2, 3)])

time: 137 us -> 135 us (0.985)
  waiting for transfers between devices: 24 us -> 18.6 us
  Pallas kernels: 52 us -> 56.1 us
  starting transfers between devices: 51.9 us -> 50.3 us
    ppermute x2, waiting for transfers between devices: 10.6 us -> 5.65 us  [rims(): lax.ppermute(low, ALL, [(y * LON + i, (y - 1) * LON + i) for y in range(1...]
    pallas_call x1 -> x4, Pallas kernels: 6.16 us -> 10.7 us  [the longest x1 4.54 us: backward_matrices(): pl.pallas_call(backward_kernel, out_shape=(jax.ShapeDtypeStruct((CH, R, 2...]
    ppermute x2, waiting for transfers between devices: 6.37 us -> 2.54 us  [rims(): lax.ppermute(high, ALL, [(y * LON + i, (y + 1) * LON + i) for y in range(...]
    ppermute x2, starting transfers between devices: 4.3 us -> 6.72 us  [rims(): lax.ppermute(high, ALL, [(y * LON + i, (y + 1) * LON + i) for y in range(...]
    ppermute x2, waiting for transfers between devices: 0.01 us -> 2.03 us  [rims(): left = lax.ppermute(side, ALL, lon_route(1))]
    pallas_call x1, Pallas kernels: 11.1 us -> 9.13 us  [taps(): pl.pallas_call(tap_kernel, grid=(1,), out_shape=jax.ShapeDtypeStruct(w.sh...]
    ppermute x2, starting transfers between devices: 6.96 us -> 5.02 us  [rims(): right = lax.ppermute(side, ALL, lon_route(-1))]
    pallas_call x1, Pallas kernels: 20.9 us -> 22.6 us  [front(): pl.pallas_call(front_kernel, out_shape=(block, block, block, jax.ShapeDty...]
  transfers between devices with their start and end apart: 19 -> 20, of which waited for: 7 -> 11; matrix products, arithmetic and copies ran while one was open for 0% -> 0% of each run, Pallas kernels for 19% -> 20%
where the time goes in v3:
time: 135 us; the launch traced here: 133 us
  Pallas kernels  56.1 us (42%)
  starting transfers between devices  50.3 us (37%)
  waiting for transfers between devices  18.6 us (14%)
  local copies, waits for them, and re-layouts  6.24 us (5%)
    pallas_call x1, Pallas kernels, front(): pl.pallas_call(front_kernel, out_shape=(block, block, block, jax.ShapeDty...  22.6 us
    pallas_call x1, Pallas kernels, taps(): pl.pallas_call(tap_kernel, grid=(1,), out_shape=jax.ShapeDtypeStruct(w.sh...  9.13 us
    all_to_all x1, starting transfers between devices, on_device(): w = spread(lax.all_to_all(w.reshape(16, 80, Q), PLANE, 0, 0), 8, *ends)  8.86 us
    pallas_call x1, Pallas kernels, back(): pl.pallas_call(lambda *refs: back_kernel(first, *refs), grid=(count,), ou...  8.49 us
    ppermute x2, starting transfers between devices, rims(): lax.ppermute(low, ALL, [(y * LON + i, (y - 1) * LON + i) for y in range(1...  7.74 us
    ppermute x2, starting transfers between devices, rims(): lax.ppermute(high, ALL, [(y * LON + i, (y + 1) * LON + i) for y in range(...  6.72 us
    unnamed x46, local copies, waits for them, and re-layouts  6.22 us
    ppermute x3, starting transfers between devices, on_device(): lax.ppermute(w, ALL, swap_route(bx=k))  5.98 us
  transfers between devices with their start and end apart: 20, of which 11 were waited for; matrix products, arithmetic and copies ran while one was open for 0% of the time, Pallas kernels for 20%

profile of v3, /device:TPU:3, one launch (start us, length us, event | category | flops | bytes accessed | tf_op | source)
XLA Modules:
  0.0 132.8 jit_solution(8773606066068571044)
XLA Ops:
  0.6 2.7 %start.1 = (bf16[192,16,128]{2,1,0:T(8,128)(2,1)}, bf16[12,16,128]{2,1,0:T(8,128)(2,1)}, bf16[576,128]{1,0:T(8,128)(2,1)}, bf16[576,128]{1,0:T(8,128)(2,1)}) custom-call(bf16[192,16,128]{2,1,0:T(8,128)(2,1)} %f_hbm.1, s32[16,128]{1,0:T(8,128)} %refs_8_.1), custom_call_target="tpu_custom_call" | custom-call | tf_op jit(solution)/shard_map/start/pallas_call | solution.py:164
  4.0 1.2 collective-permute-start
  5.2 4.0 %forward_matrices.1 = (bf16[192,16,256]{2,1,0:T(8,128)(2,1)}, f32[192,1]{1,0:T(8,128)}) custom-call(bf16[7,7,192]{2,1,0:T(8,128)(2,1)} %bitcast.21, bf16[7,7,256]{2,1,0:T(8,128)(2,1)} %constant.32.clone.tab_ref, f32[16,256]{1,0:T(8,128)} %constant.33.clone.valid_ref, f32[1,192]{1,0:T(1,128)} %bitcast.23), custom_call_target="tpu_custom_call" | custom-call | flops 1073741824 | bytes 8388608 | tf_op jit(solution)/shard_map/forward_matrices/pallas_call | solution.py:118
  9.2 2.0 %collective-permute-done.left_ref = bf16[12,16,128]{2,1,0:T(8,128)(2,1)S(1)} collective-permute-done((bf16[12,16,128]{2,1,0:T(8,128)(2,1)}, bf16[12,16,128]{2,1,0:T(8,128)(2,1)S(1)}, u32[]{:S(2)}, u32[]{:S(2)}) %collective-permute-start) | collective-permute-done | bytes 49184 | tf_op jit(solution)/shard_map/ppermute | solution.py:594
  11.2 1.4 %copy-done.5 = bf16[192,16,256]{2,1,0:T(8,128)(2,1)S(1)} copy-done((bf16[192,16,256]{2,1,0:T(8,128)(2,1)S(1)}, bf16[192,16,256]{2,1,0:T(8,128)(2,1)}, u32[]{:S(2)}) %copy-start.5) | copy-done | bytes 1572888
  14.0 4.5 %collective-permute-start.2 = (bf16[672,128]{1,0:T(8,128)(2,1)S(1)}, bf16[672,128]{1,0:T(8,128)(2,1)S(1)}, u32[]{:S(2)}, u32[]{:S(2)}) collective-permute-start(bf16[672,128]{1,0:T(8,128)(2,1)S(1)} %get-tuple-element.40), channel_id=1, source_target_pairs={{0,32},{1,33},{2,34},{3,35},{4,36},{5,37},{6,38},{7,39},{8,40},{9,... | collective-permute-start | bytes 516104 | tf_op jit(solution)/shard_map/ppermute | solution.py:599
  18.5 3.2 %collective-permute-start.3 = (bf16[672,128]{1,0:T(8,128)(2,1)S(1)}, bf16[672,128]{1,0:T(8,128)(2,1)S(1)}, u32[]{:S(2)}, u32[]{:S(2)}) collective-permute-start(bf16[672,128]{1,0:T(8,128)(2,1)S(1)} %get-tuple-element.41), channel_id=1, source_target_pairs={{32,0},{33,1},{34,2},{35,3},{36,4},{37,5},{38,6},{39,7},{40,8},{41... | collective-permute-start | bytes 516104 | tf_op jit(solution)/shard_map/ppermute | solution.py:600
  22.2 4.5 %backward_matrices.1 = (bf16[192,16,256]{2,1,0:T(8,128)(2,1)}, bf16[768,192]{1,0:T(8,128)(2,1)}, bf16[768,192]{1,0:T(8,128)(2,1)}) custom-call(s32[4]{0:T(128)} %pad_add_fusion.at_ref.refs_0_, bf16[7,7,192]{2,1,0:T(8,128)(2,1)} %bitcast.22, bf16[7,7,512]{2,1,0:T(8,128)(2,1)} %constant.34.clone.tab_ref, f32[16,256]{1,0:T(8,128)} %constant.33.clone.valid_ref, ...), custom_call_target="tpu_custom_call" | custom-call | flops 1073741824 | bytes 8388608 | tf_op jit(solution)/shard_map/backward_matrices/pallas_call | solution.py:131
  26.8 1.4 %collective-permute-done.3.north_ref = bf16[672,128]{1,0:T(8,128)(2,1)S(1)} collective-permute-done((bf16[672,128]{1,0:T(8,128)(2,1)S(1)}, bf16[672,128]{1,0:T(8,128)(2,1)S(1)}, u32[]{:S(2)}, u32[]{:S(2)}) %collective-permute-start.3) | collective-permute-done | bytes 172064 | tf_op jit(solution)/shard_map/ppermute | solution.py:600
  29.1 22.6 %front.1 = (bf16[192,16,128]{2,1,0:T(8,128)(2,1)}, bf16[192,16,128]{2,1,0:T(8,128)(2,1)}, bf16[192,16,128]{2,1,0:T(8,128)(2,1)}, bf16[12,16,128]{2,1,0:T(8,128)(...) custom-call(s32[4]{0:T(128)} %pad_add_fusion.at_ref.refs_0_, ...), custom_call_target="tpu_custom_call" | custom-call | flops 6442450944 | bytes 12582912 | tf_op jit(solution)/shard_map/front/pallas_call | solution.py:399
  51.7 4.3 %collective-permute-start.6 = (bf16[12,16,128]{2,1,0:T(8,128)(2,1)}, bf16[12,16,128]{2,1,0:T(8,128)(2,1)S(1)}, u32[]{:S(2)}, u32[]{:S(2)}) collective-permute-start(bf16[12,16,128]{2,1,0:T(8,128)(2,1)} %get-tuple-element.48), channel_id=1, source_target_pairs={{0,31},{1,0},{2,1},{3,2},{4,3},{5,4},{6,5},{7,6},{8,7},{9,8},{10,9... | collective-permute-start | bytes 147464 | tf_op jit(solution)/shard_map/ppermute | solution.py:595
  56.1 9.1 %taps.1.refs_0_.w_hbm = bf16[2560,128]{1,0:T(8,128)(2,1)} custom-call(bf16[192,176,128]{2,1,0:T(8,128)(2,1)} %get-tuple-element.51.im_hbm, bf16[192,16,128]{2,1,0:T(8,128)(2,1)} %get-tuple-element.52.grev_hbm, f32[192,128]{1,0:T(8,128)} %get-tuple-element.53.gacc_ref, f32[16,256]{1,0:T(8,128)} %constant.36.clone.valid_ref, ...), custom_call_target="tpu_custom_call", output_to_operand_aliasing={{}: (5, {})} | custom-call | flops 2147483648 | bytes 8388608 | tf_op jit(solution)/shard_map/taps/pallas_call | solution.py:451
  65.2 1.1 copy-done
  67.0 1.3 %collective-permute-start.10 = (bf16[1280,128]{1,0:T(8,128)(2,1)S(1)}, bf16[1280,128]{1,0:T(8,128)(2,1)S(1)}, u32[]{:S(2)}, u32[]{:S(2)}) collective-permute-start(bf16[1280,128]{1,0:T(8,128)(2,1)S(1)} %half.1), channel_id=1, source_target_pairs={{0,1},{1,0},{4,5},{5,4},{8,9},{9,8},{12,13},{13,12},{16,17},{17,16... | collective-permute-start | bytes 983048 | tf_op jit(solution)/shard_map/ppermute | solution.py:625
  68.3 1.1 copy-done.1
  69.6 1.5 %merge.1 = bf16[1280,128]{1,0:T(8,128)(2,1)} custom-call(s32[4]{0:T(128)S(1)} %copy-done.14, bf16[2560,128]{1,0:T(8,128)(2,1)S(1)} %copy-done.2, bf16[1280,128]{1,0:T(8,128)(2,1)S(1)} %collective-permute-done.10.other_ref, bf16[12,16,128]{2,1,0:T(8,128)(2,1)S(1)} %get-tuple-element.55.after_ref.refs_0_.refs_2_), custom_call_target="tpu_custom_call" | custom-call | tf_op jit(solution)/shard_map/merge/pallas_call | solution.py:525
  71.1 8.9 %all-to-all-start = ((bf16[16,80,128]{2,1,0:T(8,128)(2,1)}), bf16[16,80,128]{2,1,0:T(8,128)(2,1)S(1)}, u32[]{:S(2)}, u32[]{:S(2)}) async-start(bf16[16,80,128]{2,1,0:T(8,128)(2,1)} %bitcast.7), calls=%async_computation | async-start | bytes 655360 | tf_op jit(solution)/shard_map/all_to_all | solution.py:627
  79.9 4.6 %collective-permute-start.8 = (bf16[672,128]{1,0:T(8,128)(2,1)S(1)}, bf16[672,128]{1,0:T(8,128)(2,1)S(1)}, u32[]{:S(2)}, u32[]{:S(2)}) collective-permute-start(bf16[672,128]{1,0:T(8,128)(2,1)S(1)} %get-tuple-element.57), channel_id=1, source_target_pairs={{32,0},{33,1},{34,2},{35,3},{36,4},{37,5},{38,6},{39,7},{40,8},{41... | collective-permute-start | bytes 516104 | tf_op jit(solution)/shard_map/ppermute | solution.py:600
  85.2 2.2 %collective-permute-start.7 = (bf16[672,128]{1,0:T(8,128)(2,1)S(1)}, bf16[672,128]{1,0:T(8,128)(2,1)S(1)}, u32[]{:S(2)}, u32[]{:S(2)}) collective-permute-start(bf16[672,128]{1,0:T(8,128)(2,1)S(1)} %get-tuple-element.56), channel_id=1, source_target_pairs={{0,32},{1,33},{2,34},{3,35},{4,36},{5,37},{6,38},{7,39},{8,40},{9,... | collective-permute-start | bytes 516104 | tf_op jit(solution)/shard_map/ppermute | solution.py:599
  87.4 4.2 %collective-permute-done.8.refs_2_.refs_4_ = bf16[672,128]{1,0:T(8,128)(2,1)S(1)} collective-permute-done((bf16[672,128]{1,0:T(8,128)(2,1)S(1)}, bf16[672,128]{1,0:T(8,128)(2,1)S(1)}, u32[]{:S(2)}, u32[]{:S(2)}) %collective-permute-start.8) | collective-permute-done | bytes 172064 | tf_op jit(solution)/shard_map/ppermute | solution.py:600
  91.6 2.5 %collective-permute-done.7.refs_1_.refs_3_ = bf16[672,128]{1,0:T(8,128)(2,1)S(1)} collective-permute-done((bf16[672,128]{1,0:T(8,128)(2,1)S(1)}, bf16[672,128]{1,0:T(8,128)(2,1)S(1)}, u32[]{:S(2)}, u32[]{:S(2)}) %collective-permute-start.7) | collective-permute-done | bytes 172064 | tf_op jit(solution)/shard_map/ppermute | solution.py:599
  94.9 4.4 %all-to-all-start.1 = ((bf16[8,80,128]{2,1,0:T(8,128)(2,1)}), bf16[8,80,128]{2,1,0:T(8,128)(2,1)S(1)}, u32[]{:S(2)}, u32[]{:S(2)}) async-start(bf16[8,80,128]{2,1,0:T(8,128)(2,1)} %spread.2.refs_10_), calls=%async_computation.1 | async-start | bytes 327680 | tf_op jit(solution)/shard_map/all_to_all | solution.py:629
  99.3 8.5 %back.1.refs_0_.after_ref = bf16[192,16,128]{2,1,0:T(8,128)(2,1)} custom-call(s32[4]{0:T(128)} %pad_add_fusion.at_ref.refs_0_, bf16[192,16,128]{2,1,0:T(8,128)(2,1)} %get-tuple-element.47.refs_1_, bf16[12,16,128]{2,1,0:T(8,128)(2,1)} %copy-done.9, bf16[672,128]{1,0:T(8,128)(2,1)} %copy-done.8, bf16[672,128]{1,0:T(8,128)(2,1)} %copy-done.6, ...), custom_call_target="tpu_custom_call" | custom-call | flops 1073741824 | bytes 8388608 | tf_op jit(solution)/shard_map/back/pallas_call | solution.py:487
  107.8 1.1 copy-done.3
  109.0 5.0 %collective-permute-start.13 = (bf16[80,128]{1,0:T(8,128)(2,1)S(1)}, bf16[80,128]{1,0:T(8,128)(2,1)S(1)}, u32[]{:S(2)}, u32[]{:S(2)}) collective-permute-start(bf16[80,128]{1,0:T(8,128)(2,1)S(1)} %bitcast.13), channel_id=1, source_target_pairs={{0,128},{1,129},{4,132},{5,133},{8,136},{9,137},{12,140},{13,141},... | collective-permute-start | bytes 61448 | tf_op jit(solution)/shard_map/ppermute | solution.py:630
  115.1 1.5 %collective-permute-done.12 = bf16[80,128]{1,0:T(8,128)(2,1)S(1)} collective-permute-done((bf16[80,128]{1,0:T(8,128)(2,1)S(1)}, bf16[80,128]{1,0:T(8,128)(2,1)S(1)}, u32[]{:S(2)}, u32[]{:S(2)}) %collective-permute-start.12) | collective-permute-done | bytes 20512 | tf_op jit(solution)/shard_map/ppermute | solution.py:630
  116.7 4.3 %collective-permute-start.16 = (bf16[320,128]{1,0:T(8,128)(2,1)S(1)}, bf16[320,128]{1,0:T(8,128)(2,1)S(1)}, u32[]{:S(2)}, u32[]{:S(2)}) collective-permute-start(bf16[320,128]{1,0:T(8,128)(2,1)S(1)} %pad_maximum_fusion), channel_id=1, source_target_pairs={{0,32},{1,33},{4,36},{5,37},{8,40},{9,41},{12,44},{13,45},{16,48},... | collective-permute-start | bytes 245768 | tf_op jit(solution)/shard_map/ppermute | solution.py:631
  121.0 3.3 %collective-permute-done.14 = bf16[320,128]{1,0:T(8,128)(2,1)S(1)} collective-permute-done((bf16[320,128]{1,0:T(8,128)(2,1)S(1)}, bf16[320,128]{1,0:T(8,128)(2,1)S(1)}, u32[]{:S(2)}, u32[]{:S(2)}) %collective-permute-start.14) | collective-permute-done | bytes 81952 | tf_op jit(solution)/shard_map/ppermute | solution.py:631
  124.2 2.1 %collective-permute-done.15 = bf16[320,128]{1,0:T(8,128)(2,1)S(1)} collective-permute-done((bf16[320,128]{1,0:T(8,128)(2,1)S(1)}, bf16[320,128]{1,0:T(8,128)(2,1)S(1)}, u32[]{:S(2)}, u32[]{:S(2)}) %collective-permute-start.15) | collective-permute-done | bytes 81952 | tf_op jit(solution)/shard_map/ppermute | solution.py:631
  126.4 3.4 %collective-permute-start.17 = (bf16[1280,128]{1,0:T(8,128)(2,1)S(1)}, bf16[1280,128]{1,0:T(8,128)(2,1)S(1)}, u32[]{:S(2)}, u32[]{:S(2)}) collective-permute-start(bf16[1280,128]{1,0:T(8,128)(2,1)S(1)} %constant_dynamic-update-slice_fusion.a_ref), channel_id=1, source_target_pairs={{0,1},{1,0},{4,5},{5,4},{8,9},{9,8},{12,13},{13,12},{16,17},{17,16... | collective-permute-start | bytes 983048 | tf_op jit(solution)/shard_map/ppermute | solution.py:632
  129.8 1.3 collective-permute-done.17.b_ref
  131.1 1.7 %finish.1 = (f32[192,768]{1,0:T(8,128)}, f32[192,768]{1,0:T(8,128)}, f32[7,7,192]{2,1,0:T(8,128)}, f32[1,192]{1,0:T(1,128)}) custom-call(s32[4]{0:T(128)S(1)} %copy-done.15, bf16[1280,128]{1,0:T(8,128)(2,1)S(1)} %constant_dynamic-update-slice_fusion.a_ref, bf16[1280,128]{1,0:T(8,128)(2,1)S(1)} %collective-permute-done.17.b_ref, ...), custom_call_target="tpu_custom_call" | custom-call | tf_op jit(solution)/shard_map/finish/pallas_call | solution.py:575
  (70 shorter events, 7.0 us)
Async XLA Ops:
  3.3 5.9 %collective-permute-start.1 = (bf16[12,16,128]{2,1,0:T(8,128)(2,1)}, bf16[12,16,128]{2,1,0:T(8,128)(2,1)S(1)}, u32[]{:S(2)}, u32[]{:S(2)}) collective-permute-start(bf16[12,16,128]{2,1,0:T(8,128)(2,1)} %get-tuple-element.35), channel_id=1, source_target_pairs={{0,31},{1,0},{2,1},{3,2},{4,3},{5,4},{6,5},{7,6},{8,7},{9,8},{10,9... | collective-permute-start | bytes 147464 | tf_op jit(solution)/shard_map/ppermute | solution.py:595
  4.0 7.2 %collective-permute-start = (bf16[12,16,128]{2,1,0:T(8,128)(2,1)}, bf16[12,16,128]{2,1,0:T(8,128)(2,1)S(1)}, u32[]{:S(2)}, u32[]{:S(2)}) collective-permute-start(bf16[12,16,128]{2,1,0:T(8,128)(2,1)} %get-tuple-element.35), channel_id=1, source_target_pairs={{0,1},{1,2},{2,3},{3,4},{4,5},{5,6},{6,7},{7,8},{8,9},{9,10},{10,1... | collective-permute-start | bytes 147464 | tf_op jit(solution)/shard_map/ppermute | solution.py:594
  5.2 6.1 %copy-start.12 = (bf16[576,128]{1,0:T(8,128)(2,1)S(1)}, bf16[576,128]{1,0:T(8,128)(2,1)}, u32[]{:S(2)}) copy-start(bf16[576,128]{1,0:T(8,128)(2,1)} %get-tuple-element.36.low_ref) | copy-start | bytes 442372
  5.2 6.1 %copy-start.13 = (bf16[576,128]{1,0:T(8,128)(2,1)S(1)}, bf16[576,128]{1,0:T(8,128)(2,1)}, u32[]{:S(2)}) copy-start(bf16[576,128]{1,0:T(8,128)(2,1)} %get-tuple-element.37.high_ref) | copy-start | bytes 442372
  13.3 14.9 %collective-permute-start.4 = (bf16[672,128]{1,0:T(8,128)(2,1)S(1)}, bf16[672,128]{1,0:T(8,128)(2,1)S(1)}, u32[]{:S(2)}, u32[]{:S(2)}) collective-permute-start(bf16[672,128]{1,0:T(8,128)(2,1)S(1)} %get-tuple-element.40), channel_id=1, source_target_pairs={{224,255},{225,254},{226,253},{227,252},{228,251},{229,250},{230,2... | collective-permute-start | bytes 516104 | tf_op jit(solution)/shard_map/ppermute | solution.py:598
  14.0 14.3 %collective-permute-start.2 = (bf16[672,128]{1,0:T(8,128)(2,1)S(1)}, bf16[672,128]{1,0:T(8,128)(2,1)S(1)}, u32[]{:S(2)}, u32[]{:S(2)}) collective-permute-start(bf16[672,128]{1,0:T(8,128)(2,1)S(1)} %get-tuple-element.40), channel_id=1, source_target_pairs={{0,32},{1,33},{2,34},{3,35},{4,36},{5,37},{6,38},{7,39},{8,40},{9,... | collective-permute-start | bytes 516104 | tf_op jit(solution)/shard_map/ppermute | solution.py:599
  18.5 9.7 %collective-permute-start.3 = (bf16[672,128]{1,0:T(8,128)(2,1)S(1)}, bf16[672,128]{1,0:T(8,128)(2,1)S(1)}, u32[]{:S(2)}, u32[]{:S(2)}) collective-permute-start(bf16[672,128]{1,0:T(8,128)(2,1)S(1)} %get-tuple-element.41), channel_id=1, source_target_pairs={{32,0},{33,1},{34,2},{35,3},{36,4},{37,5},{38,6},{39,7},{40,8},{41... | collective-permute-start | bytes 516104 | tf_op jit(solution)/shard_map/ppermute | solution.py:600
  51.7 13.5 %collective-permute-start.6 = (bf16[12,16,128]{2,1,0:T(8,128)(2,1)}, bf16[12,16,128]{2,1,0:T(8,128)(2,1)S(1)}, u32[]{:S(2)}, u32[]{:S(2)}) collective-permute-start(bf16[12,16,128]{2,1,0:T(8,128)(2,1)} %get-tuple-element.48), channel_id=1, source_target_pairs={{0,31},{1,0},{2,1},{3,2},{4,3},{5,4},{6,5},{7,6},{8,7},{9,8},{10,9... | collective-permute-start | bytes 147464 | tf_op jit(solution)/shard_map/ppermute | solution.py:595
  56.0 9.2 %collective-permute-start.5 = (bf16[12,16,128]{2,1,0:T(8,128)(2,1)}, bf16[12,16,128]{2,1,0:T(8,128)(2,1)S(1)}, u32[]{:S(2)}, u32[]{:S(2)}) collective-permute-start(bf16[12,16,128]{2,1,0:T(8,128)(2,1)} %get-tuple-element.48), channel_id=1, source_target_pairs={{0,1},{1,2},{2,3},{3,4},{4,5},{5,6},{6,7},{7,8},{8,9},{9,10},{10,1... | collective-permute-start | bytes 147464 | tf_op jit(solution)/shard_map/ppermute | solution.py:594
  56.0 9.2 %copy-start.14 = (s32[4]{0:T(128)S(1)}, s32[4]{0:T(128)}, u32[]{:S(2)}) copy-start(s32[4]{0:T(128)} %pad_add_fusion.at_ref.refs_0_) | copy-start | bytes 52
  56.0 12.3 %copy-start.10 = (bf16[576,128]{1,0:T(8,128)(2,1)S(1)}, bf16[576,128]{1,0:T(8,128)(2,1)}, u32[]{:S(2)}) copy-start(bf16[576,128]{1,0:T(8,128)(2,1)} %get-tuple-element.49.low_ref) | copy-start | bytes 442372
  56.0 12.3 %copy-start.11 = (bf16[576,128]{1,0:T(8,128)(2,1)S(1)}, bf16[576,128]{1,0:T(8,128)(2,1)}, u32[]{:S(2)}) copy-start(bf16[576,128]{1,0:T(8,128)(2,1)} %get-tuple-element.50.high_ref) | copy-start | bytes 442372
  66.3 3.3 %copy-start.2 = (bf16[2560,128]{1,0:T(8,128)(2,1)S(1)}, bf16[2560,128]{1,0:T(8,128)(2,1)}, u32[]{:S(2)}) copy-start(bf16[2560,128]{1,0:T(8,128)(2,1)} %taps.1.refs_0_.w_hbm) | copy-start | bytes 1966084
  67.0 2.6 %collective-permute-start.10 = (bf16[1280,128]{1,0:T(8,128)(2,1)S(1)}, bf16[1280,128]{1,0:T(8,128)(2,1)S(1)}, u32[]{:S(2)}, u32[]{:S(2)}) collective-permute-start(bf16[1280,128]{1,0:T(8,128)(2,1)S(1)} %half.1), channel_id=1, source_target_pairs={{0,1},{1,0},{4,5},{5,4},{8,9},{9,8},{12,13},{13,12},{16,17},{17,16... | collective-permute-start | bytes 983048 | tf_op jit(solution)/shard_map/ppermute | solution.py:625
  69.5 25.4 %copy-start.9 = (bf16[12,16,128]{2,1,0:T(8,128)(2,1)}, bf16[12,16,128]{2,1,0:T(8,128)(2,1)S(1)}, u32[]{:S(2)}) copy-start(bf16[12,16,128]{2,1,0:T(8,128)(2,1)S(1)} %get-tuple-element.55.after_ref.refs_0_.refs_2_) | copy-start | bytes 147460
  71.1 23.1 %all-to-all-start = ((bf16[16,80,128]{2,1,0:T(8,128)(2,1)}), bf16[16,80,128]{2,1,0:T(8,128)(2,1)S(1)}, u32[]{:S(2)}, u32[]{:S(2)}) async-start(bf16[16,80,128]{2,1,0:T(8,128)(2,1)} %bitcast.7), calls=%async_computation | async-start | bytes 655360 | tf_op jit(solution)/shard_map/all_to_all | solution.py:627
  79.9 11.7 %collective-permute-start.8 = (bf16[672,128]{1,0:T(8,128)(2,1)S(1)}, bf16[672,128]{1,0:T(8,128)(2,1)S(1)}, u32[]{:S(2)}, u32[]{:S(2)}) collective-permute-start(bf16[672,128]{1,0:T(8,128)(2,1)S(1)} %get-tuple-element.57), channel_id=1, source_target_pairs={{32,0},{33,1},{34,2},{35,3},{36,4},{37,5},{38,6},{39,7},{40,8},{41... | collective-permute-start | bytes 516104 | tf_op jit(solution)/shard_map/ppermute | solution.py:600
  84.5 7.1 %collective-permute-start.9 = (bf16[672,128]{1,0:T(8,128)(2,1)S(1)}, bf16[672,128]{1,0:T(8,128)(2,1)S(1)}, u32[]{:S(2)}, u32[]{:S(2)}) collective-permute-start(bf16[672,128]{1,0:T(8,128)(2,1)S(1)} %get-tuple-element.56), channel_id=1, source_target_pairs={{224,255},{225,254},{226,253},{227,252},{228,251},{229,250},{230,2... | collective-permute-start | bytes 516104 | tf_op jit(solution)/shard_map/ppermute | solution.py:598
  85.2 8.9 %collective-permute-start.7 = (bf16[672,128]{1,0:T(8,128)(2,1)S(1)}, bf16[672,128]{1,0:T(8,128)(2,1)S(1)}, u32[]{:S(2)}, u32[]{:S(2)}) collective-permute-start(bf16[672,128]{1,0:T(8,128)(2,1)S(1)} %get-tuple-element.56), channel_id=1, source_target_pairs={{0,32},{1,33},{2,34},{3,35},{4,36},{5,37},{6,38},{7,39},{8,40},{9,... | collective-permute-start | bytes 516104 | tf_op jit(solution)/shard_map/ppermute | solution.py:599
  91.6 7.7 %copy-start.6 = (bf16[672,128]{1,0:T(8,128)(2,1)}, bf16[672,128]{1,0:T(8,128)(2,1)S(1)}, u32[]{:S(2)}) copy-start(bf16[672,128]{1,0:T(8,128)(2,1)S(1)} %collective-permute-done.8.refs_2_.refs_4_) | copy-start | bytes 516100
  91.6 7.7 %copy-start.7 = (bf16[672,128]{1,0:T(8,128)(2,1)}, bf16[672,128]{1,0:T(8,128)(2,1)S(1)}, u32[]{:S(2)}) copy-start(bf16[672,128]{1,0:T(8,128)(2,1)S(1)} %collective-permute-done.9.refs_3_.refs_5_) | copy-start | bytes 516100
  94.1 5.2 %copy-start.8 = (bf16[672,128]{1,0:T(8,128)(2,1)}, bf16[672,128]{1,0:T(8,128)(2,1)S(1)}, u32[]{:S(2)}) copy-start(bf16[672,128]{1,0:T(8,128)(2,1)S(1)} %collective-permute-done.7.refs_1_.refs_3_) | copy-start | bytes 516100
  94.9 12.9 %all-to-all-start.1 = ((bf16[8,80,128]{2,1,0:T(8,128)(2,1)}), bf16[8,80,128]{2,1,0:T(8,128)(2,1)S(1)}, u32[]{:S(2)}, u32[]{:S(2)}) async-start(bf16[8,80,128]{2,1,0:T(8,128)(2,1)} %spread.2.refs_10_), calls=%async_computation.1 | async-start | bytes 327680 | tf_op jit(solution)/shard_map/all_to_all | solution.py:629
  108.9 22.1 %copy-start.4 = (bf16[192,16,128]{2,1,0:T(8,128)(2,1)S(1)}, bf16[192,16,128]{2,1,0:T(8,128)(2,1)}, u32[]{:S(2)}) copy-start(bf16[192,16,128]{2,1,0:T(8,128)(2,1)} %back.1.refs_0_.after_ref) | copy-start | bytes 2359300
  108.9 22.1 %copy-start.15 = (s32[4]{0:T(128)S(1)}, s32[4]{0:T(128)}, u32[]{:S(2)}) copy-start(s32[4]{0:T(128)} %pad_add_fusion.at_ref.refs_0_) | copy-start | bytes 52
  109.0 6.2 %collective-permute-start.13 = (bf16[80,128]{1,0:T(8,128)(2,1)S(1)}, bf16[80,128]{1,0:T(8,128)(2,1)S(1)}, u32[]{:S(2)}, u32[]{:S(2)}) collective-permute-start(bf16[80,128]{1,0:T(8,128)(2,1)S(1)} %bitcast.13), channel_id=1, source_target_pairs={{0,128},{1,129},{4,132},{5,133},{8,136},{9,137},{12,140},{13,141},... | collective-permute-start | bytes 61448 | tf_op jit(solution)/shard_map/ppermute | solution.py:630
  114.0 2.6 %collective-permute-start.12 = (bf16[80,128]{1,0:T(8,128)(2,1)S(1)}, bf16[80,128]{1,0:T(8,128)(2,1)S(1)}, u32[]{:S(2)}, u32[]{:S(2)}) collective-permute-start(bf16[80,128]{1,0:T(8,128)(2,1)S(1)} %bitcast.14), channel_id=1, source_target_pairs={{0,192},{1,193},{4,196},{5,197},{8,200},{9,201},{12,204},{13,205},... | collective-permute-start | bytes 61448 | tf_op jit(solution)/shard_map/ppermute | solution.py:630
  114.0 2.7 %collective-permute-start.11 = (bf16[80,128]{1,0:T(8,128)(2,1)S(1)}, bf16[80,128]{1,0:T(8,128)(2,1)S(1)}, u32[]{:S(2)}, u32[]{:S(2)}) collective-permute-start(bf16[80,128]{1,0:T(8,128)(2,1)S(1)} %bitcast.15), channel_id=1, source_target_pairs={{0,64},{1,65},{4,68},{5,69},{8,72},{9,73},{12,76},{13,77},{16,80},... | collective-permute-start | bytes 61448 | tf_op jit(solution)/shard_map/ppermute | solution.py:630
  116.7 9.7 %collective-permute-start.16 = (bf16[320,128]{1,0:T(8,128)(2,1)S(1)}, bf16[320,128]{1,0:T(8,128)(2,1)S(1)}, u32[]{:S(2)}, u32[]{:S(2)}) collective-permute-start(bf16[320,128]{1,0:T(8,128)(2,1)S(1)} %pad_maximum_fusion), channel_id=1, source_target_pairs={{0,32},{1,33},{4,36},{5,37},{8,40},{9,41},{12,44},{13,45},{16,48},... | collective-permute-start | bytes 245768 | tf_op jit(solution)/shard_map/ppermute | solution.py:631
  120.9 5.4 %collective-permute-start.15 = (bf16[320,128]{1,0:T(8,128)(2,1)S(1)}, bf16[320,128]{1,0:T(8,128)(2,1)S(1)}, u32[]{:S(2)}, u32[]{:S(2)}) collective-permute-start(bf16[320,128]{1,0:T(8,128)(2,1)S(1)} %pad_maximum_fusion), channel_id=1, source_target_pairs={{0,34},{1,35},{4,38},{5,39},{8,42},{9,43},{12,46},{13,47},{16,50},... | collective-permute-start | bytes 245768 | tf_op jit(solution)/shard_map/ppermute | solution.py:631
  120.9 3.3 %collective-permute-start.14 = (bf16[320,128]{1,0:T(8,128)(2,1)S(1)}, bf16[320,128]{1,0:T(8,128)(2,1)S(1)}, u32[]{:S(2)}, u32[]{:S(2)}) collective-permute-start(bf16[320,128]{1,0:T(8,128)(2,1)S(1)} %pad_maximum_fusion), channel_id=1, source_target_pairs={{0,2},{1,3},{4,6},{5,7},{8,10},{9,11},{12,14},{13,15},{16,18},{17,... | collective-permute-start | bytes 245768 | tf_op jit(solution)/shard_map/ppermute | solution.py:631
  126.4 4.7 %collective-permute-start.17 = (bf16[1280,128]{1,0:T(8,128)(2,1)S(1)}, bf16[1280,128]{1,0:T(8,128)(2,1)S(1)}, u32[]{:S(2)}, u32[]{:S(2)}) collective-permute-start(bf16[1280,128]{1,0:T(8,128)(2,1)S(1)} %constant_dynamic-update-slice_fusion.a_ref), channel_id=1, source_target_pairs={{0,1},{1,0},{4,5},{5,4},{8,9},{9,8},{12,13},{13,12},{16,17},{17,16... | collective-permute-start | bytes 983048 | tf_op jit(solution)/shard_map/ppermute | solution.py:632
  (8 other events, 7.5 us)
